TPU v7x, 256 devices: a whole 4x4x8 slice. The times are simulated.
256 devices in a mesh: dp: 32 (over z, x_lo, core), tp: 8 (over y, x_hi).
Axes of the slice: x: 4 (x_hi: 2, x_lo: 2; x = x_hi * 2 + x_lo), y: 4, z: 8, core: 2. Of those that a mesh axis runs over, the one named last changes fastest.
Arguments:
- hidden: bfloat16 [1024, 4, 5120], P('dp', None, 'tp'), may hold values from -6 to 6
- norm_gain: bfloat16 [5120], P('tp'), may hold values from 0.3984375 to 2.5
- w_query: bfloat16 [5120, 4096], P(None, 'tp'), may hold values from -0.078125 to 0.078125
- key_projection: bfloat16 [5120, 1024], P(None, 'tp'), may hold values from -0.078125 to 0.078125
- value_projection: bfloat16 [5120, 1024], P(None, 'tp'), may hold values from -0.078125 to 0.078125
- query_gain: bfloat16 [128], replicated, may hold values from 0.5 to 2
- key_gain: bfloat16 [128], replicated, may hold values from 0.5 to 2
- cache_keys: bfloat16 [32, 32, 2, 128, 1024], P('dp', None, None, None, 'tp'), may hold values from -400 to 400
- cached_value_pages: bfloat16 [32, 32, 2, 128, 1024], P('dp', None, None, None, 'tp'), may hold values from -6 to 6
- cache_len: int32 [1024], replicated, may hold values from 1 to 256, as said below
- remaining: int32 [1024], P('dp'), may hold values from 0 to 7
- page_row: int32 [32, 32, 2], replicated, may hold values from 0 to 32, as said below
- page_seq: int32 [32, 32, 2], replicated, may hold values from 0 to 1, as said below
Outputs:
- attention: bfloat16 [1024, 4, 4096], P('dp', None, 'tp')
- new_keys: bfloat16 [1024, 4, 1024], P('dp', None, 'tp')
- new_values: bfloat16 [1024, 4, 1024], P('dp', None, 'tp')
Inputs may be any that keep to these rules, and one draw needn't show every extreme that they name: `cache_len`: the pages of a row of n cached tokens fill exactly ceil(n / 128) slots. `page_row`: for holder group g, owner group o and slot c: the owner's row whose page the slot holds, or 32 for an empty slot. `page_seq`: each page number 0 to ceil(n / 128) - 1 of a row of n cached tokens appears once among the row's slots; empty slots hold 0.
All inputs are finite; a program needn't handle non-finite values.
Results may differ from a plain program's by a relative error of at most 0.015.
The roundings to bfloat16 on the way count: a program that leaves them out, or rounds other values in their place, can miss the bound.
Values may be sent and summed in bfloat16 or wider, within the bound.
No kernel may reach another device: no remote copies, remote signals or barrier semaphores. Data moves between devices by JAX's collectives and lax.ppermute only.
A program may use at most 64 MiB of HBM per device.

v0:
```python
import math

import jax
import jax.numpy as jnp
from jax import lax
from jax.sharding import PartitionSpec as P

EPSILON = 1e-06
ROPE_BASE = 1000000.0
MASKED_SCORE = -1e30


def head_norm_rope(heads, gain_vector, positions):
    head_width = heads.shape[-1]
    half_width = head_width // 2
    scaled = (
        heads
        * lax.rsqrt(jnp.mean(heads * heads, axis=-1, keepdims=True) + EPSILON)
        * gain_vector.astype(jnp.float32)
    )
    frequency = jnp.exp(
        jnp.arange(half_width, dtype=jnp.float32) * (-2.0 * math.log(ROPE_BASE) / head_width)
    )
    angles = positions.astype(jnp.float32)[:, :, None, None] * frequency
    cosine = jnp.cos(angles)
    sine_part = jnp.sin(angles)
    first_half = scaled[..., :half_width]
    second = scaled[..., half_width:]
    return jnp.concatenate(
        [first_half * cosine - second * sine_part, second * cosine + first_half * sine_part],
        axis=-1,
    )


def masked_parts(group_scores, usable):
    group_scores = jnp.where(usable, group_scores, MASKED_SCORE)
    block_max = jnp.max(group_scores, axis=-1)
    weights = jnp.where(usable, jnp.exp(group_scores - block_max[..., None]), 0.0).astype(
        jnp.bfloat16
    )
    return (block_max, weights, jnp.sum(weights.astype(jnp.float32), axis=-1))


def page_partial(queries, page_keys, page_values, usable):
    scale = 1.0 / math.sqrt(queries.shape[-1])
    group_scores = (
        jnp.einsum("nkqd,npkd->nkqp", queries, page_keys, preferred_element_type=jnp.float32)
        * scale
    )
    block_max, weights, block_total = masked_parts(group_scores, usable[:, None, None, :])
    output = jnp.einsum("nkqp,npkd->nkqd", weights, page_values, preferred_element_type=jnp.float32)
    return (block_max, block_total, output)


def new_partial(arranged, fresh_keys, fresh_values, step_count):
    scale = 1.0 / math.sqrt(arranged.shape[-1])
    group_scores = (
        jnp.einsum("rkqd,rjkd->rkqj", arranged, fresh_keys, preferred_element_type=jnp.float32)
        * scale
    )
    step_index = jnp.arange(arranged.shape[2], dtype=jnp.int32) % step_count
    causal = jnp.arange(step_count, dtype=jnp.int32)[None, :] <= step_index[:, None]
    block_max, weights, block_total = masked_parts(group_scores, causal[None, None])
    output = jnp.einsum(
        "rkqj,rjkd->rkqd", weights, fresh_values, preferred_element_type=jnp.float32
    )
    return (block_max, block_total, output)


def combine_pages(
    page_rows, page_max, page_total, page_out, new_max, new_total, new_out, row_count
):
    row_hit = (page_rows[:, None] == jnp.arange(row_count, dtype=jnp.int32)[None, :])[
        :, :, None, None
    ]
    page_top = jnp.max(jnp.where(row_hit, page_max[:, None], MASKED_SCORE), axis=0)
    row_max = jnp.maximum(page_top, new_max)
    factor = jnp.exp(jnp.where(row_hit, page_max[:, None] - row_max[None], MASKED_SCORE))
    own_factor = jnp.exp(new_max - row_max)
    denominator = (
        jnp.einsum("nrkq,nkq->rkq", factor, page_total, precision=lax.Precision.HIGHEST)
        + own_factor * new_total
    )
    numerator = (
        jnp.einsum("nrkq,nkqd->rkqd", factor, page_out, precision=lax.Precision.HIGHEST)
        + own_factor[..., None] * new_out
    )
    return numerator / denominator[..., None]


def shards(
    hidden,
    norm_gain,
    w_query,
    key_projection,
    value_projection,
    query_gain,
    key_gain,
    cache_keys,
    cached_value_pages,
    cache_len,
    remaining,
    page_row,
    page_seq,
):
    gathered, full_gain = (
        lax.all_gather(hidden, "tp", axis=2, tiled=True),
        lax.all_gather(norm_gain, "tp", axis=0, tiled=True),
    )
    row_count, step_count, feature_count = gathered.shape
    head_width = query_gain.shape[0]
    groups = page_row.shape[0]
    capacity = page_row.shape[2]
    page_len = cache_keys.shape[3]
    kv_heads = key_projection.shape[1] // head_width
    my_group = lax.axis_index("dp")
    hidden_wide = gathered.astype(jnp.float32)
    normed = (
        hidden_wide
        * lax.rsqrt(jnp.mean(hidden_wide * hidden_wide, axis=-1, keepdims=True) + EPSILON)
        * full_gain.astype(jnp.float32)
    ).astype(jnp.bfloat16)
    flattened = normed.reshape(row_count * step_count, feature_count)
    local_lengths = lax.dynamic_slice_in_dim(cache_len, my_group * row_count, row_count)
    positions = local_lengths[:, None] + jnp.arange(step_count, dtype=jnp.int32)[None, :]
    queries = jnp.dot(flattened, w_query, preferred_element_type=jnp.float32).reshape(
        row_count, step_count, -1, head_width
    )
    queries = head_norm_rope(queries, query_gain, positions).astype(jnp.bfloat16)
    fresh_keys = jnp.dot(flattened, key_projection, preferred_element_type=jnp.float32).reshape(
        row_count, step_count, kv_heads, head_width
    )
    fresh_keys = head_norm_rope(fresh_keys, key_gain, positions).astype(jnp.bfloat16)
    fresh_values = (
        jnp.dot(flattened, value_projection, preferred_element_type=jnp.float32)
        .astype(jnp.bfloat16)
        .reshape(row_count, step_count, kv_heads, head_width)
    )
    group_size = queries.shape[2] // kv_heads
    arranged = (
        queries.reshape(row_count, step_count, kv_heads, group_size, head_width)
        .transpose(0, 2, 3, 1, 4)
        .reshape(row_count, kv_heads, group_size * step_count, head_width)
    )
    new_max, new_total, new_out = new_partial(arranged, fresh_keys, fresh_values, step_count)
    slot_count = groups * capacity
    token_index = jnp.arange(page_len, dtype=jnp.int32)[None, :]
    rows_sent = lax.dynamic_index_in_dim(page_row, my_group, 1, keepdims=False)
    page_rows = rows_sent.reshape(-1)
    got_keys, got_values = (
        lax.all_to_all(cache_keys, "dp", split_axis=1, concat_axis=0, tiled=True),
        lax.all_to_all(cached_value_pages, "dp", split_axis=1, concat_axis=0, tiled=True),
    )
    seq_sent = lax.dynamic_index_in_dim(page_seq, my_group, 1, keepdims=False).reshape(-1)
    safe_row = jnp.minimum(page_rows, row_count - 1)
    length_cap = jnp.where(page_rows < row_count, local_lengths[safe_row], 0)
    usable = seq_sent[:, None] * page_len + token_index < length_cap[:, None]
    page_max, page_total, page_out = page_partial(
        arranged[safe_row],
        got_keys.reshape(slot_count, page_len, kv_heads, head_width),
        got_values.reshape(slot_count, page_len, kv_heads, head_width),
        usable,
    )
    attended = combine_pages(
        page_rows, page_max, page_total, page_out, new_max, new_total, new_out, row_count
    )
    attended = (
        attended.reshape(row_count, kv_heads, group_size, step_count, head_width)
        .transpose(0, 3, 1, 2, 4)
        .reshape(row_count, step_count, -1)
    )
    live = jnp.arange(step_count, dtype=jnp.int32)[None, :] < remaining[:, None]
    attention = jnp.where(live[:, :, None], attended, 0.0).astype(jnp.bfloat16)
    return (
        attention,
        fresh_keys.reshape(row_count, step_count, -1),
        fresh_values.reshape(row_count, step_count, -1),
    )


def solution(mesh):
    in_specs = (
        P("dp", None, "tp"),
        P("tp"),
        P(None, "tp"),
        P(None, "tp"),
        P(None, "tp"),
        P(),
        P(),
        P("dp", None, None, None, "tp"),
        P("dp", None, None, None, "tp"),
        P(),
        P("dp"),
        P(),
        P(),
    )
    out_specs = (P("dp", None, "tp"), P("dp", None, "tp"), P("dp", None, "tp"))
    return jax.shard_map(shards, mesh=mesh, in_specs=in_specs, out_specs=out_specs, check_vma=False)
```

profile of v0, /device:TPU:1, one launch (start us, length us, event | category | flops | bytes accessed | tf_op | source)
XLA Modules:
  0.0 150.5 jit_solution(10704960076941873637)
XLA Ops:
  7.2 0.0 copy-start
  7.2 0.0 all-gather.3.cloned.1.call-start
  7.2 0.7 all-gather.3.cloned.1.call-update
  7.9 0.0 copy-start.3
  7.9 11.2 %all-to-all-start = ((bf16[1,32,2,128,128]{4,3,2,0,1:T(8,128)(2,1)}), bf16[1,32,2,128,128]{4,3,2,0,1:T(8,128)(2,1)}, u32[]{:S(2)}, u32[]{:S(2)}) async-start(bf16[1,32,2,128,128]{4,3,2,0,1:T(8,128)(2,1)} %bitcast.68), calls=%async_computation | async-start | bytes 4194304 | tf_op jit(solution)/shard_map/all_to_all | solution.py:151
  19.2 0.0 copy-done.3
  19.2 0.0 copy-done.4
  19.2 1.8 %dynamic-slice_reduce_fusion = (s32[32,2]{1,0:T(8,128)S(1)}, s32[32,2]{1,0:T(8,128)S(1)}, s32[32,2]{1,0:T(8,128)S(1)}) fusion(s32[32,32,2]{1,2,0:T(2,128)S(1)} %copy-done.3, s32[]{:T(128)S(6)} %select_n.82, s32[32,32,2]{1,2,0:T(2,128)S(1)} %copy-done.4), kind=kLoop, calls=%fused_computation.58 | loop fusion | flops 128 | bytes 1284 | tf_op jit(solution)/shard_map/jit(dynamic_index_in_dim)/dynamic_slice | solution.py:148
  21.0 0.1 min.18
  21.1 0.8 dynamic_slice.12
  22.0 30.5 %all-gather = bf16[8,1,640]{2,1,0:T(2,128)(2,1)S(1)} all-gather(bf16[1,1,640]{2,1,0:T(2,128)(2,1)S(1)} %reshape.497), channel_id=1, replica_groups=mesh['dp'=32,'tp'=8] {'tp'}, dimensions={0}, use_global_device_ids=true | all-gather | bytes 11520 | tf_op jit(solution)/shard_map/all_gather | solution.py:108
  52.4 0.0 copy-start.8
  52.5 0.0 copy-start.9
  52.5 0.0 copy-start.7
  52.5 7.8 %copy.130 = bf16[512,5120]{1,0:T(8,128)(2,1)} copy(bf16[512,5120]{0,1:T(8,128)(2,1)} %bitcast.66) | data formatting | bytes 10485760 | tf_op jit(solution)/shard_map/dot_general | solution.py:126
  60.3 0.1 copy.112
  60.4 0.8 gather_fusion
  61.2 0.1 reshape.466
  61.3 0.1 mul.221
  61.4 0.0 copy-done.7
  61.4 0.1 iota_compare_fusion.1
  61.5 0.1 add_compare_fusion
  61.6 0.3 multiply_cosine_fusion
  61.9 12.7 %all-gather.3.cloned.1.call-done = bf16[32,4,5120]{2,1,0:T(4,128)(2,1)} async-done(((bf16[32,4,640]{2,1,0:T(4,128)(2,1)}), bf16[32,4,5120]{2,1,0:T(4,128)(2,1)}) %all-gather.3.cloned.1.call-update) | async-done | bytes 1310736 | tf_op jit(solution)/shard_map/all_gather | solution.py:107
  74.6 2.2 %fusion = f32[32,4]{1,0:T(8,128)S(1)} fusion(bf16[32,4,5120]{2,1,0:T(4,128)(2,1)} %all-gather.3.cloned.1.call-done), kind=kLoop, calls=%fused_computation.4 | loop fusion | flops 1965952 | bytes 1311232 | tf_op jit(solution)/shard_map/reduce_sum | solution.py:120
  76.8 0.0 copy-done.1
  76.8 0.7 fusion.48
  77.6 4.5 %multiply_reduce_fusion.1 = (f32[32,4,4]{0,2,1:T(4,128)S(1)}, f32[32,4,4,128]{3,0,2,1:T(8,128)S(1)}) fusion(bf16[4,128,5120,1]{2,1,0,3:T(8,128)(2,1)} %bitcast.67, bf16[32,4,5120,1]{2,1,0,3:T(4,128)(2,1)S(1)} %fusion.48), kind=kOutput, calls=%fused_computation.28 | convolution fusion | flops 671219200 | bytes 6817792 | tf_op jit(solution)/shard_map/dot_general | solution.py:126
  82.1 0.1 multiply_multiply_fusion
  82.2 0.2 fusion.10
  82.4 0.1 maximum_bitcast_fusion
  82.5 0.0 all-to-all-done
  82.5 7.1 %all-to-all-start.1 = ((bf16[1,32,2,128,128]{4,3,2,0,1:T(8,128)(2,1)}), bf16[1,32,2,128,128]{4,3,2,0,1:T(8,128)(2,1)}, u32[]{:S(2)}, u32[]{:S(2)}) async-start(bf16[1,32,2,128,128]{4,3,2,0,1:T(8,128)(2,1)} %bitcast.69), calls=%async_computation.1 | async-start | bytes 4194304 | tf_op jit(solution)/shard_map/all_to_all | solution.py:152
  89.6 1.8 %fusion.2 = bf16[32,4,5120]{2,1,0:T(4,128)(2,1)} fusion(bf16[32,4,5120]{2,1,0:T(4,128)(2,1)S(1)} %copy-done.1, f32[5120]{0:T(1024)S(1)} %bitcast.74, f32[32,4]{1,0:T(8,128)S(1)} %add_rsqrt_fusion), kind=kLoop, calls=%fused_computation.6 | loop fusion | flops 2621440 | bytes 2642432 | tf_op jit(solution)/shard_map/convert_element_type | solution.py:122
  91.4 2.5 %reshape.472 = bf16[128,5120]{1,0:T(8,128)(2,1)S(1)} reshape(bf16[32,4,5120]{2,1,0:T(4,128)(2,1)} %fusion.2) | data formatting | bytes 2621440 | tf_op jit(solution)/shard_map/reshape | solution.py:123
  93.9 0.6 multiply_reduce_fusion.2
  94.5 0.1 rsqrt.30
  94.6 0.1 copy.107
  94.6 0.1 multiply_multiply_fusion.1
  94.7 0.6 fusion.25
  95.3 0.1 pad_maximum_fusion
  95.4 0.0 copy-start.5
  95.4 0.2 fusion.37
  95.6 0.1 copy.115
  95.7 0.6 gather_fusion.1
  96.4 0.1 convert_reduce_fusion.1
  96.4 1.8 %convolution_convert_fusion = bf16[128,128]{1,0:T(8,128)(2,1)S(1)} fusion(bf16[128,5120]{1,0:T(8,128)(2,1)S(1)} %reshape.472, bf16[5120,128]{1,0:T(8,128)(2,1)} %param.17), kind=kOutput, calls=%fused_computation.16 | convolution fusion | flops 167788544 | bytes 2654208 | tf_op jit(solution)/shard_map/dot_general | solution.py:135
  98.2 0.0 copy-start.2
  98.2 0.2 fusion.34
  98.5 2.9 %fusion.36 = (f32[64,16]{1,0:T(8,128)S(1)}, f32[64,16,128]{2,1,0:T(8,128)S(1)}) fusion(bf16[64,16,128]{2,1,0:T(8,128)(2,1)S(1)} %gather_fusion.1, bf16[64,128,128]{2,1,0:T(8,128)(2,1)} %bitcast.13, pred[64,128]{1,0:T(8,128)(4,1)S(1)} %add_compare_fusion), kind=kOutput, calls=%fused_computation.83 | convolution fusion | flops 33946624 | bytes 2895872 | tf_op jit(solution)/shard_map/nkqd,npkd->nkqp/dot_general | solution.py:47
  101.4 0.1 copy.110
  101.4 0.2 select_reduce_fusion
  101.6 0.1 copy.114
  101.7 0.4 convert_reduce_fusion
  102.0 0.1 copy.131
  102.1 0.3 multiply_reduce_fusion
  102.4 0.1 copy.127
  102.5 0.1 copy.119
  102.6 37.1 %all-to-all-done.1 = bf16[1,32,2,128,128]{4,3,2,0,1:T(8,128)(2,1)} async-done(((bf16[1,32,2,128,128]{4,3,2,0,1:T(8,128)(2,1)}), bf16[1,32,2,128,128]{4,3,2,0,1:T(8,128)(2,1)}, u32[]{:S(2)}, u32[]{:S(2)}) %all-to-all-start.1) | async-done | bytes 2097184 | tf_op jit(solution)/shard_map/all_to_all | solution.py:152
  139.7 2.3 %fusion.26 = f32[64,16,128]{2,1,0:T(8,128)S(1)} fusion(bf16[64,128,128]{2,1,0:T(8,128)(2,1)} %bitcast.15, f32[64,16,128]{2,1,0:T(8,128)S(1)} %get-tuple-element.16, f32[64,16]{1,0:T(8,128)S(1)} %get-tuple-element.15, pred[64,128]{1,0:T(8,128)(4,1)S(1)} %add_compare_fusion), kind=kOutput, calls=%fused_computation.60 | convolution fusion | flops 33947648 | bytes 3158016 | tf_op jit(solution)/shard_map/nkqp,npkd->nkqd/dot_general | solution.py:51
  142.0 0.8 fusion.7
  142.7 0.1 copy.120
  142.9 0.1 reshape.476
  142.9 0.8 select_convert_fusion.1
  (27 shorter events, 0.2 us)
Async XLA Ops:
  7.2 86.7 %copy-start = (bf16[5120,128]{1,0:T(8,128)(2,1)S(1)}, bf16[5120,128]{1,0:T(8,128)(2,1)}, u32[]{:S(2)}) copy-start(bf16[5120,128]{1,0:T(8,128)(2,1)} %param.16) | copy-start | bytes 3932164
  7.2 67.5 %all-gather.3.cloned.1.call-start = ((), (), s32[]{:S(2)}) async-start(), calls=%async_computation.2 | async-start | bytes 1474560 | tf_op jit(solution)/shard_map/all_gather | solution.py:107
  7.9 11.3 %copy-start.3 = (s32[32,32,2]{1,2,0:T(2,128)S(1)}, s32[32,32,2]{1,2,0:T(2,128)}, u32[]{:S(2)}) copy-start(s32[32,32,2]{1,2,0:T(2,128)} %param.24) | copy-start | bytes 24580
  7.9 11.3 %copy-start.4 = (s32[32,32,2]{1,2,0:T(2,128)S(1)}, s32[32,32,2]{1,2,0:T(2,128)}, u32[]{:S(2)}) copy-start(s32[32,32,2]{1,2,0:T(2,128)} %param.25) | copy-start | bytes 24580
  7.9 14.0 %copy-start.6 = (bf16[640]{0:T(1024)(128)(2,1)S(1)}, bf16[640]{0:T(1024)(128)(2,1)}, u32[]{:S(2)}) copy-start(bf16[640]{0:T(1024)(128)(2,1)} %param.14) | copy-start | bytes 3844
  7.9 74.6 %all-to-all-start = ((bf16[1,32,2,128,128]{4,3,2,0,1:T(8,128)(2,1)}), bf16[1,32,2,128,128]{4,3,2,0,1:T(8,128)(2,1)}, u32[]{:S(2)}, u32[]{:S(2)}) async-start(bf16[1,32,2,128,128]{4,3,2,0,1:T(8,128)(2,1)} %bitcast.68), calls=%async_computation | async-start | bytes 4194304 | tf_op jit(solution)/shard_map/all_to_all | solution.py:151
  52.4 7.8 %copy-start.8 = (bf16[128]{0:T(256)(128)(2,1)S(1)}, bf16[128]{0:T(256)(128)(2,1)}, u32[]{:S(2)}) copy-start(bf16[128]{0:T(256)(128)(2,1)} %param.18) | copy-start | bytes 772
  52.5 7.9 %copy-start.9 = (bf16[128]{0:T(256)(128)(2,1)S(1)}, bf16[128]{0:T(256)(128)(2,1)}, u32[]{:S(2)}) copy-start(bf16[128]{0:T(256)(128)(2,1)} %param.19) | copy-start | bytes 772
  52.5 8.9 %copy-start.7 = (s32[32]{0:T(128)S(1)}, s32[32]{0:T(128)}, u32[]{:S(2)}) copy-start(s32[32]{0:T(128)} %param.23) | copy-start | bytes 388
  74.6 2.2 %copy-start.1 = (bf16[32,4,5120]{2,1,0:T(4,128)(2,1)S(1)}, bf16[32,4,5120]{2,1,0:T(4,128)(2,1)}, u32[]{:S(2)}) copy-start(bf16[32,4,5120]{2,1,0:T(4,128)(2,1)} %all-gather.3.cloned.1.call-done) | copy-start | bytes 3932164
  82.5 57.1 %all-to-all-start.1 = ((bf16[1,32,2,128,128]{4,3,2,0,1:T(8,128)(2,1)}), bf16[1,32,2,128,128]{4,3,2,0,1:T(8,128)(2,1)}, u32[]{:S(2)}, u32[]{:S(2)}) async-start(bf16[1,32,2,128,128]{4,3,2,0,1:T(8,128)(2,1)} %bitcast.69), calls=%async_computation.1 | async-start | bytes 4194304 | tf_op jit(solution)/shard_map/all_to_all | solution.py:152
  95.4 5.9 %copy-start.5 = (bf16[32,4,128]{2,1,0:T(4,128)(2,1)}, bf16[32,4,128]{2,1,0:T(4,128)(2,1)S(1)}, u32[]{:S(2)}) copy-start(bf16[32,4,128]{2,1,0:T(4,128)(2,1)S(1)} %pad_maximum_fusion) | copy-start | bytes 98308
  98.2 4.3 %copy-start.2 = (bf16[128,128]{1,0:T(8,128)(2,1)}, bf16[128,128]{1,0:T(8,128)(2,1)S(1)}, u32[]{:S(2)}) copy-start(bf16[128,128]{1,0:T(8,128)(2,1)S(1)} %convolution_convert_fusion) | copy-start | bytes 98308
Sparse Core Ops, SparseCore 0:
  10.5 64.0 all-gather.2
where the time goes:
time: 151 us
  waiting for transfers between devices  50.5 us (33%)
  blocking collectives  30.5 us (20%)
  starting transfers between devices  18.3 us (12%)
  between operations  14.4 us (10%)
  local copies, waits for them, and re-layouts  13.6 us (9%)
  matrix products  13.2 us (9%)
  other arithmetic  9.93 us (7%)
    all_to_all x1, waiting for transfers between devices, shards(): lax.all_to_all(cached_value_pages, 'dp', split_axis=1, concat_axis=0, til...  37.1 us
    all_gather x1, blocking collectives, shards(): lax.all_gather(norm_gain, 'tp', axis=0, tiled=True)  30.5 us
    all_gather x1, waiting for transfers between devices, shards(): lax.all_gather(hidden, 'tp', axis=2, tiled=True)  12.7 us
    all_to_all x1, starting transfers between devices, shards(): lax.all_to_all(cache_keys, 'dp', split_axis=1, concat_axis=0, tiled=True)  11.2 us
    dot_general x1, local copies, waits for them, and re-layouts, shards(): jnp.dot(flattened, w_query, preferred_element_type=jnp.float32)  7.81 us
    all_to_all x1, starting transfers between devices, shards(): lax.all_to_all(cached_value_pages, 'dp', split_axis=1, concat_axis=0, til...  7.06 us
    dot_general x1, matrix products, shards(): jnp.dot(flattened, w_query, preferred_element_type=jnp.float32)  4.48 us
  transfers between devices with their start and end apart: 3, of which 2 were waited for; matrix products, arithmetic and copies ran while one was open for 22% of the time, Pallas kernels for 0%

commit v1 on v0

v1 whole, which is shorter than its diff:
```python
import functools
import math

import jax
import jax.numpy as jnp
from jax import lax
from jax.experimental import pallas as pl
from jax.experimental.pallas import tpu as pltpu
from jax.sharding import PartitionSpec as P

EPSILON = 1e-06
ROPE_BASE = 1000000.0
MASKED = -1e30
ROWS = 32
STEPS = 4
HEADS = 4
QUERIES = HEADS * STEPS
WIDTH = 128
GROUPS = 32
SLOTS = 2
TOKENS = ROWS * STEPS
SIDE = 8
SCALE = 1.0 / math.sqrt(WIDTH)

VMEM = pltpu.VMEM
SMEM = pltpu.SMEM


def project_kernel(
    x_ref, wq_ref, wk_ref, wv_ref, qg_ref, kg_ref, cos_ref, sin_ref, row_ref, me_ref,
    send_ref, pack_ref, key_ref, value_ref, norm_ref,
):
    shards, _, features = x_ref.shape
    total = jnp.zeros((TOKENS, 1), jnp.float32)
    for t in range(shards):
        x = x_ref[t, :TOKENS, :].astype(jnp.float32)
        total = total + jnp.sum(x * x, axis=1, keepdims=True)
    rstd = lax.rsqrt(total * (1.0 / (shards * features)) + EPSILON)
    for t in range(shards):
        x = x_ref[t, :TOKENS, :].astype(jnp.float32)
        gain = x_ref[t, TOKENS : TOKENS + 8, :].astype(jnp.float32)[0:1]
        norm_ref[:, t * features : (t + 1) * features] = (x * rstd * gain).astype(jnp.bfloat16)
    cos = cos_ref[...]
    sin = sin_ref[...]

    def rotated(heads, gain):
        mean = jnp.sum(heads * heads, axis=1, keepdims=True) * (1.0 / WIDTH)
        scaled = heads * lax.rsqrt(mean + EPSILON) * gain
        return scaled * cos + pltpu.roll(scaled, WIDTH // 2, 1) * sin

    normed = norm_ref[...]
    queries = jnp.dot(normed, wq_ref[...], preferred_element_type=jnp.float32)
    q_gain = qg_ref[...].astype(jnp.float32)
    low = lax.broadcasted_iota(jnp.int32, (8, WIDTH), 0) < STEPS
    turned = [
        rotated(queries[:, h * WIDTH : (h + 1) * WIDTH], q_gain) for h in range(HEADS)
    ]
    for i in range(ROWS // 2):
        parts = [turned[h][8 * i : 8 * i + 8] for h in range(HEADS)]
        rolled = [pltpu.roll(p, STEPS, 0) for p in parts]
        even = [jnp.where(low, parts[h], rolled[h + 1]) for h in (0, 2)]
        odd = [jnp.where(low, rolled[h], parts[h + 1]) for h in (0, 2)]
        pack_ref[2 * i] = jnp.concatenate(even, axis=0).astype(jnp.bfloat16)
        pack_ref[2 * i + 1] = jnp.concatenate(odd, axis=0).astype(jnp.bfloat16)
    me = me_ref[0]
    for g in range(GROUPS):
        for c in range(SLOTS):
            row = jnp.minimum(row_ref[(g * GROUPS + me) * SLOTS + c], ROWS - 1)
            send_ref[g, c * QUERIES : (c + 1) * QUERIES, :] = pack_ref[row]
    keys = jnp.dot(normed, wk_ref[...], preferred_element_type=jnp.float32)
    key_ref[...] = rotated(keys, kg_ref[...].astype(jnp.float32)).astype(jnp.bfloat16)
    values = jnp.dot(normed, wv_ref[...], preferred_element_type=jnp.float32)
    value_ref[...] = values.astype(jnp.bfloat16)


def fresh_kernel(pack_ref, key_ref, value_ref, lse_ref, out_ref):
    count = ROWS * QUERIES
    scores = (
        lax.dot_general(
            pack_ref[...].reshape(count, WIDTH), key_ref[...],
            (((1,), (1,)), ((), ())), preferred_element_type=jnp.float32,
        )
        * SCALE
    )
    query = lax.broadcasted_iota(jnp.int32, (count, TOKENS), 0)
    token = lax.broadcasted_iota(jnp.int32, (count, TOKENS), 1)
    usable = ((query >> 4) == (token >> 2)) & ((token & 3) <= (query & 3))
    scores = jnp.where(usable, scores, MASKED)
    top = jnp.max(scores, axis=1, keepdims=True)
    weights = jnp.where(usable, jnp.exp(scores - top), 0.0).astype(jnp.bfloat16)
    total = jnp.sum(weights.astype(jnp.float32), axis=1, keepdims=True)
    out = jnp.dot(weights, value_ref[...], preferred_element_type=jnp.float32)
    out_ref[...] = out / total
    lse_ref[...] = jnp.broadcast_to(top + jnp.log(total), (count, WIDTH))


def page_kernel(q_ref, key_ref, value_ref, len_ref, row_ref, seq_ref, me_ref, send_ref):
    me = me_ref[0]
    lane = lax.broadcasted_iota(jnp.int32, (QUERIES, WIDTH), 1)
    wide_lane = lax.broadcasted_iota(jnp.int32, (SLOTS * QUERIES, WIDTH), 1)
    side = jnp.zeros((SLOTS * QUERIES, WIDTH), jnp.float32)
    for o in range(GROUPS):
        column = []
        for c in range(SLOTS):
            slot = o * SLOTS + c
            place = (me * GROUPS + o) * SLOTS + c
            row = row_ref[place]
            length = len_ref[o * ROWS + jnp.minimum(row, ROWS - 1)]
            cap = jnp.where(row < ROWS, length - seq_ref[place] * WIDTH, 0)
            usable = lane < cap
            scores = (
                lax.dot_general(
                    q_ref[o, c * QUERIES : (c + 1) * QUERIES, :], key_ref[slot],
                    (((1,), (1,)), ((), ())), preferred_element_type=jnp.float32,
                )
                * SCALE
            )
            scores = jnp.where(usable, scores, MASKED)
            top = jnp.max(scores, axis=1, keepdims=True)
            weights = jnp.where(usable, jnp.exp(scores - top), 0.0).astype(jnp.bfloat16)
            total = jnp.sum(weights.astype(jnp.float32), axis=1, keepdims=True)
            out = jnp.dot(weights, value_ref[slot], preferred_element_type=jnp.float32)
            safe = jnp.maximum(total, 1e-30)
            send_ref[o, c * QUERIES : (c + 1) * QUERIES, :] = (out / safe).astype(jnp.bfloat16)
            column.append(top + jnp.log(safe))
        side = jnp.where(wide_lane == o, jnp.concatenate(column, axis=0), side)
    pairs = SLOTS * QUERIES
    square = jnp.concatenate([side, jnp.zeros((WIDTH - pairs, WIDTH), jnp.float32)], axis=0).T
    whole = square[:GROUPS]
    high = whole.astype(jnp.bfloat16).astype(jnp.float32)
    rest = whole - high
    middle = rest.astype(jnp.bfloat16).astype(jnp.float32)
    last = rest - middle
    pieces = high + pltpu.roll(middle, pairs, 1) + pltpu.roll(last, 2 * pairs, 1)
    for o in range(GROUPS):
        send_ref[o, pairs : pairs + SIDE, :] = jnp.broadcast_to(
            pieces[o : o + 1], (SIDE, WIDTH)
        ).astype(jnp.bfloat16)


def combine_kernel(
    got_ref, lse_ref, out_ref, row_ref, seq_ref, me_ref, remaining_ref,
    attention_ref, wide_ref, index_ref,
):
    me = me_ref[0]
    pairs = SLOTS * QUERIES
    none = GROUPS * SLOTS
    for i in range(ROWS * SLOTS):
        index_ref[i] = none
    for g in range(GROUPS):
        for c in range(SLOTS):
            place = (g * GROUPS + me) * SLOTS + c
            row = row_ref[place]
            index_ref[jnp.where(row < ROWS, row * SLOTS + seq_ref[place], none)] = g * SLOTS + c
    sub = lax.broadcasted_iota(jnp.int32, (8, WIDTH), 0)
    blocks = []
    for b in range(GROUPS // 8):
        block = jnp.zeros((8, WIDTH), jnp.float32)
        for i in range(8):
            tile = got_ref[8 * b + i, pairs : pairs + SIDE, :].astype(jnp.float32)
            block = jnp.where(sub == i, tile, block)
        blocks.append(block)
    side = jnp.concatenate(blocks, axis=0)
    side = side + pltpu.roll(side, WIDTH - pairs, 1) + pltpu.roll(side, WIDTH - 2 * pairs, 1)
    square = jnp.concatenate([side, jnp.zeros((WIDTH - GROUPS, WIDTH), jnp.float32)], axis=0).T
    for g in range(GROUPS):
        for c in range(SLOTS):
            wide_ref[g * SLOTS + c] = jnp.broadcast_to(
                square[c * QUERIES : (c + 1) * QUERIES, g : g + 1], (QUERIES, WIDTH)
            )
    wide_ref[none] = jnp.full((QUERIES, WIDTH), MASKED, jnp.float32)
    step = lax.broadcasted_iota(jnp.int32, (QUERIES, WIDTH), 0) & (STEPS - 1)
    for r in range(ROWS):
        lses = [lse_ref[r * QUERIES : (r + 1) * QUERIES, :]]
        outs = [out_ref[r * QUERIES : (r + 1) * QUERIES, :]]
        for k in range(SLOTS):
            slot = index_ref[r * SLOTS + k]
            lses.append(wide_ref[slot])
            known = jnp.minimum(slot, none - 1)
            start = pl.multiple_of((known & (SLOTS - 1)) * QUERIES, QUERIES)
            outs.append(got_ref[known >> 1, pl.ds(start, QUERIES), :].astype(jnp.float32))
        top = functools.reduce(jnp.maximum, lses)
        factors = [jnp.exp(l - top) for l in lses]
        above = sum(f * o for f, o in zip(factors, outs))
        result = above / sum(factors)
        result = jnp.where(step < remaining_ref[r], result, 0.0).astype(jnp.bfloat16)
        for h in range(HEADS):
            attention_ref[r, :, h * WIDTH : (h + 1) * WIDTH] = result[
                h * STEPS : (h + 1) * STEPS, :
            ]


def shards(
    hidden, norm_gain, w_query, key_projection, value_projection, query_gain, key_gain,
    cache_keys, cached_value_pages, cache_len, remaining, page_row, page_seq,
):
    features = hidden.shape[2]
    tensor = lax.axis_size("tp")
    me = lax.axis_index("dp")
    block = jnp.concatenate(
        [
            hidden.reshape(TOKENS, features),
            jnp.broadcast_to(norm_gain[None, :], (8, features)),
        ],
        axis=0,
    )
    gathered = lax.all_to_all(
        jnp.broadcast_to(block[None], (tensor,) + block.shape), "tp",
        split_axis=0, concat_axis=0, tiled=True,
    )
    lengths = lax.dynamic_slice_in_dim(cache_len, me * ROWS, ROWS)
    positions = (lengths[:, None] + jnp.arange(STEPS, dtype=jnp.int32)[None, :]).reshape(-1, 1)
    frequency = jnp.exp(
        jnp.arange(WIDTH // 2, dtype=jnp.float32) * (-2.0 * math.log(ROPE_BASE) / WIDTH)
    )
    angles = positions.astype(jnp.float32) * frequency[None, :]
    cos = jnp.cos(angles)
    sin = jnp.sin(angles)
    cos = jnp.concatenate([cos, cos], axis=1)
    sin = jnp.concatenate([-sin, sin], axis=1)
    mine = me.reshape(1).astype(jnp.int32)
    rows_flat = page_row.reshape(-1)
    seqs_flat = page_seq.reshape(-1)
    params = pltpu.CompilerParams(vmem_limit_bytes=48 * 1024 * 1024)

    def vmem(n):
        return [pl.BlockSpec(memory_space=VMEM)] * n

    def smem(n):
        return [pl.BlockSpec(memory_space=SMEM)] * n

    send_q, pack, new_key, new_value = pl.pallas_call(
        project_kernel,
        out_shape=(
            jax.ShapeDtypeStruct((GROUPS, SLOTS * QUERIES, WIDTH), jnp.bfloat16),
            jax.ShapeDtypeStruct((ROWS, QUERIES, WIDTH), jnp.bfloat16),
            jax.ShapeDtypeStruct((TOKENS, WIDTH), jnp.bfloat16),
            jax.ShapeDtypeStruct((TOKENS, WIDTH), jnp.bfloat16),
        ),
        in_specs=vmem(8) + smem(2),
        out_specs=tuple(vmem(4)),
        scratch_shapes=[pltpu.VMEM((TOKENS, tensor * features), jnp.bfloat16)],
        compiler_params=params,
        name="project",
    )(
        gathered, w_query, key_projection, value_projection, query_gain[None, :],
        key_gain[None, :], cos, sin, rows_flat, mine,
    )
    got_q = lax.all_to_all(send_q, "dp", split_axis=0, concat_axis=0, tiled=True)
    new_lse, new_out = pl.pallas_call(
        fresh_kernel,
        out_shape=(
            jax.ShapeDtypeStruct((ROWS * QUERIES, WIDTH), jnp.float32),
            jax.ShapeDtypeStruct((ROWS * QUERIES, WIDTH), jnp.float32),
        ),
        in_specs=vmem(3),
        out_specs=tuple(vmem(2)),
        compiler_params=params,
        name="fresh",
    )(pack, new_key, new_value)
    send_out = pl.pallas_call(
        page_kernel,
        out_shape=jax.ShapeDtypeStruct((GROUPS, SLOTS * QUERIES + SIDE, WIDTH), jnp.bfloat16),
        in_specs=vmem(3) + smem(4),
        out_specs=vmem(1)[0],
        compiler_params=params,
        name="pages",
    )(
        got_q,
        cache_keys.reshape(GROUPS * SLOTS, WIDTH, WIDTH),
        cached_value_pages.reshape(GROUPS * SLOTS, WIDTH, WIDTH),
        cache_len, rows_flat, seqs_flat, mine,
    )
    got_out = lax.all_to_all(send_out, "dp", split_axis=0, concat_axis=0, tiled=True)
    attention = pl.pallas_call(
        combine_kernel,
        out_shape=jax.ShapeDtypeStruct((ROWS, STEPS, HEADS * WIDTH), jnp.bfloat16),
        in_specs=vmem(3) + smem(4),
        out_specs=vmem(1)[0],
        scratch_shapes=[
            pltpu.VMEM((GROUPS * SLOTS + 1, QUERIES, WIDTH), jnp.float32),
            pltpu.SMEM((ROWS * SLOTS + 8,), jnp.int32),
        ],
        compiler_params=params,
        name="combine",
    )(got_out, new_lse, new_out, rows_flat, seqs_flat, mine, remaining)
    return (
        attention,
        new_key.reshape(ROWS, STEPS, WIDTH),
        new_value.reshape(ROWS, STEPS, WIDTH),
    )


def solution(mesh):
    in_specs = (
        P("dp", None, "tp"),
        P("tp"),
        P(None, "tp"),
        P(None, "tp"),
        P(None, "tp"),
        P(),
        P(),
        P("dp", None, None, None, "tp"),
        P("dp", None, None, None, "tp"),
        P(),
        P("dp"),
        P(),
        P(),
    )
    out_specs = (P("dp", None, "tp"), P("dp", None, "tp"), P("dp", None, "tp"))
    return jax.shard_map(shards, mesh=mesh, in_specs=in_specs, out_specs=out_specs, check_vma=False)
```

time: 151 us -> 104 us (0.69)
  blocking collectives: 30.5 us -> 0 us
  Pallas kernels: 0 us -> 24.6 us
  between operations: 14.4 us -> 0.74 us
  matrix products: 13.2 us -> 0 us
  waiting for transfers between devices: 50.5 us -> 39.3 us
  other arithmetic: 9.93 us -> 1.13 us
  starting transfers between devices: 18.3 us -> 22.8 us
    all_gather x1 -> x0, blocking collectives: 30.5 us -> none  [shards(): lax.all_gather(norm_gain, 'tp', axis=0, tiled=True)]
    pallas_call x0 -> x4, Pallas kernels: none -> 24.6 us  [the longest x1 16.9 us: shards(): pl.pallas_call(page_kernel, out_shape=jax.ShapeDtypeStruct((GROUPS, SLOTS...]
    dot_general x8 -> x0, matrix products: 13.2 us -> none  [the longest x1 4.48 us: shards(): jnp.dot(flattened, w_query, preferred_element_type=jnp.float32)]
    all_gather x1 -> x0, waiting for transfers between devices: 12.7 us -> none  [shards(): lax.all_gather(hidden, 'tp', axis=2, tiled=True)]
    unnamed x22 -> x36, local copies, waits for them, and re-layouts: 0.12 us -> 9.75 us
    dot_general x2 -> x0, local copies, waits for them, and re-layouts: 7.88 us -> none  [the longest x1 7.81 us: shards(): jnp.dot(flattened, w_query, preferred_element_type=jnp.float32)]
    all_to_all x2 -> x3, starting transfers between devices: 18.3 us -> 22.8 us  [the longest x1 10.7 us: shards(): lax.all_to_all(send_q, 'dp', split_axis=0, concat_axis=0, tiled=True)]
    convert_element_type x7 -> x1, other arithmetic: 3.36 us -> 0.07 us  [shards(): angles = positions.astype(jnp.float32) * frequency[None, :]]
  transfers between devices with their start and end apart: 3 -> 3, of which waited for: 2 -> 3; matrix products, arithmetic and copies ran while one was open for 22% -> 4% of each run, Pallas kernels for 0% -> 0%
where the time goes in v1:
time: 104 us; the launch traced here: 103 us
  waiting for transfers between devices  39.3 us (38%)
  Pallas kernels  24.6 us (24%)
  starting transfers between devices  22.8 us (22%)
  local copies, waits for them, and re-layouts  14.6 us (14%)
  other arithmetic  1.13 us (1%)
    pallas_call x1, Pallas kernels, shards(): pl.pallas_call(page_kernel, out_shape=jax.ShapeDtypeStruct((GROUPS, SLOTS...  16.9 us
    all_to_all x1, waiting for transfers between devices, shards(): lax.all_to_all(jnp.broadcast_to(block[None], (tensor,) + block.shape), 't...  16.8 us
    all_to_all x1, waiting for transfers between devices, shards(): lax.all_to_all(send_out, 'dp', split_axis=0, concat_axis=0, tiled=True)  12.3 us
    all_to_all x1, starting transfers between devices, shards(): lax.all_to_all(send_q, 'dp', split_axis=0, concat_axis=0, tiled=True)  10.7 us
    all_to_all x1, waiting for transfers between devices, shards(): lax.all_to_all(send_q, 'dp', split_axis=0, concat_axis=0, tiled=True)  10.1 us
    unnamed x36, local copies, waits for them, and re-layouts  9.75 us
    all_to_all x1, starting transfers between devices, shards(): lax.all_to_all(jnp.broadcast_to(block[None], (tensor,) + block.shape), 't...  7.61 us
    pallas_call x1, Pallas kernels, shards(): pl.pallas_call(project_kernel, out_shape=(jax.ShapeDtypeStruct((GROUPS, S...  5.15 us
  transfers between devices with their start and end apart: 3, of which 3 were waited for; matrix products, arithmetic and copies ran while one was open for 4% of the time, Pallas kernels for 0%

profile of v1, /device:TPU:1, one launch (start us, length us, event | category | flops | bytes accessed | tf_op | source)
XLA Modules:
  0.0 103.2 jit_solution(4194331932948835084)
XLA Ops:
  0.6 1.0 reshape.55
  1.6 0.7 broadcast_in_dim.8
  2.3 1.2 %broadcast_in_dim.9 = bf16[8,136,640]{2,1,0:T(8,128)(2,1)} broadcast(bf16[136,640]{1,0:T(8,128)(2,1)S(1)} %pad_maximum_fusion), dimensions={1,2} | broadcast | bytes 1566720 | tf_op jit(solution)/shard_map/broadcast_in_dim | solution.py:208
  3.5 0.0 copy-start.16
  3.5 7.6 %all-to-all-start = ((bf16[8,136,640]{2,1,0:T(8,128)(2,1)}), bf16[8,136,640]{2,1,0:T(8,128)(2,1)S(1)}, u32[]{:S(2)}, u32[]{:S(2)}) async-start(bf16[8,136,640]{2,1,0:T(8,128)(2,1)} %broadcast_in_dim.9), calls=%async_computation | async-start | bytes 2785280 | tf_op jit(solution)/shard_map/all_to_all | solution.py:207
  11.1 0.8 dynamic_slice.3
  11.9 0.1 add_convert_fusion
  12.0 0.1 convert_element_type.12
  12.1 0.0 copy-done.16
  12.1 0.3 copy.16
  12.4 0.9 reshape.56.row_ref
  13.2 0.3 fusion
  13.5 0.7 pad_maximum_fusion.1
  14.3 16.8 %all-to-all-done.x_ref = bf16[8,136,640]{2,1,0:T(8,128)(2,1)S(1)} async-done(((bf16[8,136,640]{2,1,0:T(8,128)(2,1)}), bf16[8,136,640]{2,1,0:T(8,128)(2,1)S(1)}, u32[]{:S(2)}, u32[]{:S(2)}) %all-to-all-start) | async-done | bytes 1392672 | tf_op jit(solution)/shard_map/all_to_all | solution.py:207
  31.1 0.0 copy-start.2
  31.1 1.3 %copy-done.2 = bf16[5120,128]{1,0:T(8,128)(2,1)S(1)} copy-done((bf16[5120,128]{1,0:T(8,128)(2,1)S(1)}, bf16[5120,128]{1,0:T(8,128)(2,1)}, u32[]{:S(2)}) %copy-start.2) | copy-done | bytes 1310744
  32.4 0.0 copy-start.3
  32.4 1.3 %copy-done.3 = bf16[5120,128]{1,0:T(8,128)(2,1)S(1)} copy-done((bf16[5120,128]{1,0:T(8,128)(2,1)S(1)}, bf16[5120,128]{1,0:T(8,128)(2,1)}, u32[]{:S(2)}) %copy-start.3) | copy-done | bytes 1310744
  33.7 0.0 copy-start.4
  33.7 0.8 copy-done.4
  34.6 0.0 copy-start.8
  34.6 0.7 copy-done.8
  35.3 0.0 copy-start.13
  35.3 0.7 copy-done.13
  35.9 0.0 copy-start.14
  35.9 0.7 copy-done.14
  36.6 0.0 copy-start
  36.6 5.2 %project.1 = (bf16[32,32,128]{2,1,0:T(8,128)(2,1)S(1)}, bf16[32,16,128]{2,1,0:T(8,128)(2,1)S(1)}, bf16[128,128]{1,0:T(8,128)(2,1)}, bf16[128,128]{1,0:T(8,128)(2,1)}) custom-call(bf16[8,136,640]{2,1,0:T(8,128)(2,1)S(1)} %all-to-all-done.x_ref, bf16[5120,512]{1,0:T(8,128)(2,1)} %wq_ref.1, bf16[5120,128]{1,0:T(8,128)(2,1)S(1)} %copy-done.2, ...), custom_call_target="tpu_custom_call" | custom-call | tf_op jit(solution)/shard_map/project/pallas_call | solution.py:232
  41.7 0.0 copy-start.5
  41.8 0.7 copy-done.5
  42.5 0.0 copy-start.6
  42.5 0.7 copy-done.6
  43.1 0.0 copy-start.9
  43.1 0.0 copy-start.12
  43.1 10.7 %all-to-all-start.1 = ((bf16[32,32,128]{2,1,0:T(8,128)(2,1)}), bf16[32,32,128]{2,1,0:T(8,128)(2,1)S(1)}, u32[]{:S(2)}, u32[]{:S(2)}) async-start(bf16[32,32,128]{2,1,0:T(8,128)(2,1)} %copy-done.5), calls=%async_computation.1 | async-start | bytes 524288 | tf_op jit(solution)/shard_map/all_to_all | solution.py:249
  53.8 1.0 copy.17
  54.8 0.3 reshape.60.seq_ref
  55.1 10.1 %all-to-all-done.1.q_ref = bf16[32,32,128]{2,1,0:T(8,128)(2,1)S(1)} async-done(((bf16[32,32,128]{2,1,0:T(8,128)(2,1)}), bf16[32,32,128]{2,1,0:T(8,128)(2,1)S(1)}, u32[]{:S(2)}, u32[]{:S(2)}) %all-to-all-start.1) | async-done | bytes 262176 | tf_op jit(solution)/shard_map/all_to_all | solution.py:249
  65.2 0.0 copy-done
  65.2 0.0 copy-done.9
  65.2 0.0 copy-done.12
  65.2 0.0 copy-start.1
  65.3 1.6 %copy-done.1 = bf16[1,32,2,128,128]{4,3,2,1,0:T(8,128)(2,1)S(1)} copy-done((bf16[1,32,2,128,128]{4,3,2,1,0:T(8,128)(2,1)S(1)}, bf16[1,32,2,128,128]{4,3,2,1,0:T(8,128)(2,1)}, u32[]{:S(2)}) %copy-start.1) | copy-done | bytes 2097176
  66.8 0.0 copy-start.7
  66.8 0.0 copy-start.10
  66.8 0.0 copy-start.11
  66.8 0.0 copy-start.15
  66.8 16.9 %pages.1 = bf16[32,40,128]{2,1,0:T(8,128)(2,1)} custom-call(bf16[32,32,128]{2,1,0:T(8,128)(2,1)S(1)} %all-to-all-done.1.q_ref, bf16[64,128,128]{2,1,0:T(8,128)(2,1)S(1)} %bitcast.7, bf16[64,128,128]{2,1,0:T(8,128)(2,1)S(1)} %bitcast.8, s32[1024]{0:T(1024)S(1)} %copy-done.12, s32[2048]{0:T(1024)S(1)} %copy-done.9, s32[2048]{0:T(1024)S(1)} %reshape.60.seq_ref, ...), custom_call_target="tpu_custom_call" | custom-call | tf_op jit(solution)/shard_map/pages/pallas_call | solution.py:261
  83.7 4.5 %all-to-all-start.2 = ((bf16[32,40,128]{2,1,0:T(8,128)(2,1)}), bf16[32,40,128]{2,1,0:T(8,128)(2,1)S(1)}, u32[]{:S(2)}, u32[]{:S(2)}) async-start(bf16[32,40,128]{2,1,0:T(8,128)(2,1)} %pages.1), calls=%async_computation.2 | async-start | bytes 655360 | tf_op jit(solution)/shard_map/all_to_all | solution.py:274
  88.3 0.0 copy-done.7
  88.3 0.0 copy-done.10
  88.3 0.0 copy-done.11
  88.3 0.4 fresh.1
  88.7 12.3 %all-to-all-done.2.got_ref = bf16[32,40,128]{2,1,0:T(8,128)(2,1)S(1)} async-done(((bf16[32,40,128]{2,1,0:T(8,128)(2,1)}), bf16[32,40,128]{2,1,0:T(8,128)(2,1)S(1)}, u32[]{:S(2)}, u32[]{:S(2)}) %all-to-all-start.2) | async-done | bytes 327712 | tf_op jit(solution)/shard_map/all_to_all | solution.py:274
  101.0 0.0 copy-done.15
  101.0 2.2 %combine.1 = bf16[32,4,512]{2,1,0:T(4,128)(2,1)} custom-call(bf16[32,40,128]{2,1,0:T(8,128)(2,1)S(1)} %all-to-all-done.2.got_ref, f32[512,128]{1,0:T(8,128)S(1)} %get-tuple-element.13.lse_ref, f32[512,128]{1,0:T(8,128)S(1)} %get-tuple-element.14.out_ref, s32[2048]{0:T(1024)S(1)} %copy-done.9, s32[2048]{0:T(1024)S(1)} %reshape.60.seq_ref, s32[1]{0:T(128)} %bitcast.2.me_ref, ...), custom_call_target="tpu_custom_call" | custom-call | tf_op jit(solution)/shard_map/combine/pallas_call | solution.py:275
  (2 shorter events, 0.0 us)
Async XLA Ops:
  3.5 8.6 %copy-start.16 = (s32[32,32,2]{1,2,0:T(2,128)S(1)}, s32[32,32,2]{1,2,0:T(2,128)}, u32[]{:S(2)}) copy-start(s32[32,32,2]{1,2,0:T(2,128)} %param.24) | copy-start | bytes 24580
  3.5 27.6 %all-to-all-start = ((bf16[8,136,640]{2,1,0:T(8,128)(2,1)}), bf16[8,136,640]{2,1,0:T(8,128)(2,1)S(1)}, u32[]{:S(2)}, u32[]{:S(2)}) async-start(bf16[8,136,640]{2,1,0:T(8,128)(2,1)} %broadcast_in_dim.9), calls=%async_computation | async-start | bytes 2785280 | tf_op jit(solution)/shard_map/all_to_all | solution.py:207
  31.1 1.3 %copy-start.2 = (bf16[5120,128]{1,0:T(8,128)(2,1)S(1)}, bf16[5120,128]{1,0:T(8,128)(2,1)}, u32[]{:S(2)}) copy-start(bf16[5120,128]{1,0:T(8,128)(2,1)} %wk_ref.1) | copy-start | bytes 3932164
  32.4 1.3 %copy-start.3 = (bf16[5120,128]{1,0:T(8,128)(2,1)S(1)}, bf16[5120,128]{1,0:T(8,128)(2,1)}, u32[]{:S(2)}) copy-start(bf16[5120,128]{1,0:T(8,128)(2,1)} %wv_ref.1) | copy-start | bytes 3932164
  33.7 0.8 copy-start.4
  34.6 0.7 copy-start.8
  35.3 0.7 copy-start.13
  35.9 0.7 copy-start.14
  36.6 28.6 %copy-start = (bf16[1,32,2,128,128]{4,3,2,1,0:T(8,128)(2,1)S(1)}, bf16[1,32,2,128,128]{4,3,2,1,0:T(8,128)(2,1)}, u32[]{:S(2)}) copy-start(bf16[1,32,2,128,128]{4,3,2,1,0:T(8,128)(2,1)} %param.20) | copy-start | bytes 6291460
  41.7 0.7 copy-start.5
  42.5 0.7 copy-start.6
  43.1 22.1 %copy-start.9 = (s32[2048]{0:T(1024)S(1)}, s32[2048]{0:T(1024)}, u32[]{:S(2)}) copy-start(s32[2048]{0:T(1024)} %reshape.56.row_ref) | copy-start | bytes 24580
  43.1 22.1 %copy-start.12 = (s32[1024]{0:T(1024)S(1)}, s32[1024]{0:T(1024)}, u32[]{:S(2)}) copy-start(s32[1024]{0:T(1024)} %len_ref.1) | copy-start | bytes 12292
  43.1 22.1 %all-to-all-start.1 = ((bf16[32,32,128]{2,1,0:T(8,128)(2,1)}), bf16[32,32,128]{2,1,0:T(8,128)(2,1)S(1)}, u32[]{:S(2)}, u32[]{:S(2)}) async-start(bf16[32,32,128]{2,1,0:T(8,128)(2,1)} %copy-done.5), calls=%async_computation.1 | async-start | bytes 524288 | tf_op jit(solution)/shard_map/all_to_all | solution.py:249
  65.2 1.6 %copy-start.1 = (bf16[1,32,2,128,128]{4,3,2,1,0:T(8,128)(2,1)S(1)}, bf16[1,32,2,128,128]{4,3,2,1,0:T(8,128)(2,1)}, u32[]{:S(2)}) copy-start(bf16[1,32,2,128,128]{4,3,2,1,0:T(8,128)(2,1)} %param.21) | copy-start | bytes 6291460
  66.8 21.4 %copy-start.7 = (bf16[32,16,128]{2,1,0:T(8,128)(2,1)S(1)}, bf16[32,16,128]{2,1,0:T(8,128)(2,1)}, u32[]{:S(2)}) copy-start(bf16[32,16,128]{2,1,0:T(8,128)(2,1)} %copy-done.6) | copy-start | bytes 393220
  66.8 21.4 %copy-start.10 = (bf16[128,128]{1,0:T(8,128)(2,1)S(1)}, bf16[128,128]{1,0:T(8,128)(2,1)}, u32[]{:S(2)}) copy-start(bf16[128,128]{1,0:T(8,128)(2,1)} %get-tuple-element.11.key_ref) | copy-start | bytes 98308
  66.8 21.4 %copy-start.11 = (bf16[128,128]{1,0:T(8,128)(2,1)S(1)}, bf16[128,128]{1,0:T(8,128)(2,1)}, u32[]{:S(2)}) copy-start(bf16[128,128]{1,0:T(8,128)(2,1)} %get-tuple-element.12.value_ref) | copy-start | bytes 98308
  66.8 34.2 %copy-start.15 = (s32[32]{0:T(128)S(1)}, s32[32]{0:T(128)}, u32[]{:S(2)}) copy-start(s32[32]{0:T(128)} %remaining_ref.1) | copy-start | bytes 388
  83.7 17.3 %all-to-all-start.2 = ((bf16[32,40,128]{2,1,0:T(8,128)(2,1)}), bf16[32,40,128]{2,1,0:T(8,128)(2,1)S(1)}, u32[]{:S(2)}, u32[]{:S(2)}) async-start(bf16[32,40,128]{2,1,0:T(8,128)(2,1)} %pages.1), calls=%async_computation.2 | async-start | bytes 655360 | tf_op jit(solution)/shard_map/all_to_all | solution.py:274

commit v2 on v1

v2 whole, which is shorter than its diff:
```python
import functools
import math

import jax
import jax.numpy as jnp
from jax import lax
from jax.experimental import pallas as pl
from jax.experimental.pallas import tpu as pltpu
from jax.sharding import PartitionSpec as P

EPSILON = 1e-06
ROPE_BASE = 1000000.0
MASKED = -1e30
ROWS = 32
STEPS = 4
HEADS = 4
QUERIES = HEADS * STEPS
WIDTH = 128
GROUPS = 32
CORES = 2
CHIPS = GROUPS // CORES
SLOTS = 2
SHARED = CORES * SLOTS
TOKENS = ROWS * STEPS
SIDE = 8
SCALE = 1.0 / math.sqrt(WIDTH)

VMEM = pltpu.VMEM
SMEM = pltpu.SMEM


def slot_row(row_ref, holder, owner, c):
    return row_ref[(holder * GROUPS + owner) * SLOTS + c]


def spread_kernel(hidden_hbm, gain_hbm, out_ref, hidden_ref, gain_ref, block_ref, sem):
    features = hidden_hbm.shape[2]
    copies = [
        pltpu.make_async_copy(hidden_hbm, hidden_ref, sem.at[0]),
        pltpu.make_async_copy(gain_hbm, gain_ref, sem.at[1]),
    ]
    for copy in copies:
        copy.start()
    for copy in copies:
        copy.wait()
    tiles = features // WIDTH
    for i in range(0, ROWS, 4):
        part = [hidden_ref[i + k].astype(jnp.float32) for k in range(4)]
        part = jnp.concatenate(part, axis=0).astype(jnp.bfloat16)
        for f in range(tiles):
            first = f * TOKENS + i * STEPS
            block_ref[first : first + 4 * STEPS, :] = part[:, f * WIDTH : (f + 1) * WIDTH]
    gain = gain_ref[...].astype(jnp.float32)
    gain = jnp.concatenate([gain, jnp.zeros((16 - tiles, WIDTH), jnp.float32)], axis=0)
    block_ref[tiles * TOKENS : tiles * TOKENS + 16, :] = gain.astype(jnp.bfloat16)
    copies = [
        pltpu.make_async_copy(block_ref, out_ref.at[t], sem.at[2 + t])
        for t in range(out_ref.shape[0])
    ]
    for copy in copies:
        copy.start()
    for copy in copies:
        copy.wait()


def table_kernel(
    cos_ref, sin_ref, qg_ref, kg_ref, key_hbm, value_hbm, len_ref, row_ref, seq_ref, me_ref,
    turn_out, cap_out, keep_hbm, give_hbm, sem,
):
    me = me_ref[0]
    core = lax.rem(me, CORES)
    copies = []
    for n, pages in enumerate((key_hbm, value_hbm)):
        copies.append(pltpu.make_async_copy(pages.at[:, core], keep_hbm.at[n], sem.at[2 * n]))
        copies.append(
            pltpu.make_async_copy(pages.at[:, 1 - core], give_hbm.at[n], sem.at[2 * n + 1])
        )
    for copy in copies:
        copy.start()
    cos = cos_ref[...]
    sin = sin_ref[...]
    cos = jnp.concatenate([cos, cos], axis=1)
    sin = jnp.concatenate([-sin, sin], axis=1)
    for n, gain_ref in enumerate((qg_ref, kg_ref)):
        gain = jnp.broadcast_to(gain_ref[...].astype(jnp.float32), (8, WIDTH))
        other = pltpu.roll(gain, WIDTH // 2, 1)
        turn_out[2 * n] = cos * gain[0:1]
        turn_out[2 * n + 1] = sin * other[0:1]
    lane = lax.broadcasted_iota(jnp.int32, (1, WIDTH), 1) // QUERIES
    for j in range(GROUPS * SLOTS // 8):
        cap = jnp.zeros((1, WIDTH), jnp.int32)
        for i in range(8):
            chip, k, c = 2 * j + i // SHARED, i // SLOTS % CORES, i % SLOTS
            owner = chip * CORES + core
            holder = me if k == 0 else me + 1 - 2 * core
            place = (holder * GROUPS + owner) * SLOTS + c
            row = row_ref[place]
            length = len_ref[owner * ROWS + jnp.minimum(row, ROWS - 1)]
            cap = jnp.where(
                lane == i, jnp.where(row < ROWS, length - seq_ref[place] * WIDTH, 0), cap
            )
        cap_out[j : j + 1, :] = cap
    for copy in copies:
        copy.wait()


def rotated(heads, cos, sin):
    mean = jnp.sum(heads * heads, axis=1, keepdims=True) * (1.0 / WIDTH)
    scaled = heads * lax.rsqrt(mean + EPSILON)
    return scaled * cos + pltpu.roll(scaled, WIDTH // 2, 1) * sin


def project_kernel(
    x_ref, wq_ref, turn_ref, me_ref, row_hbm,
    send_ref, pack_ref, norm_hbm, norm_ref, row_ref, sem,
):
    rows_copy = pltpu.make_async_copy(row_hbm, row_ref, sem.at[0])
    rows_copy.start()
    count = x_ref.shape[0]
    tiles = wq_ref.shape[0] // count // WIDTH

    def block(n):
        t, f = n // tiles, n % tiles
        return x_ref[t, f * TOKENS : (f + 1) * TOKENS, :].astype(jnp.float32)

    total = jnp.zeros((TOKENS, WIDTH), jnp.float32)
    for n in range(count * tiles):
        x = block(n)
        total = total + x * x
    total = jnp.sum(total, axis=1, keepdims=True)
    rstd = lax.rsqrt(total * (1.0 / (count * tiles * WIDTH)) + EPSILON)
    queries = jnp.zeros((TOKENS, HEADS * WIDTH), jnp.float32)
    chunk = 2 * tiles
    copies = []
    for s in range(0, count * tiles, chunk):
        parts = []
        for n in range(s, s + chunk):
            t, f = n // tiles, n % tiles
            last = tiles * TOKENS
            gain = x_ref[t, last : last + 16, :].astype(jnp.float32)[f : f + 1]
            parts.append((block(n) * rstd * gain).astype(jnp.bfloat16))
        part = jnp.concatenate(parts, axis=1)
        span = slice(s * WIDTH, (s + chunk) * WIDTH)
        norm_ref[:, span] = part
        copies.append(
            pltpu.make_async_copy(
                norm_ref.at[:, span], norm_hbm.at[:, span], sem.at[2 + s // chunk]
            )
        )
        copies[-1].start()
        queries += jnp.dot(part, wq_ref[span, :], preferred_element_type=jnp.float32)
    low = lax.broadcasted_iota(jnp.int32, (8, WIDTH), 0) < STEPS
    turned = [
        rotated(queries[:, h * WIDTH : (h + 1) * WIDTH], turn_ref[0], turn_ref[1])
        for h in range(HEADS)
    ]
    for i in range(ROWS // 2):
        parts = [turned[h][8 * i : 8 * i + 8] for h in range(HEADS)]
        rolled = [pltpu.roll(p, STEPS, 0) for p in parts]
        even = [jnp.where(low, parts[h], rolled[h + 1]) for h in (0, 2)]
        odd = [jnp.where(low, rolled[h], parts[h + 1]) for h in (0, 2)]
        pack_ref[2 * i] = jnp.concatenate(even, axis=0).astype(jnp.bfloat16)
        pack_ref[2 * i + 1] = jnp.concatenate(odd, axis=0).astype(jnp.bfloat16)
    me = me_ref[0]
    rows_copy.wait()
    core = lax.rem(me, CORES)
    for chip in range(CHIPS):
        for k in range(CORES):
            holder = chip * CORES + (core if k == 0 else 1 - core)
            for c in range(SLOTS):
                row = jnp.minimum(slot_row(row_ref, holder, me, c), ROWS - 1)
                first = (k * SLOTS + c) * QUERIES
                send_ref[chip, first : first + QUERIES, :] = pack_ref[row]
    for copy in copies:
        copy.wait()


def fresh_kernel(
    norm_ref, wk_ref, wv_ref, turn_ref, pack_ref, key_ref, value_ref, max_ref, total_ref, out_ref
):
    count = ROWS * QUERIES
    normed = norm_ref[...]
    keys = jnp.dot(normed, wk_ref[...], preferred_element_type=jnp.float32)
    keys = rotated(keys, turn_ref[2], turn_ref[3]).astype(jnp.bfloat16)
    values = jnp.dot(normed, wv_ref[...], preferred_element_type=jnp.float32)
    values = values.astype(jnp.bfloat16)
    key_ref[...] = keys
    value_ref[...] = values
    scores = (
        lax.dot_general(
            pack_ref[...].reshape(count, WIDTH), keys,
            (((1,), (1,)), ((), ())), preferred_element_type=jnp.float32,
        )
        * SCALE
    )
    query = lax.broadcasted_iota(jnp.int32, (count, TOKENS), 0)
    token = lax.broadcasted_iota(jnp.int32, (count, TOKENS), 1)
    usable = ((query >> 4) == (token >> 2)) & ((token & 3) <= (query & 3))
    scores = jnp.where(usable, scores, MASKED)
    top = jnp.max(scores, axis=1, keepdims=True)
    weights = jnp.where(usable, jnp.exp(scores - top), 0.0).astype(jnp.bfloat16)
    total = jnp.sum(weights.astype(jnp.float32), axis=1, keepdims=True)
    out_ref[...] = jnp.dot(weights, values, preferred_element_type=jnp.float32)
    max_ref[...] = jnp.broadcast_to(top, (count, WIDTH))
    total_ref[...] = jnp.broadcast_to(total, (count, WIDTH))


def in_pieces(x):
    high = x.astype(jnp.bfloat16).astype(jnp.float32)
    rest = x - high
    middle = rest.astype(jnp.bfloat16).astype(jnp.float32)
    return [high, middle, rest - middle]


def page_kernel(
    q_ref, keep_ref, got_ref, cap_ref, send_hbm, send_ref, score_ref, weight_ref, sem
):
    token = lax.broadcasted_iota(jnp.int32, (WIDTH, WIDTH), 0)
    member = lax.broadcasted_iota(jnp.int32, (WIDTH, WIDTH), 1) // QUERIES
    side_row = lax.broadcasted_iota(jnp.int32, (SIDE, WIDTH), 0)
    batches = GROUPS * SLOTS // 8
    pairs = SHARED * QUERIES

    def page(n, slot):
        chip, k, c = slot // SHARED, slot // SLOTS % CORES, slot % SLOTS
        return (keep_ref if k == 0 else got_ref)[n, chip, c]

    zero = jnp.zeros((), jnp.bfloat16)
    for j in range(batches):
        queries = q_ref[2 * j : 2 * j + 2].reshape(WIDTH, WIDTH)
        turned = queries.astype(jnp.float32).T.astype(jnp.bfloat16)
        keys = jnp.concatenate([page(0, 8 * j + i) for i in range(8)], axis=1)
        spread = jnp.concatenate([jnp.where(member == i, turned, zero) for i in range(8)], axis=0)
        scores = jnp.dot(keys, spread, preferred_element_type=jnp.float32) * SCALE
        score_ref[j * WIDTH : (j + 1) * WIDTH, :] = jnp.where(
            token < cap_ref[j : j + 1, :], scores, MASKED
        )
    for j in range(batches):
        scores = score_ref[j * WIDTH : (j + 1) * WIDTH, :]
        top = jnp.max(scores, axis=0, keepdims=True)
        weights = jnp.exp(scores - top).astype(jnp.bfloat16).astype(jnp.float32)
        total = jnp.sum(weights, axis=0, keepdims=True)
        weight_ref[j * WIDTH : (j + 1) * WIDTH, :] = weights.T.astype(jnp.bfloat16)
        tile = jnp.zeros((SIDE, WIDTH), jnp.float32)
        for n, piece in enumerate(in_pieces(top) + in_pieces(total)):
            tile = jnp.where(side_row == n, piece, tile)
        for k in range(2):
            send_ref[2 * j + k, pairs : pairs + SIDE, :] = tile.astype(jnp.bfloat16)
    for slot in range(GROUPS * SLOTS):
        out = jnp.dot(
            weight_ref[slot * QUERIES : (slot + 1) * QUERIES, :], page(1, slot),
            preferred_element_type=jnp.float32,
        )
        c = slot % SHARED
        send_ref[slot // SHARED, c * QUERIES : (c + 1) * QUERIES, :] = out.astype(jnp.bfloat16)
    send = pltpu.make_async_copy(send_ref, send_hbm, sem.at[0])
    send.start()
    send.wait()


def combine_kernel(
    got_ref, max_ref, total_ref, out_ref, me_ref, row_hbm, seq_hbm, remaining_hbm,
    attention_ref, top_wide, total_wide, index_ref, row_ref, seq_ref, remaining_ref, sem,
):
    copies = [
        pltpu.make_async_copy(row_hbm, row_ref, sem.at[0]),
        pltpu.make_async_copy(seq_hbm, seq_ref, sem.at[1]),
        pltpu.make_async_copy(remaining_hbm, remaining_ref, sem.at[2]),
    ]
    for copy in copies:
        copy.start()
    me = me_ref[0]
    core = lax.rem(me, CORES)
    pairs = SHARED * QUERIES
    none = GROUPS * SLOTS
    for i in range(ROWS * SLOTS):
        index_ref[i] = none
    sub = lax.broadcasted_iota(jnp.int32, (8, WIDTH), 0)
    tops, totals = [], []
    for b in range(CHIPS // 8):
        top_block = jnp.zeros((8, WIDTH), jnp.float32)
        total_block = jnp.zeros((8, WIDTH), jnp.float32)
        for i in range(8):
            tile = got_ref[8 * b + i, pairs : pairs + SIDE, :].astype(jnp.float32)
            top_block = jnp.where(sub == i, tile[0:1] + tile[1:2] + tile[2:3], top_block)
            total_block = jnp.where(sub == i, tile[3:4] + tile[4:5] + tile[5:6], total_block)
        tops.append(top_block)
        totals.append(total_block)
    side = jnp.concatenate(
        tops + totals + [jnp.zeros((WIDTH - 2 * CHIPS, WIDTH), jnp.float32)], axis=0
    )
    side = pltpu.roll(side, lax.rem((2 - lax.rem(me // CORES, 2)) * pairs, WIDTH), 1).T
    for chip in range(CHIPS):
        for c in range(SHARED):
            span = slice(c * QUERIES, (c + 1) * QUERIES)
            slot = chip * SHARED + c
            top_wide[slot] = jnp.broadcast_to(side[span, chip : chip + 1], (QUERIES, WIDTH))
            total_wide[slot] = jnp.broadcast_to(
                side[span, CHIPS + chip : CHIPS + chip + 1], (QUERIES, WIDTH)
            )
    top_wide[none] = jnp.full((QUERIES, WIDTH), MASKED, jnp.float32)
    total_wide[none] = jnp.zeros((QUERIES, WIDTH), jnp.float32)
    for copy in copies:
        copy.wait()
    for chip in range(CHIPS):
        for c in range(SHARED):
            holder = chip * CORES + (core if c < SLOTS else 1 - core)
            place = (holder * GROUPS + me) * SLOTS + c % SLOTS
            row = row_ref[place]
            index_ref[jnp.where(row < ROWS, row * SLOTS + seq_ref[place], none)] = (
                chip * SHARED + c
            )
    step = lax.broadcasted_iota(jnp.int32, (QUERIES, WIDTH), 0) & (STEPS - 1)
    for r in range(ROWS):
        span = slice(r * QUERIES, (r + 1) * QUERIES)
        tops, totals, outs = [max_ref[span, :]], [total_ref[span, :]], [out_ref[span, :]]
        for k in range(SLOTS):
            slot = index_ref[r * SLOTS + k]
            tops.append(top_wide[slot])
            totals.append(total_wide[slot])
            known = jnp.minimum(slot, none - 1)
            start = pl.multiple_of((known & (SHARED - 1)) * QUERIES, QUERIES)
            outs.append(got_ref[known >> 2, pl.ds(start, QUERIES), :].astype(jnp.float32))
        top = functools.reduce(jnp.maximum, tops)
        factors = [jnp.exp(t - top) for t in tops]
        above = sum(f * o for f, o in zip(factors, outs))
        below = sum(f * t for f, t in zip(factors, totals))
        result = jnp.where(step < remaining_ref[r], above / below, 0.0).astype(jnp.bfloat16)
        for h in range(HEADS):
            attention_ref[r, :, h * WIDTH : (h + 1) * WIDTH] = result[
                h * STEPS : (h + 1) * STEPS, :
            ]


SPREAD_MIB = 60
TABLE_MIB = 4
PROJECT_MIB = 8
FRESH_MIB = 8
PAGES_MIB = 6
COMBINE_MIB = 6
TABLE_COST = 20
PROJECT_COST = 10
FRESH_COST = 10


def limit(mib):
    return pltpu.CompilerParams(vmem_limit_bytes=mib * 1024 * 1024)


def cost(us):
    return pl.CostEstimate(flops=us << 30, bytes_accessed=1 << 20, transcendentals=0)


def shards(
    hidden, norm_gain, w_query, key_projection, value_projection, query_gain, key_gain,
    cache_keys, cached_value_pages, cache_len, remaining, page_row, page_seq,
):
    features = hidden.shape[2]
    tensor = lax.axis_size("tp")
    me = lax.axis_index("dp")
    mine = me.reshape(1).astype(jnp.int32)
    bf16, f32 = jnp.bfloat16, jnp.float32
    width = tensor * features
    slots = GROUPS * SLOTS
    pairs = SHARED * QUERIES
    same_core = [[chip * CORES + core for chip in range(CHIPS)] for core in range(CORES)]
    flip = [(g, g ^ 1) for g in range(GROUPS)]
    vmem = pl.BlockSpec(memory_space=VMEM)
    smem = pl.BlockSpec(memory_space=SMEM)
    hbm = pl.BlockSpec(memory_space=pltpu.HBM)
    shape = jax.ShapeDtypeStruct
    dma = pltpu.SemaphoreType.DMA

    tiles = features // WIDTH
    rows = tiles * TOKENS + 16
    spread = pl.pallas_call(
        spread_kernel,
        out_shape=pltpu.HBM((tensor, rows, WIDTH), bf16),
        in_specs=[hbm, hbm],
        out_specs=hbm,
        scratch_shapes=[
            VMEM(hidden.shape, bf16), VMEM((tiles, WIDTH), bf16), VMEM((rows, WIDTH), bf16),
            dma((2 + tensor,)),
        ],
        compiler_params=limit(SPREAD_MIB),
        name="spread",
    )(hidden, norm_gain.reshape(tiles, WIDTH))
    gathered = lax.all_to_all(spread, "tp", split_axis=0, concat_axis=0, tiled=True)

    lengths = lax.dynamic_slice_in_dim(cache_len, me * ROWS, ROWS)
    positions = (lengths[:, None] + jnp.arange(STEPS, dtype=jnp.int32)[None, :]).reshape(-1, 1)
    frequency = jnp.exp(
        jnp.arange(WIDTH // 2, dtype=f32) * (-2.0 * math.log(ROPE_BASE) / WIDTH)
    )
    angles = positions.astype(f32) * frequency[None, :]
    rows_flat = page_row.reshape(-1)
    seqs_flat = page_seq.reshape(-1)
    page_shape = (CHIPS, CORES, SLOTS, WIDTH, WIDTH)
    moved = (2, CHIPS, SLOTS, WIDTH, WIDTH)
    turns, caps, keep, give = pl.pallas_call(
        table_kernel,
        out_shape=(
            shape((4, TOKENS, WIDTH), f32), shape((slots // 8, WIDTH), jnp.int32),
            pltpu.HBM(moved, bf16), pltpu.HBM(moved, bf16),
        ),
        in_specs=[vmem] * 4 + [hbm] * 2 + [smem] * 4,
        out_specs=(vmem, vmem, hbm, hbm),
        scratch_shapes=[dma((4,))],
        compiler_params=limit(TABLE_MIB),
        cost_estimate=cost(TABLE_COST),
        name="tables",
    )(
        jnp.cos(angles), jnp.sin(angles), query_gain[None, :], key_gain[None, :],
        cache_keys.reshape(page_shape), cached_value_pages.reshape(page_shape),
        cache_len, rows_flat, seqs_flat, mine,
    )
    got = lax.ppermute(give, "dp", flip)
    send_q, pack, normed = pl.pallas_call(
        project_kernel,
        out_shape=(
            VMEM((CHIPS, pairs, WIDTH), bf16),
            shape((ROWS, QUERIES, WIDTH), bf16),
            pltpu.HBM((TOKENS, width), bf16),
        ),
        in_specs=[vmem] * 3 + [smem, hbm],
        out_specs=(vmem, vmem, hbm),
        scratch_shapes=[
            VMEM((TOKENS, width), bf16),
            SMEM((rows_flat.size,), jnp.int32), dma((2 + tensor // 2,)),
        ],
        compiler_params=limit(PROJECT_MIB),
        cost_estimate=cost(PROJECT_COST),
        name="project",
    )(gathered, w_query, turns, mine, rows_flat)
    got_q = lax.all_to_all(
        send_q, "dp", split_axis=0, concat_axis=0, tiled=True, axis_index_groups=same_core
    )
    new_key, new_value, new_max, new_total, new_out = pl.pallas_call(
        fresh_kernel,
        out_shape=(shape((TOKENS, WIDTH), bf16),) * 2
        + (shape((ROWS * QUERIES, WIDTH), f32),) * 3,
        in_specs=[vmem] * 5,
        out_specs=(vmem,) * 5,
        compiler_params=limit(FRESH_MIB),
        cost_estimate=cost(FRESH_COST),
        name="fresh",
    )(normed, key_projection, value_projection, turns, pack)
    send_out = pl.pallas_call(
        page_kernel,
        out_shape=pltpu.HBM((CHIPS, pairs + SIDE, WIDTH), bf16),
        in_specs=[vmem] * 4,
        out_specs=hbm,
        scratch_shapes=[
            VMEM((CHIPS, pairs + SIDE, WIDTH), bf16),
            VMEM((slots * QUERIES, WIDTH), f32),
            VMEM((slots * QUERIES, WIDTH), bf16),
            dma((1,)),
        ],
        compiler_params=limit(PAGES_MIB),
        name="pages",
    )(
        got_q, keep, got, caps,
    )
    got_out = lax.all_to_all(
        send_out, "dp", split_axis=0, concat_axis=0, tiled=True, axis_index_groups=same_core
    )
    attention = pl.pallas_call(
        combine_kernel,
        out_shape=shape((ROWS, STEPS, HEADS * WIDTH), bf16),
        in_specs=[vmem] * 4 + [smem] + [hbm] * 3,
        out_specs=vmem,
        scratch_shapes=[
            VMEM((slots + 1, QUERIES, WIDTH), f32),
            VMEM((slots + 1, QUERIES, WIDTH), f32),
            SMEM((slots + 8,), jnp.int32),
            SMEM((rows_flat.size,), jnp.int32),
            SMEM((seqs_flat.size,), jnp.int32),
            SMEM((ROWS,), jnp.int32),
            dma((3,)),
        ],
        compiler_params=limit(COMBINE_MIB),
        name="combine",
    )(got_out, new_max, new_total, new_out, mine, rows_flat, seqs_flat, remaining)
    return (
        attention,
        new_key.reshape(ROWS, STEPS, WIDTH),
        new_value.reshape(ROWS, STEPS, WIDTH),
    )


def solution(mesh):
    in_specs = (
        P("dp", None, "tp"),
        P("tp"),
        P(None, "tp"),
        P(None, "tp"),
        P(None, "tp"),
        P(),
        P(),
        P("dp", None, None, None, "tp"),
        P("dp", None, None, None, "tp"),
        P(),
        P("dp"),
        P(),
        P(),
    )
    out_specs = (P("dp", None, "tp"), P("dp", None, "tp"), P("dp", None, "tp"))
    return jax.shard_map(shards, mesh=mesh, in_specs=in_specs, out_specs=out_specs, check_vma=False)
```

time: 104 us -> 73.3 us (0.70)
  the two profiles are of different devices: /device:TPU:1 before, /device:TPU:12 now
where the time goes in v2:
time: 73.3 us; the launch traced here: 72.7 us
  blocking collectives  21.2 us (29%)
  local copies, waits for them, and re-layouts  15.2 us (21%)
  Pallas kernels  12.3 us (17%)
  waiting for transfers between devices  11.7 us (16%)
  starting transfers between devices  11 us (15%)
  between operations  0.84 us (1%)
    all_to_all x1, blocking collectives, shards(): lax.all_to_all(send_q, 'dp', split_axis=0, concat_axis=0, tiled=True, axi...  21.2 us
    unnamed x38, local copies, waits for them, and re-layouts  12.4 us
    all_to_all x1, starting transfers between devices, shards(): lax.all_to_all(spread, 'tp', split_axis=0, concat_axis=0, tiled=True)  7.46 us
    all_to_all x1, waiting for transfers between devices, shards(): lax.all_to_all(spread, 'tp', split_axis=0, concat_axis=0, tiled=True)  6.18 us
    all_to_all x1, waiting for transfers between devices, shards(): lax.all_to_all(send_out, 'dp', split_axis=0, concat_axis=0, tiled=True, a...  5.55 us
    all_to_all x1, starting transfers between devices, shards(): lax.all_to_all(send_out, 'dp', split_axis=0, concat_axis=0, tiled=True, a...  3.55 us
    pallas_call x1, Pallas kernels, shards(): pl.pallas_call(table_kernel, out_shape=(shape((4, TOKENS, WIDTH), f32), s...  2.9 us
    pallas_call x1, Pallas kernels, shards(): pl.pallas_call(spread_kernel, out_shape=pltpu.HBM((tensor, rows, WIDTH),...  2.15 us
  transfers between devices with their start and end apart: 3, of which 2 were waited for; matrix products, arithmetic and copies ran while one was open for 7% of the time, Pallas kernels for 8%

profile of v2, /device:TPU:12, one launch (start us, length us, event | category | flops | bytes accessed | tf_op | source)
XLA Modules:
  0.0 72.7 jit_solution(11074176823580082112)
XLA Ops:
  0.6 0.0 copy-start.7
  0.6 0.0 copy-start.16
  0.7 2.2 %spread.1 = bf16[8,656,128]{2,1,0:T(8,128)(2,1)} custom-call(bf16[32,4,640]{2,1,0:T(4,128)(2,1)} %hidden_hbm.1, bf16[5,128]{1,0:T(8,128)(2,1)} %bitcast.12), custom_call_target="tpu_custom_call" | custom-call | tf_op jit(solution)/shard_map/spread/pallas_call | solution.py:376
  2.8 0.0 copy-start.17
  2.8 0.0 copy-start.3
  2.8 0.0 copy-start.8
  2.8 0.0 copy-start.9
  2.9 7.5 %all-to-all-start = ((bf16[8,656,128]{2,1,0:T(8,128)(2,1)}), bf16[8,656,128]{2,1,0:T(8,128)(2,1)S(1)}, u32[]{:S(2)}, u32[]{:S(2)}) async-start(bf16[8,656,128]{2,1,0:T(8,128)(2,1)} %spread.1), calls=%async_computation | async-start | bytes 2686976 | tf_op jit(solution)/shard_map/all_to_all | solution.py:388
  10.3 0.0 copy-done.7
  10.3 0.1 dynamic_slice.3
  10.4 0.1 add_convert_fusion
  10.5 0.1 convert_element_type.12
  10.6 0.0 copy-done.16
  10.6 1.1 %copy.16 = s32[32,32,2]{2,1,0:T(8,128)} copy(s32[32,32,2]{1,2,0:T(2,128)S(1)} %copy-done.16) | data formatting | bytes 16384 | tf_op args[11]
  11.7 1.3 %reshape.56.row_ref.row_hbm = s32[2048]{0:T(1024)S(1)} reshape(s32[32,32,2]{2,1,0:T(8,128)} %copy.16) | data formatting | bytes 16384 | tf_op jit(solution)/shard_map/reshape | solution.py:396
  13.0 0.0 copy-done.17
  13.0 1.1 %copy.17 = s32[32,32,2]{2,1,0:T(8,128)} copy(s32[32,32,2]{1,2,0:T(2,128)S(1)} %copy-done.17) | data formatting | bytes 16384 | tf_op args[12]
  14.1 1.3 %reshape.57.seq_ref.seq_hbm = s32[2048]{0:T(1024)S(1)} reshape(s32[32,32,2]{2,1,0:T(8,128)} %copy.17) | data formatting | bytes 16384 | tf_op jit(solution)/shard_map/reshape | solution.py:397
  15.4 0.3 multiply_sine_fusion
  15.7 0.0 copy-done.3
  15.7 0.0 copy-done.8
  15.7 0.0 copy-done.9
  15.7 0.0 copy-start.4
  15.7 1.6 %copy-done.4 = bf16[1,32,2,128,128]{4,3,2,1,0:T(8,128)(2,1)S(1)} copy-done((bf16[1,32,2,128,128]{4,3,2,1,0:T(8,128)(2,1)S(1)}, bf16[1,32,2,128,128]{4,3,2,1,0:T(8,128)(2,1)}, u32[]{:S(2)}) %copy-start.4) | copy-done | bytes 2097176
  17.3 2.9 %tables.1 = (f32[4,128,128]{2,1,0:T(8,128)S(1)}, s32[8,128]{1,0:T(8,128)S(1)}, bf16[2,16,2,128,128]{4,3,2,1,0:T(8,128)(2,1)}, bf16[2,16,2,128,128]{4,3,2,1,0:T(8,128)(2,1)}) custom-call(f32[128,64]{1,0:T(8,128)S(1)} %get-tuple-element.28.cos_ref, f32[128,64]{1,0:T(8,128)S(1)} %get-tuple-element.27.sin_ref, bf16[1,128]{1,0:T(2,128)(2,1)S(1)} %bitcast.10, ...), custom_call_target="tpu_custom_call" | custom-call | flops 21474836480 | bytes 1048576 | tf_op jit(solution)/shard_map/tables/pallas_call | solution.py:400
  20.2 0.0 copy-start.11
  20.2 0.7 copy-done.11
  20.9 0.0 collective-permute-start
  20.9 6.2 %all-to-all-done.x_ref = bf16[8,656,128]{2,1,0:T(8,128)(2,1)S(1)} async-done(((bf16[8,656,128]{2,1,0:T(8,128)(2,1)}), bf16[8,656,128]{2,1,0:T(8,128)(2,1)S(1)}, u32[]{:S(2)}, u32[]{:S(2)}) %all-to-all-start) | async-done | bytes 1343520 | tf_op jit(solution)/shard_map/all_to_all | solution.py:388
  27.1 0.0 copy-start.2
  27.1 2.5 %copy-done.2 = bf16[5120,512]{1,0:T(8,128)(2,1)S(1)} copy-done((bf16[5120,512]{1,0:T(8,128)(2,1)S(1)}, bf16[5120,512]{1,0:T(8,128)(2,1)}, u32[]{:S(2)}) %copy-start.2) | copy-done | bytes 5242904
  29.6 0.0 copy-start.12
  29.6 0.9 %copy-done.12 = f32[4,128,128]{2,1,0:T(8,128)S(1)} copy-done((f32[4,128,128]{2,1,0:T(8,128)S(1)}, f32[4,128,128]{2,1,0:T(8,128)}, u32[]{:S(2)}) %copy-start.12) | copy-done | bytes 262168
  30.6 0.0 copy-start
  30.6 1.8 %project.1 = (bf16[16,64,128]{2,1,0:T(8,128)(2,1)S(1)}, bf16[32,16,128]{2,1,0:T(8,128)(2,1)S(1)}, bf16[128,5120]{1,0:T(8,128)(2,1)}) custom-call(bf16[8,656,128]{2,1,0:T(8,128)(2,1)S(1)} %all-to-all-done.x_ref, bf16[5120,512]{1,0:T(8,128)(2,1)S(1)} %copy-done.2, f32[4,128,128]{2,1,0:T(8,128)S(1)} %copy-done.12, s32[1]{0:T(128)} %bitcast.5.me_ref, ...), custom_call_target="tpu_custom_call" | custom-call | flops 10737418240 | bytes 1048576 | tf_op jit(solution)/shard_map/project/pallas_call | solution.py:418
  32.4 0.0 copy-start.14
  32.4 21.2 %all_to_all.15.q_ref = bf16[16,64,128]{2,1,0:T(8,128)(2,1)S(1)} all-to-all(bf16[16,64,128]{2,1,0:T(8,128)(2,1)S(1)} %get-tuple-element.16), channel_id=1, replica_groups={{0,16,32,48,64,80,96,112,128,144,160,176,192,208,224,240},{8,24,40,56,7..., dimensions={0} | all-to-all | bytes 524288 | tf_op jit(solution)/shard_map/all_to_all | solution.py:435
  53.6 0.0 collective-permute-done.got_ref
  53.6 0.0 copy-done.14
  53.6 0.0 copy-done
  53.6 0.0 copy-start.5
  53.6 2.0 %pages.1 = bf16[16,72,128]{2,1,0:T(8,128)(2,1)} custom-call(bf16[16,64,128]{2,1,0:T(8,128)(2,1)S(1)} %all_to_all.15.q_ref, bf16[2,16,2,128,128]{4,3,2,1,0:T(8,128)(2,1)S(1)} %copy-done, bf16[2,16,2,128,128]{4,3,2,1,0:T(8,128)(2,1)S(1)} %collective-permute-done.got_ref, s32[8,128]{1,0:T(8,128)S(1)} %get-tuple-element.19.cap_ref), custom_call_target="tpu_custom_call" | custom-call | tf_op jit(solution)/shard_map/pages/pallas_call | solution.py:448
  55.7 3.5 %all-to-all-start.2 = ((bf16[16,72,128]{2,1,0:T(8,128)(2,1)}), bf16[16,72,128]{2,1,0:T(8,128)(2,1)S(1)}, u32[]{:S(2)}, u32[]{:S(2)}) async-start(bf16[16,72,128]{2,1,0:T(8,128)(2,1)} %pages.1), calls=%async_computation.2 | async-start | bytes 589824 | tf_op jit(solution)/shard_map/all_to_all | solution.py:464
  59.2 0.0 copy-done.5
  59.2 0.0 copy-start.6
  59.2 1.3 %copy-done.6 = bf16[5120,128]{1,0:T(8,128)(2,1)S(1)} copy-done((bf16[5120,128]{1,0:T(8,128)(2,1)S(1)}, bf16[5120,128]{1,0:T(8,128)(2,1)}, u32[]{:S(2)}) %copy-start.6) | copy-done | bytes 1310744
  60.5 0.0 copy-start.10
  60.5 1.3 %copy-done.10 = bf16[128,5120]{1,0:T(8,128)(2,1)S(1)} copy-done((bf16[128,5120]{1,0:T(8,128)(2,1)S(1)}, bf16[128,5120]{1,0:T(8,128)(2,1)}, u32[]{:S(2)}) %copy-start.10) | copy-done | bytes 1310744
  61.9 0.0 copy-start.13
  61.9 0.9 %copy-done.13 = f32[4,128,128]{2,1,0:T(8,128)S(1)} copy-done((f32[4,128,128]{2,1,0:T(8,128)S(1)}, f32[4,128,128]{2,1,0:T(8,128)}, u32[]{:S(2)}) %copy-start.13) | copy-done | bytes 262168
  62.8 0.0 copy-start.15
  62.8 0.9 %copy-done.15 = bf16[32,16,128]{2,1,0:T(8,128)(2,1)S(1)} copy-done((bf16[32,16,128]{2,1,0:T(8,128)(2,1)S(1)}, bf16[32,16,128]{2,1,0:T(8,128)(2,1)}, u32[]{:S(2)}) %copy-start.15) | copy-done | bytes 131096
  63.7 0.0 copy-start.1
  63.7 1.5 %fresh.1 = (bf16[128,128]{1,0:T(8,128)(2,1)}, bf16[128,128]{1,0:T(8,128)(2,1)}, f32[512,128]{1,0:T(8,128)S(1)}, f32[512,128]{1,0:T(8,128)S(1)}, f32[512,128]{1,0:T(8,128)S(1)}) custom-call(bf16[128,5120]{1,0:T(8,128)(2,1)S(1)} %copy-done.10, bf16[5120,128]{1,0:T(8,128)(2,1)S(1)} %copy-done.5, bf16[5120,128]{1,0:T(8,128)(2,1)S(1)} %copy-done.6, ...), custom_call_target="tpu_custom_call" | custom-call | flops 10737418240 | bytes 1048576 | tf_op jit(solution)/shard_map/fresh/pallas_call | solution.py:438
  65.2 5.6 %all-to-all-done.2.got_ref = bf16[16,72,128]{2,1,0:T(8,128)(2,1)S(1)} async-done(((bf16[16,72,128]{2,1,0:T(8,128)(2,1)}), bf16[16,72,128]{2,1,0:T(8,128)(2,1)S(1)}, u32[]{:S(2)}, u32[]{:S(2)}) %all-to-all-start.2) | async-done | bytes 294944 | tf_op jit(solution)/shard_map/all_to_all | solution.py:464
  70.7 0.0 copy-done.1
  70.7 2.0 %combine.1 = bf16[32,4,512]{2,1,0:T(4,128)(2,1)} custom-call(bf16[16,72,128]{2,1,0:T(8,128)(2,1)S(1)} %all-to-all-done.2.got_ref, f32[512,128]{1,0:T(8,128)S(1)} %get-tuple-element.22.max_ref, f32[512,128]{1,0:T(8,128)S(1)} %get-tuple-element.23.total_ref, f32[512,128]{1,0:T(8,128)S(1)} %get-tuple-element.24.out_ref, s32[1]{0:T(128)} %bitcast.5.me_ref, ...), custom_call_target="tpu_custom_call" | custom-call | tf_op jit(solution)/shard_map/combine/pallas_call | solution.py:467
  (1 shorter events, 0.0 us)
Async XLA Ops:
  0.6 9.7 %copy-start.7 = (s32[1024]{0:T(1024)S(1)}, s32[1024]{0:T(1024)}, u32[]{:S(2)}) copy-start(s32[1024]{0:T(1024)} %len_ref.1) | copy-start | bytes 12292
  0.6 10.0 %copy-start.16 = (s32[32,32,2]{1,2,0:T(2,128)S(1)}, s32[32,32,2]{1,2,0:T(2,128)}, u32[]{:S(2)}) copy-start(s32[32,32,2]{1,2,0:T(2,128)} %param.24) | copy-start | bytes 24580
  2.8 10.2 %copy-start.17 = (s32[32,32,2]{1,2,0:T(2,128)S(1)}, s32[32,32,2]{1,2,0:T(2,128)}, u32[]{:S(2)}) copy-start(s32[32,32,2]{1,2,0:T(2,128)} %param.25) | copy-start | bytes 24580
  2.8 12.9 %copy-start.3 = (bf16[1,32,2,128,128]{4,3,2,1,0:T(8,128)(2,1)S(1)}, bf16[1,32,2,128,128]{4,3,2,1,0:T(8,128)(2,1)}, u32[]{:S(2)}) copy-start(bf16[1,32,2,128,128]{4,3,2,1,0:T(8,128)(2,1)} %param.20) | copy-start | bytes 6291460
  2.8 12.9 %copy-start.8 = (bf16[128]{0:T(256)(128)(2,1)S(1)}, bf16[128]{0:T(256)(128)(2,1)}, u32[]{:S(2)}) copy-start(bf16[128]{0:T(256)(128)(2,1)} %param.18) | copy-start | bytes 772
  2.8 12.9 %copy-start.9 = (bf16[128]{0:T(256)(128)(2,1)S(1)}, bf16[128]{0:T(256)(128)(2,1)}, u32[]{:S(2)}) copy-start(bf16[128]{0:T(256)(128)(2,1)} %param.19) | copy-start | bytes 772
  2.9 24.3 %all-to-all-start = ((bf16[8,656,128]{2,1,0:T(8,128)(2,1)}), bf16[8,656,128]{2,1,0:T(8,128)(2,1)S(1)}, u32[]{:S(2)}, u32[]{:S(2)}) async-start(bf16[8,656,128]{2,1,0:T(8,128)(2,1)} %spread.1), calls=%async_computation | async-start | bytes 2686976 | tf_op jit(solution)/shard_map/all_to_all | solution.py:388
  15.7 1.6 %copy-start.4 = (bf16[1,32,2,128,128]{4,3,2,1,0:T(8,128)(2,1)S(1)}, bf16[1,32,2,128,128]{4,3,2,1,0:T(8,128)(2,1)}, u32[]{:S(2)}) copy-start(bf16[1,32,2,128,128]{4,3,2,1,0:T(8,128)(2,1)} %param.21) | copy-start | bytes 6291460
  20.2 0.7 copy-start.11
  20.9 32.6 %collective-permute-start = (bf16[2,16,2,128,128]{4,3,2,1,0:T(8,128)(2,1)}, bf16[2,16,2,128,128]{4,3,2,1,0:T(8,128)(2,1)S(1)}, u32[]{:S(2)}, u32[]{:S(2)}) collective-permute-start(bf16[2,16,2,128,128]{4,3,2,1,0:T(8,128)(2,1)} %get-tuple-element.18), channel_id=1, source_target_pairs={{0,8},{8,0},{16,24},{24,16},{32,40},{40,32},{48,56},{56,48},{64,72... | collective-permute-start | bytes 6291464 | tf_op jit(solution)/shard_map/ppermute | solution.py:417
  27.1 2.5 %copy-start.2 = (bf16[5120,512]{1,0:T(8,128)(2,1)S(1)}, bf16[5120,512]{1,0:T(8,128)(2,1)}, u32[]{:S(2)}) copy-start(bf16[5120,512]{1,0:T(8,128)(2,1)} %wq_ref.1) | copy-start | bytes 15728644
  29.6 0.9 %copy-start.12 = (f32[4,128,128]{2,1,0:T(8,128)S(1)}, f32[4,128,128]{2,1,0:T(8,128)}, u32[]{:S(2)}) copy-start(f32[4,128,128]{2,1,0:T(8,128)} %copy-done.11) | copy-start | bytes 786436
  30.6 23.0 %copy-start = (bf16[2,16,2,128,128]{4,3,2,1,0:T(8,128)(2,1)S(1)}, bf16[2,16,2,128,128]{4,3,2,1,0:T(8,128)(2,1)}, u32[]{:S(2)}) copy-start(bf16[2,16,2,128,128]{4,3,2,1,0:T(8,128)(2,1)} %get-tuple-element.17.keep_ref) | copy-start | bytes 6291460
  32.4 21.2 %copy-start.14 = (bf16[32,16,128]{2,1,0:T(8,128)(2,1)}, bf16[32,16,128]{2,1,0:T(8,128)(2,1)S(1)}, u32[]{:S(2)}) copy-start(bf16[32,16,128]{2,1,0:T(8,128)(2,1)S(1)} %get-tuple-element.21.pack_ref) | copy-start | bytes 393220
  53.6 5.6 %copy-start.5 = (bf16[5120,128]{1,0:T(8,128)(2,1)S(1)}, bf16[5120,128]{1,0:T(8,128)(2,1)}, u32[]{:S(2)}) copy-start(bf16[5120,128]{1,0:T(8,128)(2,1)} %wk_ref.1) | copy-start | bytes 3932164
  55.7 15.1 %all-to-all-start.2 = ((bf16[16,72,128]{2,1,0:T(8,128)(2,1)}), bf16[16,72,128]{2,1,0:T(8,128)(2,1)S(1)}, u32[]{:S(2)}, u32[]{:S(2)}) async-start(bf16[16,72,128]{2,1,0:T(8,128)(2,1)} %pages.1), calls=%async_computation.2 | async-start | bytes 589824 | tf_op jit(solution)/shard_map/all_to_all | solution.py:464
  59.2 1.3 %copy-start.6 = (bf16[5120,128]{1,0:T(8,128)(2,1)S(1)}, bf16[5120,128]{1,0:T(8,128)(2,1)}, u32[]{:S(2)}) copy-start(bf16[5120,128]{1,0:T(8,128)(2,1)} %wv_ref.1) | copy-start | bytes 3932164
  60.5 1.3 %copy-start.10 = (bf16[128,5120]{1,0:T(8,128)(2,1)S(1)}, bf16[128,5120]{1,0:T(8,128)(2,1)}, u32[]{:S(2)}) copy-start(bf16[128,5120]{1,0:T(8,128)(2,1)} %get-tuple-element.20.norm_ref) | copy-start | bytes 3932164
  61.9 0.9 %copy-start.13 = (f32[4,128,128]{2,1,0:T(8,128)S(1)}, f32[4,128,128]{2,1,0:T(8,128)}, u32[]{:S(2)}) copy-start(f32[4,128,128]{2,1,0:T(8,128)} %copy-done.11) | copy-start | bytes 786436
  62.8 0.9 %copy-start.15 = (bf16[32,16,128]{2,1,0:T(8,128)(2,1)S(1)}, bf16[32,16,128]{2,1,0:T(8,128)(2,1)}, u32[]{:S(2)}) copy-start(bf16[32,16,128]{2,1,0:T(8,128)(2,1)} %copy-done.14) | copy-start | bytes 393220
  63.7 7.0 %copy-start.1 = (s32[32]{0:T(128)S(1)}, s32[32]{0:T(128)}, u32[]{:S(2)}) copy-start(s32[32]{0:T(128)} %remaining_hbm.1) | copy-start | bytes 388

commit v3 on v2

--- a/solution.py
+++ b/solution.py
@@ -64,10 +64,9 @@
 
 
 def table_kernel(
-    cos_ref, sin_ref, qg_ref, kg_ref, key_hbm, value_hbm, len_ref, row_ref, seq_ref, me_ref,
-    turn_out, cap_out, keep_hbm, give_hbm, sem,
+    key_hbm, value_hbm, len_ref, row_ref, seq_ref, turn_out, cap_out, keep_hbm, give_hbm, sem
 ):
-    me = me_ref[0]
+    me = lax.axis_index("dp")
     core = lax.rem(me, CORES)
     copies = []
     for n, pages in enumerate((key_hbm, value_hbm)):
@@ -77,15 +76,14 @@
         )
     for copy in copies:
         copy.start()
-    cos = cos_ref[...]
-    sin = sin_ref[...]
-    cos = jnp.concatenate([cos, cos], axis=1)
-    sin = jnp.concatenate([-sin, sin], axis=1)
-    for n, gain_ref in enumerate((qg_ref, kg_ref)):
-        gain = jnp.broadcast_to(gain_ref[...].astype(jnp.float32), (8, WIDTH))
-        other = pltpu.roll(gain, WIDTH // 2, 1)
-        turn_out[2 * n] = cos * gain[0:1]
-        turn_out[2 * n + 1] = sin * other[0:1]
+    row = lax.broadcasted_iota(jnp.int32, (TOKENS, WIDTH), 0)
+    position = row & (STEPS - 1)
+    for r in range(ROWS):
+        position = position + jnp.where(row // STEPS == r, len_ref[me * ROWS + r], 0)
+    column = lax.broadcasted_iota(jnp.int32, (TOKENS, WIDTH), 1)
+    half = (column & (WIDTH // 2 - 1)).astype(jnp.float32)
+    angle = position.astype(jnp.float32) * jnp.exp(half * (-2.0 * math.log(ROPE_BASE) / WIDTH))
+    turn_out[...] = jnp.where(column < WIDTH // 2, jnp.cos(angle), jnp.sin(angle))
     lane = lax.broadcasted_iota(jnp.int32, (1, WIDTH), 1) // QUERIES
     for j in range(GROUPS * SLOTS // 8):
         cap = jnp.zeros((1, WIDTH), jnp.int32)
@@ -104,14 +102,20 @@
         copy.wait()
 
 
-def rotated(heads, cos, sin):
+def unpacked(turn):
+    other = pltpu.roll(turn, WIDTH // 2, 1)
+    left = lax.broadcasted_iota(jnp.int32, turn.shape, 1) < WIDTH // 2
+    return jnp.where(left, turn, other), jnp.where(left, -other, turn)
+
+
+def rotated(heads, gain, cos, sin):
     mean = jnp.sum(heads * heads, axis=1, keepdims=True) * (1.0 / WIDTH)
-    scaled = heads * lax.rsqrt(mean + EPSILON)
+    scaled = heads * lax.rsqrt(mean + EPSILON) * gain
     return scaled * cos + pltpu.roll(scaled, WIDTH // 2, 1) * sin
 
 
 def project_kernel(
-    x_ref, wq_ref, turn_ref, me_ref, row_hbm,
+    x_ref, wq_ref, qg_ref, turn_ref, row_hbm,
     send_ref, pack_ref, norm_hbm, norm_ref, row_ref, sem,
 ):
     rows_copy = pltpu.make_async_copy(row_hbm, row_ref, sem.at[0])
@@ -144,14 +148,16 @@
         norm_ref[:, span] = part
         copies.append(
             pltpu.make_async_copy(
-                norm_ref.at[:, span], norm_hbm.at[:, span], sem.at[2 + s // chunk]
+                norm_ref.at[:, span], norm_hbm.at[:, span], sem.at[1 + s // chunk]
             )
         )
         copies[-1].start()
         queries += jnp.dot(part, wq_ref[span, :], preferred_element_type=jnp.float32)
+    cos, sin = unpacked(turn_ref[...])
+    q_gain = qg_ref[...].astype(jnp.float32)
     low = lax.broadcasted_iota(jnp.int32, (8, WIDTH), 0) < STEPS
     turned = [
-        rotated(queries[:, h * WIDTH : (h + 1) * WIDTH], turn_ref[0], turn_ref[1])
+        rotated(queries[:, h * WIDTH : (h + 1) * WIDTH], q_gain, cos, sin)
         for h in range(HEADS)
     ]
     for i in range(ROWS // 2):
@@ -161,7 +167,7 @@
         odd = [jnp.where(low, rolled[h], parts[h + 1]) for h in (0, 2)]
         pack_ref[2 * i] = jnp.concatenate(even, axis=0).astype(jnp.bfloat16)
         pack_ref[2 * i + 1] = jnp.concatenate(odd, axis=0).astype(jnp.bfloat16)
-    me = me_ref[0]
+    me = lax.axis_index("dp")
     rows_copy.wait()
     core = lax.rem(me, CORES)
     for chip in range(CHIPS):
@@ -176,12 +182,15 @@
 
 
 def fresh_kernel(
-    norm_ref, wk_ref, wv_ref, turn_ref, pack_ref, key_ref, value_ref, max_ref, total_ref, out_ref
+    norm_ref, wk_ref, wv_ref, kg_ref, turn_ref, pack_ref,
+    key_ref, value_ref, max_ref, total_ref, out_ref,
 ):
     count = ROWS * QUERIES
     normed = norm_ref[...]
     keys = jnp.dot(normed, wk_ref[...], preferred_element_type=jnp.float32)
-    keys = rotated(keys, turn_ref[2], turn_ref[3]).astype(jnp.bfloat16)
+    keys = rotated(
+        keys, kg_ref[...].astype(jnp.float32), *unpacked(turn_ref[...])
+    ).astype(jnp.bfloat16)
     values = jnp.dot(normed, wv_ref[...], preferred_element_type=jnp.float32)
     values = values.astype(jnp.bfloat16)
     key_ref[...] = keys
@@ -259,7 +268,7 @@
 
 
 def combine_kernel(
-    got_ref, max_ref, total_ref, out_ref, me_ref, row_hbm, seq_hbm, remaining_hbm,
+    got_ref, max_ref, total_ref, out_ref, row_hbm, seq_hbm, remaining_hbm,
     attention_ref, top_wide, total_wide, index_ref, row_ref, seq_ref, remaining_ref, sem,
 ):
     copies = [
@@ -269,7 +278,7 @@
     ]
     for copy in copies:
         copy.start()
-    me = me_ref[0]
+    me = lax.axis_index("dp")
     core = lax.rem(me, CORES)
     pairs = SHARED * QUERIES
     none = GROUPS * SLOTS
@@ -357,8 +366,6 @@
 ):
     features = hidden.shape[2]
     tensor = lax.axis_size("tp")
-    me = lax.axis_index("dp")
-    mine = me.reshape(1).astype(jnp.int32)
     bf16, f32 = jnp.bfloat16, jnp.float32
     width = tensor * features
     slots = GROUPS * SLOTS
@@ -387,12 +394,6 @@
     )(hidden, norm_gain.reshape(tiles, WIDTH))
     gathered = lax.all_to_all(spread, "tp", split_axis=0, concat_axis=0, tiled=True)
 
-    lengths = lax.dynamic_slice_in_dim(cache_len, me * ROWS, ROWS)
-    positions = (lengths[:, None] + jnp.arange(STEPS, dtype=jnp.int32)[None, :]).reshape(-1, 1)
-    frequency = jnp.exp(
-        jnp.arange(WIDTH // 2, dtype=f32) * (-2.0 * math.log(ROPE_BASE) / WIDTH)
-    )
-    angles = positions.astype(f32) * frequency[None, :]
     rows_flat = page_row.reshape(-1)
     seqs_flat = page_seq.reshape(-1)
     page_shape = (CHIPS, CORES, SLOTS, WIDTH, WIDTH)
@@ -400,19 +401,18 @@
     turns, caps, keep, give = pl.pallas_call(
         table_kernel,
         out_shape=(
-            shape((4, TOKENS, WIDTH), f32), shape((slots // 8, WIDTH), jnp.int32),
+            shape((TOKENS, WIDTH), f32), shape((slots // 8, WIDTH), jnp.int32),
             pltpu.HBM(moved, bf16), pltpu.HBM(moved, bf16),
         ),
-        in_specs=[vmem] * 4 + [hbm] * 2 + [smem] * 4,
+        in_specs=[hbm] * 2 + [smem] * 3,
         out_specs=(vmem, vmem, hbm, hbm),
         scratch_shapes=[dma((4,))],
         compiler_params=limit(TABLE_MIB),
         cost_estimate=cost(TABLE_COST),
         name="tables",
     )(
-        jnp.cos(angles), jnp.sin(angles), query_gain[None, :], key_gain[None, :],
         cache_keys.reshape(page_shape), cached_value_pages.reshape(page_shape),
-        cache_len, rows_flat, seqs_flat, mine,
+        cache_len, rows_flat, seqs_flat,
     )
     got = lax.ppermute(give, "dp", flip)
     send_q, pack, normed = pl.pallas_call(
@@ -422,16 +422,16 @@
             shape((ROWS, QUERIES, WIDTH), bf16),
             pltpu.HBM((TOKENS, width), bf16),
         ),
-        in_specs=[vmem] * 3 + [smem, hbm],
+        in_specs=[vmem] * 4 + [hbm],
         out_specs=(vmem, vmem, hbm),
         scratch_shapes=[
             VMEM((TOKENS, width), bf16),
-            SMEM((rows_flat.size,), jnp.int32), dma((2 + tensor // 2,)),
+            SMEM((rows_flat.size,), jnp.int32), dma((1 + tensor // 2,)),
         ],
         compiler_params=limit(PROJECT_MIB),
         cost_estimate=cost(PROJECT_COST),
         name="project",
-    )(gathered, w_query, turns, mine, rows_flat)
+    )(gathered, w_query, query_gain[None, :], turns, rows_flat)
     got_q = lax.all_to_all(
         send_q, "dp", split_axis=0, concat_axis=0, tiled=True, axis_index_groups=same_core
     )
@@ -439,12 +439,12 @@
         fresh_kernel,
         out_shape=(shape((TOKENS, WIDTH), bf16),) * 2
         + (shape((ROWS * QUERIES, WIDTH), f32),) * 3,
-        in_specs=[vmem] * 5,
+        in_specs=[vmem] * 6,
         out_specs=(vmem,) * 5,
         compiler_params=limit(FRESH_MIB),
         cost_estimate=cost(FRESH_COST),
         name="fresh",
-    )(normed, key_projection, value_projection, turns, pack)
+    )(normed, key_projection, value_projection, key_gain[None, :], turns, pack)
     send_out = pl.pallas_call(
         page_kernel,
         out_shape=pltpu.HBM((CHIPS, pairs + SIDE, WIDTH), bf16),
@@ -467,7 +467,7 @@
     attention = pl.pallas_call(
         combine_kernel,
         out_shape=shape((ROWS, STEPS, HEADS * WIDTH), bf16),
-        in_specs=[vmem] * 4 + [smem] + [hbm] * 3,
+        in_specs=[vmem] * 4 + [hbm] * 3,
         out_specs=vmem,
         scratch_shapes=[
             VMEM((slots + 1, QUERIES, WIDTH), f32),
@@ -480,7 +480,7 @@
         ],
         compiler_params=limit(COMBINE_MIB),
         name="combine",
-    )(got_out, new_max, new_total, new_out, mine, rows_flat, seqs_flat, remaining)
+    )(got_out, new_max, new_total, new_out, rows_flat, seqs_flat, remaining)
     return (
         attention,
         new_key.reshape(ROWS, STEPS, WIDTH),

time: 73.3 us -> 72.2 us (0.985)
  local copies, waits for them, and re-layouts: 15.2 us -> 12.4 us
  waiting for transfers between devices: 11.7 us -> 13.9 us
    unnamed x38 -> x32, local copies, waits for them, and re-layouts: 12.4 us -> 9.81 us
    all_to_all x1, waiting for transfers between devices: 6.18 us -> 7.44 us  [shards(): lax.all_to_all(spread, 'tp', split_axis=0, concat_axis=0, tiled=True)]
    all_to_all x1, waiting for transfers between devices: 5.55 us -> 6.49 us  [shards(): lax.all_to_all(send_out, 'dp', split_axis=0, concat_axis=0, tiled=True, a...]
where the time goes in v3:
time: 72.2 us; the launch traced here: 71.7 us
  blocking collectives  21.2 us (29%)
  waiting for transfers between devices  13.9 us (19%)
  local copies, waits for them, and re-layouts  12.4 us (17%)
  Pallas kernels  12.2 us (17%)
  starting transfers between devices  11.1 us (15%)
  between operations  0.79 us (1%)
    all_to_all x1, blocking collectives, shards(): lax.all_to_all(send_q, 'dp', split_axis=0, concat_axis=0, tiled=True, axi...  21.2 us
    unnamed x32, local copies, waits for them, and re-layouts  9.81 us
    all_to_all x1, starting transfers between devices, shards(): lax.all_to_all(spread, 'tp', split_axis=0, concat_axis=0, tiled=True)  7.46 us
    all_to_all x1, waiting for transfers between devices, shards(): lax.all_to_all(spread, 'tp', split_axis=0, concat_axis=0, tiled=True)  7.44 us
    all_to_all x1, waiting for transfers between devices, shards(): lax.all_to_all(send_out, 'dp', split_axis=0, concat_axis=0, tiled=True, a...  6.49 us
    all_to_all x1, starting transfers between devices, shards(): lax.all_to_all(send_out, 'dp', split_axis=0, concat_axis=0, tiled=True, a...  3.55 us
    pallas_call x1, Pallas kernels, shards(): pl.pallas_call(table_kernel, out_shape=(shape((TOKENS, WIDTH), f32), shap...  2.86 us
    pallas_call x1, Pallas kernels, shards(): pl.pallas_call(spread_kernel, out_shape=pltpu.HBM((tensor, rows, WIDTH),...  2.15 us
  transfers between devices with their start and end apart: 3, of which 2 were waited for; matrix products, arithmetic and copies ran while one was open for 7% of the time, Pallas kernels for 8%

profile of v3, /device:TPU:12, one launch (start us, length us, event | category | flops | bytes accessed | tf_op | source)
XLA Modules:
  0.0 71.7 jit_solution(16219140758630712028)
XLA Ops:
  0.6 0.0 copy-start.13
  0.6 2.2 %spread.1 = bf16[8,656,128]{2,1,0:T(8,128)(2,1)} custom-call(bf16[32,4,640]{2,1,0:T(4,128)(2,1)} %hidden_hbm.1, bf16[5,128]{1,0:T(8,128)(2,1)} %bitcast.11), custom_call_target="tpu_custom_call" | custom-call | tf_op jit(solution)/shard_map/spread/pallas_call | solution.py:383
  2.8 0.0 copy-start.14
  2.8 0.0 copy-start.3
  2.8 0.0 copy-start.7
  2.8 7.5 %all-to-all-start = ((bf16[8,656,128]{2,1,0:T(8,128)(2,1)}), bf16[8,656,128]{2,1,0:T(8,128)(2,1)S(1)}, u32[]{:S(2)}, u32[]{:S(2)}) async-start(bf16[8,656,128]{2,1,0:T(8,128)(2,1)} %spread.1), calls=%async_computation | async-start | bytes 2686976 | tf_op jit(solution)/shard_map/all_to_all | solution.py:395
  10.3 0.0 copy-done.13
  10.3 1.1 %copy.16 = s32[32,32,2]{2,1,0:T(8,128)} copy(s32[32,32,2]{1,2,0:T(2,128)S(1)} %copy-done.13) | data formatting | bytes 16384 | tf_op args[11]
  11.4 1.3 %reshape.30.row_ref.row_hbm = s32[2048]{0:T(1024)S(1)} reshape(s32[32,32,2]{2,1,0:T(8,128)} %copy.16) | data formatting | bytes 16384 | tf_op jit(solution)/shard_map/reshape | solution.py:397
  12.7 0.0 copy-done.14
  12.7 1.1 %copy.17 = s32[32,32,2]{2,1,0:T(8,128)} copy(s32[32,32,2]{1,2,0:T(2,128)S(1)} %copy-done.14) | data formatting | bytes 16384 | tf_op args[12]
  13.8 1.3 %reshape.31.seq_ref.seq_hbm = s32[2048]{0:T(1024)S(1)} reshape(s32[32,32,2]{2,1,0:T(8,128)} %copy.17) | data formatting | bytes 16384 | tf_op jit(solution)/shard_map/reshape | solution.py:398
  15.1 0.0 copy-done.3
  15.1 0.0 copy-done.7
  15.1 0.0 copy-start.4
  15.1 1.6 %copy-done.4 = bf16[1,32,2,128,128]{4,3,2,1,0:T(8,128)(2,1)S(1)} copy-done((bf16[1,32,2,128,128]{4,3,2,1,0:T(8,128)(2,1)S(1)}, bf16[1,32,2,128,128]{4,3,2,1,0:T(8,128)(2,1)}, u32[]{:S(2)}) %copy-start.4) | copy-done | bytes 2097176
  16.7 0.0 copy-start.8
  16.7 2.9 %tables.1 = (f32[128,128]{1,0:T(8,128)S(1)}, s32[8,128]{1,0:T(8,128)S(1)}, bf16[2,16,2,128,128]{4,3,2,1,0:T(8,128)(2,1)}, bf16[2,16,2,128,128]{4,3,2,1,0:T(8,128)(2,1)}) custom-call(bf16[16,2,2,128,128]{4,3,2,1,0:T(8,128)(2,1)S(1)} %bitcast.7, bf16[16,2,2,128,128]{4,3,2,1,0:T(8,128)(2,1)S(1)} %bitcast.8, s32[1024]{0:T(1024)S(1)} %copy-done.7, ...), custom_call_target="tpu_custom_call" | custom-call | flops 21474836480 | bytes 1048576 | tf_op jit(solution)/shard_map/tables/pallas_call | solution.py:401
  19.6 0.1 collective-permute-start
  19.7 7.4 %all-to-all-done.x_ref = bf16[8,656,128]{2,1,0:T(8,128)(2,1)S(1)} async-done(((bf16[8,656,128]{2,1,0:T(8,128)(2,1)}), bf16[8,656,128]{2,1,0:T(8,128)(2,1)S(1)}, u32[]{:S(2)}, u32[]{:S(2)}) %all-to-all-start) | async-done | bytes 1343520 | tf_op jit(solution)/shard_map/all_to_all | solution.py:395
  27.1 0.0 copy-done.8
  27.1 0.0 copy-start.2
  27.1 2.5 %copy-done.2 = bf16[5120,512]{1,0:T(8,128)(2,1)S(1)} copy-done((bf16[5120,512]{1,0:T(8,128)(2,1)S(1)}, bf16[5120,512]{1,0:T(8,128)(2,1)}, u32[]{:S(2)}) %copy-start.2) | copy-done | bytes 5242904
  29.6 0.0 copy-start
  29.6 1.7 %project.1 = (bf16[16,64,128]{2,1,0:T(8,128)(2,1)S(1)}, bf16[32,16,128]{2,1,0:T(8,128)(2,1)S(1)}, bf16[128,5120]{1,0:T(8,128)(2,1)}) custom-call(bf16[8,656,128]{2,1,0:T(8,128)(2,1)S(1)} %all-to-all-done.x_ref, bf16[5120,512]{1,0:T(8,128)(2,1)S(1)} %copy-done.2, bf16[1,128]{1,0:T(2,128)(2,1)S(1)} %bitcast.9, f32[128,128]{1,0:T(8,128)S(1)} %get-tuple-element.15.turn_ref, ...), custom_call_target="tpu_custom_call" | custom-call | flops 10737418240 | bytes 1048576 | tf_op jit(solution)/shard_map/project/pallas_call | solution.py:418
  31.3 0.0 copy-start.11
  31.3 21.2 %all_to_all.15.q_ref = bf16[16,64,128]{2,1,0:T(8,128)(2,1)S(1)} all-to-all(bf16[16,64,128]{2,1,0:T(8,128)(2,1)S(1)} %get-tuple-element.16), channel_id=1, replica_groups={{0,16,32,48,64,80,96,112,128,144,160,176,192,208,224,240},{8,24,40,56,7..., dimensions={0} | all-to-all | bytes 524288 | tf_op jit(solution)/shard_map/all_to_all | solution.py:435
  52.5 0.0 collective-permute-done.got_ref
  52.5 0.0 copy-done.11
  52.5 0.0 copy-done
  52.5 0.0 copy-start.5
  52.5 0.0 copy-start.9
  52.5 2.1 %pages.1 = bf16[16,72,128]{2,1,0:T(8,128)(2,1)} custom-call(bf16[16,64,128]{2,1,0:T(8,128)(2,1)S(1)} %all_to_all.15.q_ref, bf16[2,16,2,128,128]{4,3,2,1,0:T(8,128)(2,1)S(1)} %copy-done, bf16[2,16,2,128,128]{4,3,2,1,0:T(8,128)(2,1)S(1)} %collective-permute-done.got_ref, s32[8,128]{1,0:T(8,128)S(1)} %get-tuple-element.19.cap_ref), custom_call_target="tpu_custom_call" | custom-call | tf_op jit(solution)/shard_map/pages/pallas_call | solution.py:448
  54.6 3.5 %all-to-all-start.2 = ((bf16[16,72,128]{2,1,0:T(8,128)(2,1)}), bf16[16,72,128]{2,1,0:T(8,128)(2,1)S(1)}, u32[]{:S(2)}, u32[]{:S(2)}) async-start(bf16[16,72,128]{2,1,0:T(8,128)(2,1)} %pages.1), calls=%async_computation.2 | async-start | bytes 589824 | tf_op jit(solution)/shard_map/all_to_all | solution.py:464
  58.2 0.0 copy-done.5
  58.2 0.0 copy-done.9
  58.2 0.0 copy-start.6
  58.2 1.3 %copy-done.6 = bf16[5120,128]{1,0:T(8,128)(2,1)S(1)} copy-done((bf16[5120,128]{1,0:T(8,128)(2,1)S(1)}, bf16[5120,128]{1,0:T(8,128)(2,1)}, u32[]{:S(2)}) %copy-start.6) | copy-done | bytes 1310744
  59.5 0.0 copy-start.10
  59.5 1.3 %copy-done.10 = bf16[128,5120]{1,0:T(8,128)(2,1)S(1)} copy-done((bf16[128,5120]{1,0:T(8,128)(2,1)S(1)}, bf16[128,5120]{1,0:T(8,128)(2,1)}, u32[]{:S(2)}) %copy-start.10) | copy-done | bytes 1310744
  60.8 0.0 copy-start.12
  60.8 0.9 %copy-done.12 = bf16[32,16,128]{2,1,0:T(8,128)(2,1)S(1)} copy-done((bf16[32,16,128]{2,1,0:T(8,128)(2,1)S(1)}, bf16[32,16,128]{2,1,0:T(8,128)(2,1)}, u32[]{:S(2)}) %copy-start.12) | copy-done | bytes 131096
  61.7 0.0 copy-start.1
  61.7 1.5 %fresh.1 = (bf16[128,128]{1,0:T(8,128)(2,1)}, bf16[128,128]{1,0:T(8,128)(2,1)}, f32[512,128]{1,0:T(8,128)S(1)}, f32[512,128]{1,0:T(8,128)S(1)}, f32[512,128]{1,0:T(8,128)S(1)}) custom-call(bf16[128,5120]{1,0:T(8,128)(2,1)S(1)} %copy-done.10, bf16[5120,128]{1,0:T(8,128)(2,1)S(1)} %copy-done.5, bf16[5120,128]{1,0:T(8,128)(2,1)S(1)} %copy-done.6, ...), custom_call_target="tpu_custom_call" | custom-call | flops 10737418240 | bytes 1048576 | tf_op jit(solution)/shard_map/fresh/pallas_call | solution.py:438
  63.2 6.5 %all-to-all-done.2.got_ref = bf16[16,72,128]{2,1,0:T(8,128)(2,1)S(1)} async-done(((bf16[16,72,128]{2,1,0:T(8,128)(2,1)}), bf16[16,72,128]{2,1,0:T(8,128)(2,1)S(1)}, u32[]{:S(2)}, u32[]{:S(2)}) %all-to-all-start.2) | async-done | bytes 294944 | tf_op jit(solution)/shard_map/all_to_all | solution.py:464
  69.7 0.0 copy-done.1
  69.7 2.0 %combine.1 = bf16[32,4,512]{2,1,0:T(4,128)(2,1)} custom-call(bf16[16,72,128]{2,1,0:T(8,128)(2,1)S(1)} %all-to-all-done.2.got_ref, f32[512,128]{1,0:T(8,128)S(1)} %get-tuple-element.22.max_ref, f32[512,128]{1,0:T(8,128)S(1)} %get-tuple-element.23.total_ref, f32[512,128]{1,0:T(8,128)S(1)} %get-tuple-element.24.out_ref, s32[2048]{0:T(1024)S(1)} %reshape.30.row_ref.row_hbm, ...), custom_call_target="tpu_custom_call" | custom-call | tf_op jit(solution)/shard_map/combine/pallas_call | solution.py:467
Async XLA Ops:
  0.6 9.7 %copy-start.13 = (s32[32,32,2]{1,2,0:T(2,128)S(1)}, s32[32,32,2]{1,2,0:T(2,128)}, u32[]{:S(2)}) copy-start(s32[32,32,2]{1,2,0:T(2,128)} %param.24) | copy-start | bytes 24580
  2.8 9.9 %copy-start.14 = (s32[32,32,2]{1,2,0:T(2,128)S(1)}, s32[32,32,2]{1,2,0:T(2,128)}, u32[]{:S(2)}) copy-start(s32[32,32,2]{1,2,0:T(2,128)} %param.25) | copy-start | bytes 24580
  2.8 12.3 %copy-start.3 = (bf16[1,32,2,128,128]{4,3,2,1,0:T(8,128)(2,1)S(1)}, bf16[1,32,2,128,128]{4,3,2,1,0:T(8,128)(2,1)}, u32[]{:S(2)}) copy-start(bf16[1,32,2,128,128]{4,3,2,1,0:T(8,128)(2,1)} %param.20) | copy-start | bytes 6291460
  2.8 12.3 %copy-start.7 = (s32[1024]{0:T(1024)S(1)}, s32[1024]{0:T(1024)}, u32[]{:S(2)}) copy-start(s32[1024]{0:T(1024)} %len_ref.1) | copy-start | bytes 12292
  2.8 24.3 %all-to-all-start = ((bf16[8,656,128]{2,1,0:T(8,128)(2,1)}), bf16[8,656,128]{2,1,0:T(8,128)(2,1)S(1)}, u32[]{:S(2)}, u32[]{:S(2)}) async-start(bf16[8,656,128]{2,1,0:T(8,128)(2,1)} %spread.1), calls=%async_computation | async-start | bytes 2686976 | tf_op jit(solution)/shard_map/all_to_all | solution.py:395
  15.1 1.6 %copy-start.4 = (bf16[1,32,2,128,128]{4,3,2,1,0:T(8,128)(2,1)S(1)}, bf16[1,32,2,128,128]{4,3,2,1,0:T(8,128)(2,1)}, u32[]{:S(2)}) copy-start(bf16[1,32,2,128,128]{4,3,2,1,0:T(8,128)(2,1)} %param.21) | copy-start | bytes 6291460
  16.7 10.4 %copy-start.8 = (bf16[128]{0:T(256)(128)(2,1)S(1)}, bf16[128]{0:T(256)(128)(2,1)}, u32[]{:S(2)}) copy-start(bf16[128]{0:T(256)(128)(2,1)} %param.18) | copy-start | bytes 772
  19.6 32.9 %collective-permute-start = (bf16[2,16,2,128,128]{4,3,2,1,0:T(8,128)(2,1)}, bf16[2,16,2,128,128]{4,3,2,1,0:T(8,128)(2,1)S(1)}, u32[]{:S(2)}, u32[]{:S(2)}) collective-permute-start(bf16[2,16,2,128,128]{4,3,2,1,0:T(8,128)(2,1)} %get-tuple-element.18), channel_id=1, source_target_pairs={{0,8},{8,0},{16,24},{24,16},{32,40},{40,32},{48,56},{56,48},{64,72... | collective-permute-start | bytes 6291464 | tf_op jit(solution)/shard_map/ppermute | solution.py:417
  27.1 2.5 %copy-start.2 = (bf16[5120,512]{1,0:T(8,128)(2,1)S(1)}, bf16[5120,512]{1,0:T(8,128)(2,1)}, u32[]{:S(2)}) copy-start(bf16[5120,512]{1,0:T(8,128)(2,1)} %wq_ref.1) | copy-start | bytes 15728644
  29.6 22.9 %copy-start = (bf16[2,16,2,128,128]{4,3,2,1,0:T(8,128)(2,1)S(1)}, bf16[2,16,2,128,128]{4,3,2,1,0:T(8,128)(2,1)}, u32[]{:S(2)}) copy-start(bf16[2,16,2,128,128]{4,3,2,1,0:T(8,128)(2,1)} %get-tuple-element.17.keep_ref) | copy-start | bytes 6291460
  31.3 21.2 %copy-start.11 = (bf16[32,16,128]{2,1,0:T(8,128)(2,1)}, bf16[32,16,128]{2,1,0:T(8,128)(2,1)S(1)}, u32[]{:S(2)}) copy-start(bf16[32,16,128]{2,1,0:T(8,128)(2,1)S(1)} %get-tuple-element.21.pack_ref) | copy-start | bytes 393220
  52.5 5.6 %copy-start.5 = (bf16[5120,128]{1,0:T(8,128)(2,1)S(1)}, bf16[5120,128]{1,0:T(8,128)(2,1)}, u32[]{:S(2)}) copy-start(bf16[5120,128]{1,0:T(8,128)(2,1)} %wk_ref.1) | copy-start | bytes 3932164
  52.5 5.6 %copy-start.9 = (bf16[128]{0:T(256)(128)(2,1)S(1)}, bf16[128]{0:T(256)(128)(2,1)}, u32[]{:S(2)}) copy-start(bf16[128]{0:T(256)(128)(2,1)} %param.19) | copy-start | bytes 772
  54.6 15.1 %all-to-all-start.2 = ((bf16[16,72,128]{2,1,0:T(8,128)(2,1)}), bf16[16,72,128]{2,1,0:T(8,128)(2,1)S(1)}, u32[]{:S(2)}, u32[]{:S(2)}) async-start(bf16[16,72,128]{2,1,0:T(8,128)(2,1)} %pages.1), calls=%async_computation.2 | async-start | bytes 589824 | tf_op jit(solution)/shard_map/all_to_all | solution.py:464
  58.2 1.3 %copy-start.6 = (bf16[5120,128]{1,0:T(8,128)(2,1)S(1)}, bf16[5120,128]{1,0:T(8,128)(2,1)}, u32[]{:S(2)}) copy-start(bf16[5120,128]{1,0:T(8,128)(2,1)} %wv_ref.1) | copy-start | bytes 3932164
  59.5 1.3 %copy-start.10 = (bf16[128,5120]{1,0:T(8,128)(2,1)S(1)}, bf16[128,5120]{1,0:T(8,128)(2,1)}, u32[]{:S(2)}) copy-start(bf16[128,5120]{1,0:T(8,128)(2,1)} %get-tuple-element.20.norm_ref) | copy-start | bytes 3932164
  60.8 0.9 %copy-start.12 = (bf16[32,16,128]{2,1,0:T(8,128)(2,1)S(1)}, bf16[32,16,128]{2,1,0:T(8,128)(2,1)}, u32[]{:S(2)}) copy-start(bf16[32,16,128]{2,1,0:T(8,128)(2,1)} %copy-done.11) | copy-start | bytes 393220
  61.7 8.0 %copy-start.1 = (s32[32]{0:T(128)S(1)}, s32[32]{0:T(128)}, u32[]{:S(2)}) copy-start(s32[32]{0:T(128)} %remaining_hbm.1) | copy-start | bytes 388

commit v4 on v3

--- a/solution.py
+++ b/solution.py
@@ -20,6 +20,8 @@
 CORES = 2
 CHIPS = GROUPS // CORES
 SLOTS = 2
+FIRST_LEFT = 96
+INDEX = 1024
 SHARED = CORES * SLOTS
 TOKENS = ROWS * STEPS
 SIDE = 8
@@ -27,10 +29,6 @@
 
 VMEM = pltpu.VMEM
 SMEM = pltpu.SMEM
-
-
-def slot_row(row_ref, holder, owner, c):
-    return row_ref[(holder * GROUPS + owner) * SLOTS + c]
 
 
 def spread_kernel(hidden_hbm, gain_hbm, out_ref, hidden_ref, gain_ref, block_ref, sem):
@@ -64,11 +62,17 @@
 
 
 def table_kernel(
-    key_hbm, value_hbm, len_ref, row_ref, seq_ref, turn_out, cap_out, keep_hbm, give_hbm, sem
+    key_hbm, value_hbm, wq_hbm, len_ref, left_ref, row_ref, seq_ref,
+    turn_out, cap_out, index_out, keep_hbm, give_hbm, *rest,
 ):
+    parts, (index_ref, sem) = rest[:-2], rest[-2:]
+    depth = parts[0].shape[0]
     me = lax.axis_index("dp")
     core = lax.rem(me, CORES)
-    copies = []
+    copies = [
+        pltpu.make_async_copy(wq_hbm.at[n * depth : (n + 1) * depth], part, sem.at[4 + n])
+        for n, part in enumerate(parts)
+    ]
     for n, pages in enumerate((key_hbm, value_hbm)):
         copies.append(pltpu.make_async_copy(pages.at[:, core], keep_hbm.at[n], sem.at[2 * n]))
         copies.append(
@@ -98,6 +102,20 @@
                 lane == i, jnp.where(row < ROWS, length - seq_ref[place] * WIDTH, 0), cap
             )
         cap_out[j : j + 1, :] = cap
+    none = GROUPS * SLOTS
+    for i in range(none + 1):
+        index_ref[i] = none
+    for chip in range(CHIPS):
+        for c in range(SHARED):
+            holder = chip * CORES + (core if c < SLOTS else 1 - core)
+            place = (holder * GROUPS + me) * SLOTS + c % SLOTS
+            row = row_ref[place]
+            slot = chip * SHARED + c
+            index_ref[jnp.where(row < ROWS, row * SLOTS + seq_ref[place], none)] = slot
+    for r in range(ROWS):
+        index_ref[FIRST_LEFT + r] = left_ref[r]
+    copies.append(pltpu.make_async_copy(index_ref, index_out, sem.at[4 + len(parts)]))
+    copies[-1].start()
     for copy in copies:
         copy.wait()
 
@@ -114,14 +132,9 @@
     return scaled * cos + pltpu.roll(scaled, WIDTH // 2, 1) * sin
 
 
-def project_kernel(
-    x_ref, wq_ref, qg_ref, turn_ref, row_hbm,
-    send_ref, pack_ref, norm_hbm, norm_ref, row_ref, sem,
-):
-    rows_copy = pltpu.make_async_copy(row_hbm, row_ref, sem.at[0])
-    rows_copy.start()
+def norm_kernel(x_ref, norm_ref):
     count = x_ref.shape[0]
-    tiles = wq_ref.shape[0] // count // WIDTH
+    tiles = norm_ref.shape[1] // count // WIDTH
 
     def block(n):
         t, f = n // tiles, n % tiles
@@ -133,26 +146,29 @@
         total = total + x * x
     total = jnp.sum(total, axis=1, keepdims=True)
     rstd = lax.rsqrt(total * (1.0 / (count * tiles * WIDTH)) + EPSILON)
-    queries = jnp.zeros((TOKENS, HEADS * WIDTH), jnp.float32)
-    chunk = 2 * tiles
-    copies = []
-    for s in range(0, count * tiles, chunk):
-        parts = []
-        for n in range(s, s + chunk):
-            t, f = n // tiles, n % tiles
-            last = tiles * TOKENS
-            gain = x_ref[t, last : last + 16, :].astype(jnp.float32)[f : f + 1]
-            parts.append((block(n) * rstd * gain).astype(jnp.bfloat16))
-        part = jnp.concatenate(parts, axis=1)
-        span = slice(s * WIDTH, (s + chunk) * WIDTH)
-        norm_ref[:, span] = part
-        copies.append(
-            pltpu.make_async_copy(
-                norm_ref.at[:, span], norm_hbm.at[:, span], sem.at[1 + s // chunk]
-            )
+    last = tiles * TOKENS
+    for n in range(count * tiles):
+        t, f = n // tiles, n % tiles
+        gain = x_ref[t, last : last + 16, :].astype(jnp.float32)[f : f + 1]
+        norm_ref[:, n * WIDTH : (n + 1) * WIDTH] = (block(n) * rstd * gain).astype(jnp.bfloat16)
+
+
+def project_kernel(
+    norm_ref, qg_ref, turn_ref, row_hbm, *rest,
+):
+    parts, (send_ref, pack_ref, norm_hbm, row_ref, sem) = rest[:-5], rest[-5:]
+    copies = [pltpu.make_async_copy(norm_ref, norm_hbm, sem.at[1])]
+    copies[0].start()
+    rows_copy = pltpu.make_async_copy(row_hbm, row_ref, sem.at[0])
+    rows_copy.start()
+    depth = parts[0].shape[0]
+    queries = sum(
+        jnp.dot(
+            norm_ref[:, n * depth : (n + 1) * depth], part[...],
+            preferred_element_type=jnp.float32,
         )
-        copies[-1].start()
-        queries += jnp.dot(part, wq_ref[span, :], preferred_element_type=jnp.float32)
+        for n, part in enumerate(parts)
+    )
     cos, sin = unpacked(turn_ref[...])
     q_gain = qg_ref[...].astype(jnp.float32)
     low = lax.broadcasted_iota(jnp.int32, (8, WIDTH), 0) < STEPS
@@ -168,15 +184,14 @@
         pack_ref[2 * i] = jnp.concatenate(even, axis=0).astype(jnp.bfloat16)
         pack_ref[2 * i + 1] = jnp.concatenate(odd, axis=0).astype(jnp.bfloat16)
     me = lax.axis_index("dp")
+    core = lax.rem(me, CORES)
     rows_copy.wait()
-    core = lax.rem(me, CORES)
     for chip in range(CHIPS):
-        for k in range(CORES):
-            holder = chip * CORES + (core if k == 0 else 1 - core)
-            for c in range(SLOTS):
-                row = jnp.minimum(slot_row(row_ref, holder, me, c), ROWS - 1)
-                first = (k * SLOTS + c) * QUERIES
-                send_ref[chip, first : first + QUERIES, :] = pack_ref[row]
+        for c in range(SHARED):
+            holder = chip * CORES + (core if c < SLOTS else 1 - core)
+            place = (holder * GROUPS + me) * SLOTS + c % SLOTS
+            row = jnp.minimum(row_ref[place], ROWS - 1)
+            send_ref[chip, c * QUERIES : (c + 1) * QUERIES, :] = pack_ref[row]
     for copy in copies:
         copy.wait()
 
@@ -222,7 +237,7 @@
 
 
 def page_kernel(
-    q_ref, keep_ref, got_ref, cap_ref, send_hbm, send_ref, score_ref, weight_ref, sem
+    q_ref, keep_ref, got_ref, cap_ref, send_ref, score_ref, weight_ref
 ):
     token = lax.broadcasted_iota(jnp.int32, (WIDTH, WIDTH), 0)
     member = lax.broadcasted_iota(jnp.int32, (WIDTH, WIDTH), 1) // QUERIES
@@ -255,35 +270,26 @@
             tile = jnp.where(side_row == n, piece, tile)
         for k in range(2):
             send_ref[2 * j + k, pairs : pairs + SIDE, :] = tile.astype(jnp.bfloat16)
-    for slot in range(GROUPS * SLOTS):
+    for slot in range(0, GROUPS * SLOTS, 2):
         out = jnp.dot(
-            weight_ref[slot * QUERIES : (slot + 1) * QUERIES, :], page(1, slot),
+            weight_ref[slot * QUERIES : (slot + 2) * QUERIES, :],
+            jnp.concatenate([page(1, slot), page(1, slot + 1)], axis=1),
             preferred_element_type=jnp.float32,
         )
-        c = slot % SHARED
-        send_ref[slot // SHARED, c * QUERIES : (c + 1) * QUERIES, :] = out.astype(jnp.bfloat16)
-    send = pltpu.make_async_copy(send_ref, send_hbm, sem.at[0])
-    send.start()
-    send.wait()
+        first = slot % SHARED * QUERIES
+        out = jnp.concatenate([out[:QUERIES, :WIDTH], out[QUERIES:, WIDTH:]], axis=0)
+        send_ref[slot // SHARED, first : first + 2 * QUERIES, :] = out.astype(jnp.bfloat16)
 
 
 def combine_kernel(
-    got_ref, max_ref, total_ref, out_ref, row_hbm, seq_hbm, remaining_hbm,
-    attention_ref, top_wide, total_wide, index_ref, row_ref, seq_ref, remaining_ref, sem,
+    got_ref, max_ref, total_ref, out_ref, index_hbm,
+    attention_hbm, attention_ref, top_wide, total_wide, index_ref, sem,
 ):
-    copies = [
-        pltpu.make_async_copy(row_hbm, row_ref, sem.at[0]),
-        pltpu.make_async_copy(seq_hbm, seq_ref, sem.at[1]),
-        pltpu.make_async_copy(remaining_hbm, remaining_ref, sem.at[2]),
-    ]
-    for copy in copies:
-        copy.start()
+    index_copy = pltpu.make_async_copy(index_hbm, index_ref, sem.at[0])
+    index_copy.start()
     me = lax.axis_index("dp")
-    core = lax.rem(me, CORES)
     pairs = SHARED * QUERIES
     none = GROUPS * SLOTS
-    for i in range(ROWS * SLOTS):
-        index_ref[i] = none
     sub = lax.broadcasted_iota(jnp.int32, (8, WIDTH), 0)
     tops, totals = [], []
     for b in range(CHIPS // 8):
@@ -309,16 +315,8 @@
             )
     top_wide[none] = jnp.full((QUERIES, WIDTH), MASKED, jnp.float32)
     total_wide[none] = jnp.zeros((QUERIES, WIDTH), jnp.float32)
-    for copy in copies:
-        copy.wait()
-    for chip in range(CHIPS):
-        for c in range(SHARED):
-            holder = chip * CORES + (core if c < SLOTS else 1 - core)
-            place = (holder * GROUPS + me) * SLOTS + c % SLOTS
-            row = row_ref[place]
-            index_ref[jnp.where(row < ROWS, row * SLOTS + seq_ref[place], none)] = (
-                chip * SHARED + c
-            )
+    index_copy.wait()
+    copies = []
     step = lax.broadcasted_iota(jnp.int32, (QUERIES, WIDTH), 0) & (STEPS - 1)
     for r in range(ROWS):
         span = slice(r * QUERIES, (r + 1) * QUERIES)
@@ -334,15 +332,28 @@
         factors = [jnp.exp(t - top) for t in tops]
         above = sum(f * o for f, o in zip(factors, outs))
         below = sum(f * t for f, t in zip(factors, totals))
-        result = jnp.where(step < remaining_ref[r], above / below, 0.0).astype(jnp.bfloat16)
+        result = jnp.where(step < index_ref[FIRST_LEFT + r], above / below, 0.0).astype(jnp.bfloat16)
         for h in range(HEADS):
             attention_ref[r, :, h * WIDTH : (h + 1) * WIDTH] = result[
                 h * STEPS : (h + 1) * STEPS, :
             ]
+        if r % 8 == 7:
+            done = slice(r - 7, r + 1)
+            copies.append(
+                pltpu.make_async_copy(
+                    attention_ref.at[done], attention_hbm.at[done], sem.at[1 + r // 8]
+                )
+            )
+            copies[-1].start()
+    for copy in copies:
+        copy.wait()
 
 
 SPREAD_MIB = 60
 TABLE_MIB = 4
+PARTS = 4
+NORM_MIB = 4
+NORM_COST = 20
 PROJECT_MIB = 8
 FRESH_MIB = 8
 PAGES_MIB = 6
@@ -398,23 +409,34 @@
     seqs_flat = page_seq.reshape(-1)
     page_shape = (CHIPS, CORES, SLOTS, WIDTH, WIDTH)
     moved = (2, CHIPS, SLOTS, WIDTH, WIDTH)
-    turns, caps, keep, give = pl.pallas_call(
+    turns, caps, index, keep, give, *weights = pl.pallas_call(
         table_kernel,
         out_shape=(
             shape((TOKENS, WIDTH), f32), shape((slots // 8, WIDTH), jnp.int32),
+            VMEM((INDEX,), jnp.int32),
             pltpu.HBM(moved, bf16), pltpu.HBM(moved, bf16),
-        ),
-        in_specs=[hbm] * 2 + [smem] * 3,
-        out_specs=(vmem, vmem, hbm, hbm),
-        scratch_shapes=[dma((4,))],
+        )
+        + (pltpu.HBM((width // PARTS, HEADS * WIDTH), bf16),) * PARTS,
+        in_specs=[hbm] * 3 + [smem] * 4,
+        out_specs=(vmem, vmem, vmem) + (hbm,) * (2 + PARTS),
+        scratch_shapes=[SMEM((INDEX,), jnp.int32), dma((5 + PARTS,))],
         compiler_params=limit(TABLE_MIB),
         cost_estimate=cost(TABLE_COST),
         name="tables",
     )(
         cache_keys.reshape(page_shape), cached_value_pages.reshape(page_shape),
-        cache_len, rows_flat, seqs_flat,
+        w_query, cache_len, remaining, rows_flat, seqs_flat,
     )
     got = lax.ppermute(give, "dp", flip)
+    states = pl.pallas_call(
+        norm_kernel,
+        out_shape=VMEM((TOKENS, width), bf16),
+        in_specs=[vmem],
+        out_specs=vmem,
+        compiler_params=limit(NORM_MIB),
+        cost_estimate=cost(NORM_COST),
+        name="normalise",
+    )(gathered)
     send_q, pack, normed = pl.pallas_call(
         project_kernel,
         out_shape=(
@@ -422,16 +444,13 @@
             shape((ROWS, QUERIES, WIDTH), bf16),
             pltpu.HBM((TOKENS, width), bf16),
         ),
-        in_specs=[vmem] * 4 + [hbm],
+        in_specs=[vmem] * 3 + [hbm] + [vmem] * PARTS,
         out_specs=(vmem, vmem, hbm),
-        scratch_shapes=[
-            VMEM((TOKENS, width), bf16),
-            SMEM((rows_flat.size,), jnp.int32), dma((1 + tensor // 2,)),
-        ],
+        scratch_shapes=[SMEM((rows_flat.size,), jnp.int32), dma((2,))],
         compiler_params=limit(PROJECT_MIB),
         cost_estimate=cost(PROJECT_COST),
         name="project",
-    )(gathered, w_query, query_gain[None, :], turns, rows_flat)
+    )(states, query_gain[None, :], turns, rows_flat, *weights)
     got_q = lax.all_to_all(
         send_q, "dp", split_axis=0, concat_axis=0, tiled=True, axis_index_groups=same_core
     )
@@ -447,14 +466,12 @@
     )(normed, key_projection, value_projection, key_gain[None, :], turns, pack)
     send_out = pl.pallas_call(
         page_kernel,
-        out_shape=pltpu.HBM((CHIPS, pairs + SIDE, WIDTH), bf16),
+        out_shape=VMEM((CHIPS, pairs + SIDE, WIDTH), bf16),
         in_specs=[vmem] * 4,
-        out_specs=hbm,
+        out_specs=vmem,
         scratch_shapes=[
-            VMEM((CHIPS, pairs + SIDE, WIDTH), bf16),
             VMEM((slots * QUERIES, WIDTH), f32),
             VMEM((slots * QUERIES, WIDTH), bf16),
-            dma((1,)),
         ],
         compiler_params=limit(PAGES_MIB),
         name="pages",
@@ -466,21 +483,19 @@
     )
     attention = pl.pallas_call(
         combine_kernel,
-        out_shape=shape((ROWS, STEPS, HEADS * WIDTH), bf16),
-        in_specs=[vmem] * 4 + [hbm] * 3,
-        out_specs=vmem,
+        out_shape=pltpu.HBM((ROWS, STEPS, HEADS * WIDTH), bf16),
+        in_specs=[vmem] * 4 + [hbm],
+        out_specs=hbm,
         scratch_shapes=[
+            VMEM((ROWS, STEPS, HEADS * WIDTH), bf16),
             VMEM((slots + 1, QUERIES, WIDTH), f32),
             VMEM((slots + 1, QUERIES, WIDTH), f32),
-            SMEM((slots + 8,), jnp.int32),
-            SMEM((rows_flat.size,), jnp.int32),
-            SMEM((seqs_flat.size,), jnp.int32),
-            SMEM((ROWS,), jnp.int32),
-            dma((3,)),
+            SMEM((INDEX,), jnp.int32),
+            dma((1 + ROWS // 8,)),
         ],
         compiler_params=limit(COMBINE_MIB),
         name="combine",
-    )(got_out, new_max, new_total, new_out, rows_flat, seqs_flat, remaining)
+    )(got_out, new_max, new_total, new_out, index)
     return (
         attention,
         new_key.reshape(ROWS, STEPS, WIDTH),

time: 72.2 us -> 70.8 us (0.981)
  waiting for transfers between devices: 13.9 us -> 11.9 us
  Pallas kernels: 12.2 us -> 13.3 us
    all_to_all x1, waiting for transfers between devices: 7.44 us -> 5.37 us  [shards(): lax.all_to_all(spread, 'tp', split_axis=0, concat_axis=0, tiled=True)]
    unnamed x32 -> x40, local copies, waits for them, and re-layouts: 9.81 us -> 11.7 us
    pallas_call x1, Pallas kernels: 2.86 us -> 4.52 us  [shards(): pl.pallas_call(table_kernel, out_shape=(shape((TOKENS, WIDTH), f32), shap...]
    reshape x1, local copies, waits for them, and re-layouts: 1.31 us -> 0.27 us  [shards(): rows_flat = page_row.reshape(-1)]
    reshape x1, local copies, waits for them, and re-layouts: 1.31 us -> 0.27 us  [shards(): seqs_flat = page_seq.reshape(-1)]
    pallas_call x2 -> x3, Pallas kernels: 4.04 us -> 3.93 us  [the longest x1 1.77 us: shards(): pl.pallas_call(page_kernel, out_shape=VMEM((CHIPS, pairs + SIDE, WIDTH),...]
  transfers between devices with their start and end apart: 3 -> 3, of which waited for: 2 -> 2; matrix products, arithmetic and copies ran while one was open for 7% -> 2% of each run, Pallas kernels for 8% -> 11%
where the time goes in v4:
time: 70.8 us; the launch traced here: 70.3 us
  blocking collectives  21.2 us (30%)
  Pallas kernels  13.3 us (19%)
  local copies, waits for them, and re-layouts  12.2 us (17%)
  waiting for transfers between devices  11.9 us (17%)
  starting transfers between devices  11 us (16%)
  between operations  0.81 us (1%)
    all_to_all x1, blocking collectives, shards(): lax.all_to_all(send_q, 'dp', split_axis=0, concat_axis=0, tiled=True, axi...  21.2 us
    unnamed x40, local copies, waits for them, and re-layouts  11.7 us
    all_to_all x1, starting transfers between devices, shards(): lax.all_to_all(spread, 'tp', split_axis=0, concat_axis=0, tiled=True)  7.33 us
    all_to_all x1, waiting for transfers between devices, shards(): lax.all_to_all(send_out, 'dp', split_axis=0, concat_axis=0, tiled=True, a...  6.49 us
    all_to_all x1, waiting for transfers between devices, shards(): lax.all_to_all(spread, 'tp', split_axis=0, concat_axis=0, tiled=True)  5.37 us
    pallas_call x1, Pallas kernels, shards(): pl.pallas_call(table_kernel, out_shape=(shape((TOKENS, WIDTH), f32), shap...  4.52 us
    all_to_all x1, starting transfers between devices, shards(): lax.all_to_all(send_out, 'dp', split_axis=0, concat_axis=0, tiled=True, a...  3.54 us
    pallas_call x1, Pallas kernels, shards(): pl.pallas_call(spread_kernel, out_shape=pltpu.HBM((tensor, rows, WIDTH),...  2.14 us
  transfers between devices with their start and end apart: 3, of which 2 were waited for; matrix products, arithmetic and copies ran while one was open for 2% of the time, Pallas kernels for 11%

profile of v4, /device:TPU:12, one launch (start us, length us, event | category | flops | bytes accessed | tf_op | source)
XLA Modules:
  0.0 70.3 jit_solution(6840640243812635551)
XLA Ops:
  0.6 2.1 %spread.1 = bf16[8,656,128]{2,1,0:T(8,128)(2,1)} custom-call(bf16[32,4,640]{2,1,0:T(4,128)(2,1)} %hidden_hbm.1, bf16[5,128]{1,0:T(8,128)(2,1)} %bitcast.11), custom_call_target="tpu_custom_call" | custom-call | tf_op jit(solution)/shard_map/spread/pallas_call | solution.py:394
  2.8 0.0 copy-start.17
  2.8 0.0 copy-start.18
  2.8 7.3 %all-to-all-start = ((bf16[8,656,128]{2,1,0:T(8,128)(2,1)}), bf16[8,656,128]{2,1,0:T(8,128)(2,1)S(1)}, u32[]{:S(2)}, u32[]{:S(2)}) async-start(bf16[8,656,128]{2,1,0:T(8,128)(2,1)} %spread.1), calls=%async_computation | async-start | bytes 2686976 | tf_op jit(solution)/shard_map/all_to_all | solution.py:406
  10.1 0.0 copy-done.17
  10.1 0.0 copy-start.6
  10.1 0.0 copy-start.7
  10.1 0.3 copy.16
  10.4 0.3 reshape.30.row_ref.row_hbm
  10.7 0.0 copy-done.18
  10.7 0.3 copy.17
  11.0 0.3 reshape.31.seq_ref
  11.2 0.0 copy-done.6
  11.2 0.0 copy-done.7
  11.3 0.0 copy-start.1
  11.3 2.5 %copy-done.1 = bf16[5120,512]{1,0:T(8,128)(2,1)S(1)} copy-done((bf16[5120,512]{1,0:T(8,128)(2,1)S(1)}, bf16[5120,512]{1,0:T(8,128)(2,1)}, u32[]{:S(2)}) %copy-start.1) | copy-done | bytes 5242904
  13.7 0.0 copy-start.2
  13.7 1.6 %copy-done.2 = bf16[1,32,2,128,128]{4,3,2,1,0:T(8,128)(2,1)S(1)} copy-done((bf16[1,32,2,128,128]{4,3,2,1,0:T(8,128)(2,1)S(1)}, bf16[1,32,2,128,128]{4,3,2,1,0:T(8,128)(2,1)}, u32[]{:S(2)}) %copy-start.2) | copy-done | bytes 2097176
  15.3 0.0 copy-start.3
  15.3 1.6 %copy-done.3 = bf16[1,32,2,128,128]{4,3,2,1,0:T(8,128)(2,1)S(1)} copy-done((bf16[1,32,2,128,128]{4,3,2,1,0:T(8,128)(2,1)S(1)}, bf16[1,32,2,128,128]{4,3,2,1,0:T(8,128)(2,1)}, u32[]{:S(2)}) %copy-start.3) | copy-done | bytes 2097176
  16.9 4.5 %tables.1 = (f32[128,128]{1,0:T(8,128)S(1)}, s32[8,128]{1,0:T(8,128)S(1)}, s32[1024]{0:T(1024)S(1)}, bf16[2,16,2,128,128]{4,3,2,1,0:T(8,128)(2,1)}, bf16[2,16,2,...) custom-call(bf16[16,2,2,128,128]{4,3,2,1,0:T(8,128)(2,1)S(1)} %bitca, ...), custom_call_target="tpu_custom_call" | custom-call | flops 21474836480 | bytes 1048576 | tf_op jit(solution)/shard_map/tables/pallas_call | solution.py:412
  21.5 0.0 copy-start.8
  21.5 0.1 collective-permute-start
  21.6 5.4 %all-to-all-done.x_ref = bf16[8,656,128]{2,1,0:T(8,128)(2,1)S(1)} async-done(((bf16[8,656,128]{2,1,0:T(8,128)(2,1)}), bf16[8,656,128]{2,1,0:T(8,128)(2,1)S(1)}, u32[]{:S(2)}, u32[]{:S(2)}) %all-to-all-start) | async-done | bytes 1343520 | tf_op jit(solution)/shard_map/all_to_all | solution.py:406
  26.9 0.0 copy-start.11
  26.9 0.0 copy-start.12
  26.9 0.0 copy-start.13
  26.9 0.0 copy-start.14
  26.9 0.6 normalise.1.norm_ref
  27.5 0.0 copy-done.8
  27.6 0.7 copy-done.11
  28.2 0.4 copy-done.12
  28.6 0.4 copy-done.13
  29.0 0.4 copy-done.14
  29.4 0.0 copy-start
  29.4 1.2 %project.1 = (bf16[16,64,128]{2,1,0:T(8,128)(2,1)S(1)}, bf16[32,16,128]{2,1,0:T(8,128)(2,1)S(1)}, bf16[128,5120]{1,0:T(8,128)(2,1)}) custom-call(bf16[128,5120]{1,0:T(8,128)(2,1)S(1)} %normalise.1.norm_ref, bf16[1,128]{1,0:T(2,128)(2,1)S(1)} %bitcast.9, f32[128,128]{1,0:T(8,128)S(1)} %get-tuple-element.20.turn_ref, s32[2048]{0:T(1024)S(1)} %reshape.30.row_ref.row_hbm, ...), custom_call_target="tpu_custom_call" | custom-call | flops 10737418240 | bytes 1048576 | tf_op jit(solution)/shard_map/project/pallas_call | solution.py:440
  30.7 0.0 copy-start.15
  30.7 21.2 %all_to_all.15.q_ref = bf16[16,64,128]{2,1,0:T(8,128)(2,1)S(1)} all-to-all(bf16[16,64,128]{2,1,0:T(8,128)(2,1)S(1)} %get-tuple-element.25), channel_id=1, replica_groups={{0,16,32,48,64,80,96,112,128,144,160,176,192,208,224,240},{8,24,40,56,7..., dimensions={0} | all-to-all | bytes 524288 | tf_op jit(solution)/shard_map/all_to_all | solution.py:454
  51.9 0.0 collective-permute-done.got_ref
  51.9 0.0 copy-done.15
  51.9 0.0 copy-done
  51.9 0.0 copy-start.4
  51.9 0.0 copy-start.9
  51.9 1.8 %pages.1 = bf16[16,72,128]{2,1,0:T(8,128)(2,1)} custom-call(bf16[16,64,128]{2,1,0:T(8,128)(2,1)S(1)} %all_to_all.15.q_ref, bf16[2,16,2,128,128]{4,3,2,1,0:T(8,128)(2,1)S(1)} %copy-done, bf16[2,16,2,128,128]{4,3,2,1,0:T(8,128)(2,1)S(1)} %collective-permute-done.got_ref, s32[8,128]{1,0:T(8,128)S(1)} %get-tuple-element.28.cap_ref), custom_call_target="tpu_custom_call" | custom-call | tf_op jit(solution)/shard_map/pages/pallas_call | solution.py:467
  53.7 3.5 %all-to-all-start.2 = ((bf16[16,72,128]{2,1,0:T(8,128)(2,1)}), bf16[16,72,128]{2,1,0:T(8,128)(2,1)S(1)}, u32[]{:S(2)}, u32[]{:S(2)}) async-start(bf16[16,72,128]{2,1,0:T(8,128)(2,1)} %pages.1), calls=%async_computation.2 | async-start | bytes 589824 | tf_op jit(solution)/shard_map/all_to_all | solution.py:481
  57.2 0.0 copy-done.4
  57.2 0.0 copy-done.9
  57.2 0.0 copy-start.5
  57.2 1.3 %copy-done.5 = bf16[5120,128]{1,0:T(8,128)(2,1)S(1)} copy-done((bf16[5120,128]{1,0:T(8,128)(2,1)S(1)}, bf16[5120,128]{1,0:T(8,128)(2,1)}, u32[]{:S(2)}) %copy-start.5) | copy-done | bytes 1310744
  58.5 0.0 copy-start.10
  58.5 1.3 %copy-done.10 = bf16[128,5120]{1,0:T(8,128)(2,1)S(1)} copy-done((bf16[128,5120]{1,0:T(8,128)(2,1)S(1)}, bf16[128,5120]{1,0:T(8,128)(2,1)}, u32[]{:S(2)}) %copy-start.10) | copy-done | bytes 1310744
  59.9 0.0 copy-start.16
  59.9 0.9 %copy-done.16 = bf16[32,16,128]{2,1,0:T(8,128)(2,1)S(1)} copy-done((bf16[32,16,128]{2,1,0:T(8,128)(2,1)S(1)}, bf16[32,16,128]{2,1,0:T(8,128)(2,1)}, u32[]{:S(2)}) %copy-start.16) | copy-done | bytes 131096
  60.8 1.5 %fresh.1 = (bf16[128,128]{1,0:T(8,128)(2,1)}, bf16[128,128]{1,0:T(8,128)(2,1)}, f32[512,128]{1,0:T(8,128)S(1)}, f32[512,128]{1,0:T(8,128)S(1)}, f32[512,128]{1,0:T(8,128)S(1)}) custom-call(bf16[128,5120]{1,0:T(8,128)(2,1)S(1)} %copy-done.10, bf16[5120,128]{1,0:T(8,128)(2,1)S(1)} %copy-done.4, bf16[5120,128]{1,0:T(8,128)(2,1)S(1)} %copy-done.5, ...), custom_call_target="tpu_custom_call" | custom-call | flops 10737418240 | bytes 1048576 | tf_op jit(solution)/shard_map/fresh/pallas_call | solution.py:457
  62.2 6.5 %all-to-all-done.2.got_ref = bf16[16,72,128]{2,1,0:T(8,128)(2,1)S(1)} async-done(((bf16[16,72,128]{2,1,0:T(8,128)(2,1)}), bf16[16,72,128]{2,1,0:T(8,128)(2,1)S(1)}, u32[]{:S(2)}, u32[]{:S(2)}) %all-to-all-start.2) | async-done | bytes 294944 | tf_op jit(solution)/shard_map/all_to_all | solution.py:481
  68.7 1.6 %combine.1 = bf16[32,4,512]{2,1,0:T(4,128)(2,1)} custom-call(bf16[16,72,128]{2,1,0:T(8,128)(2,1)S(1)} %all-to-all-done.2.got_ref, f32[512,128]{1,0:T(8,128)S(1)} %get-tuple-element.31.max_ref, f32[512,128]{1,0:T(8,128)S(1)} %get-tuple-element.32.total_ref, f32[512,128]{1,0:T(8,128)S(1)} %get-tuple-element.33.out_ref, s32[1024]{0:T(1024)S(1)} %get-tuple-element.34.index_hbm), custom_call_target="tpu_custom_call" | custom-call | tf_op jit(solution)/shard_map/combine/pallas_call | solution.py:484
Async XLA Ops:
  2.8 7.4 %copy-start.17 = (s32[32,32,2]{1,2,0:T(2,128)S(1)}, s32[32,32,2]{1,2,0:T(2,128)}, u32[]{:S(2)}) copy-start(s32[32,32,2]{1,2,0:T(2,128)} %param.24) | copy-start | bytes 24580
  2.8 7.9 %copy-start.18 = (s32[32,32,2]{1,2,0:T(2,128)S(1)}, s32[32,32,2]{1,2,0:T(2,128)}, u32[]{:S(2)}) copy-start(s32[32,32,2]{1,2,0:T(2,128)} %param.25) | copy-start | bytes 24580
  2.8 24.1 %all-to-all-start = ((bf16[8,656,128]{2,1,0:T(8,128)(2,1)}), bf16[8,656,128]{2,1,0:T(8,128)(2,1)S(1)}, u32[]{:S(2)}, u32[]{:S(2)}) async-start(bf16[8,656,128]{2,1,0:T(8,128)(2,1)} %spread.1), calls=%async_computation | async-start | bytes 2686976 | tf_op jit(solution)/shard_map/all_to_all | solution.py:406
  10.1 1.1 %copy-start.6 = (s32[1024]{0:T(1024)S(1)}, s32[1024]{0:T(1024)}, u32[]{:S(2)}) copy-start(s32[1024]{0:T(1024)} %len_ref.1) | copy-start | bytes 12292
  10.1 1.1 %copy-start.7 = (s32[32]{0:T(128)S(1)}, s32[32]{0:T(128)}, u32[]{:S(2)}) copy-start(s32[32]{0:T(128)} %left_ref.1) | copy-start | bytes 388
  11.3 2.5 %copy-start.1 = (bf16[5120,512]{1,0:T(8,128)(2,1)S(1)}, bf16[5120,512]{1,0:T(8,128)(2,1)}, u32[]{:S(2)}) copy-start(bf16[5120,512]{1,0:T(8,128)(2,1)} %wq_hbm.1) | copy-start | bytes 15728644
  13.7 1.6 %copy-start.2 = (bf16[1,32,2,128,128]{4,3,2,1,0:T(8,128)(2,1)S(1)}, bf16[1,32,2,128,128]{4,3,2,1,0:T(8,128)(2,1)}, u32[]{:S(2)}) copy-start(bf16[1,32,2,128,128]{4,3,2,1,0:T(8,128)(2,1)} %param.20) | copy-start | bytes 6291460
  15.3 1.6 %copy-start.3 = (bf16[1,32,2,128,128]{4,3,2,1,0:T(8,128)(2,1)S(1)}, bf16[1,32,2,128,128]{4,3,2,1,0:T(8,128)(2,1)}, u32[]{:S(2)}) copy-start(bf16[1,32,2,128,128]{4,3,2,1,0:T(8,128)(2,1)} %param.21) | copy-start | bytes 6291460
  21.5 6.1 %copy-start.8 = (bf16[128]{0:T(256)(128)(2,1)S(1)}, bf16[128]{0:T(256)(128)(2,1)}, u32[]{:S(2)}) copy-start(bf16[128]{0:T(256)(128)(2,1)} %param.18) | copy-start | bytes 772
  21.5 30.4 %collective-permute-start = (bf16[2,16,2,128,128]{4,3,2,1,0:T(8,128)(2,1)}, bf16[2,16,2,128,128]{4,3,2,1,0:T(8,128)(2,1)S(1)}, u32[]{:S(2)}, u32[]{:S(2)}) collective-permute-start(bf16[2,16,2,128,128]{4,3,2,1,0:T(8,128)(2,1)} %get-tuple-element.27), channel_id=1, source_target_pairs={{0,8},{8,0},{16,24},{24,16},{32,40},{40,32},{48,56},{56,48},{64,72... | collective-permute-start | bytes 6291464 | tf_op jit(solution)/shard_map/ppermute | solution.py:430
  26.9 1.3 %copy-start.11 = (bf16[1280,512]{1,0:T(8,128)(2,1)S(1)}, bf16[1280,512]{1,0:T(8,128)(2,1)}, u32[]{:S(2)}) copy-start(bf16[1280,512]{1,0:T(8,128)(2,1)} %get-tuple-element.21.rest_0_) | copy-start | bytes 3932164
  26.9 1.7 %copy-start.12 = (bf16[1280,512]{1,0:T(8,128)(2,1)S(1)}, bf16[1280,512]{1,0:T(8,128)(2,1)}, u32[]{:S(2)}) copy-start(bf16[1280,512]{1,0:T(8,128)(2,1)} %get-tuple-element.22.rest_1_) | copy-start | bytes 3932164
  26.9 2.1 %copy-start.13 = (bf16[1280,512]{1,0:T(8,128)(2,1)S(1)}, bf16[1280,512]{1,0:T(8,128)(2,1)}, u32[]{:S(2)}) copy-start(bf16[1280,512]{1,0:T(8,128)(2,1)} %get-tuple-element.23.rest_2_) | copy-start | bytes 3932164
  26.9 2.5 %copy-start.14 = (bf16[1280,512]{1,0:T(8,128)(2,1)S(1)}, bf16[1280,512]{1,0:T(8,128)(2,1)}, u32[]{:S(2)}) copy-start(bf16[1280,512]{1,0:T(8,128)(2,1)} %get-tuple-element.24.rest_3_) | copy-start | bytes 3932164
  29.4 22.4 %copy-start = (bf16[2,16,2,128,128]{4,3,2,1,0:T(8,128)(2,1)S(1)}, bf16[2,16,2,128,128]{4,3,2,1,0:T(8,128)(2,1)}, u32[]{:S(2)}) copy-start(bf16[2,16,2,128,128]{4,3,2,1,0:T(8,128)(2,1)} %get-tuple-element.26.keep_ref) | copy-start | bytes 6291460
  30.7 21.2 %copy-start.15 = (bf16[32,16,128]{2,1,0:T(8,128)(2,1)}, bf16[32,16,128]{2,1,0:T(8,128)(2,1)S(1)}, u32[]{:S(2)}) copy-start(bf16[32,16,128]{2,1,0:T(8,128)(2,1)S(1)} %get-tuple-element.30.pack_ref) | copy-start | bytes 393220
  51.9 5.3 %copy-start.4 = (bf16[5120,128]{1,0:T(8,128)(2,1)S(1)}, bf16[5120,128]{1,0:T(8,128)(2,1)}, u32[]{:S(2)}) copy-start(bf16[5120,128]{1,0:T(8,128)(2,1)} %wk_ref.1) | copy-start | bytes 3932164
  51.9 5.3 %copy-start.9 = (bf16[128]{0:T(256)(128)(2,1)S(1)}, bf16[128]{0:T(256)(128)(2,1)}, u32[]{:S(2)}) copy-start(bf16[128]{0:T(256)(128)(2,1)} %param.19) | copy-start | bytes 772
  53.7 15.1 %all-to-all-start.2 = ((bf16[16,72,128]{2,1,0:T(8,128)(2,1)}), bf16[16,72,128]{2,1,0:T(8,128)(2,1)S(1)}, u32[]{:S(2)}, u32[]{:S(2)}) async-start(bf16[16,72,128]{2,1,0:T(8,128)(2,1)} %pages.1), calls=%async_computation.2 | async-start | bytes 589824 | tf_op jit(solution)/shard_map/all_to_all | solution.py:481
  57.2 1.3 %copy-start.5 = (bf16[5120,128]{1,0:T(8,128)(2,1)S(1)}, bf16[5120,128]{1,0:T(8,128)(2,1)}, u32[]{:S(2)}) copy-start(bf16[5120,128]{1,0:T(8,128)(2,1)} %wv_ref.1) | copy-start | bytes 3932164
  58.5 1.3 %copy-start.10 = (bf16[128,5120]{1,0:T(8,128)(2,1)S(1)}, bf16[128,5120]{1,0:T(8,128)(2,1)}, u32[]{:S(2)}) copy-start(bf16[128,5120]{1,0:T(8,128)(2,1)} %get-tuple-element.29.norm_ref) | copy-start | bytes 3932164
  59.9 0.9 %copy-start.16 = (bf16[32,16,128]{2,1,0:T(8,128)(2,1)S(1)}, bf16[32,16,128]{2,1,0:T(8,128)(2,1)}, u32[]{:S(2)}) copy-start(bf16[32,16,128]{2,1,0:T(8,128)(2,1)} %copy-done.15) | copy-start | bytes 393220

commit v5 on v4

--- a/solution.py
+++ b/solution.py
@@ -21,7 +21,10 @@
 CHIPS = GROUPS // CORES
 SLOTS = 2
 FIRST_LEFT = 96
+FIRST_ROW = 128
 INDEX = 1024
+SHARDS = 8
+CUT = 320
 SHARED = CORES * SLOTS
 TOKENS = ROWS * STEPS
 SIDE = 8
@@ -31,8 +34,7 @@
 SMEM = pltpu.SMEM
 
 
-def spread_kernel(hidden_hbm, gain_hbm, out_ref, hidden_ref, gain_ref, block_ref, sem):
-    features = hidden_hbm.shape[2]
+def block_kernel(hidden_hbm, gain_hbm, block_ref, hidden_ref, gain_ref, sem):
     copies = [
         pltpu.make_async_copy(hidden_hbm, hidden_ref, sem.at[0]),
         pltpu.make_async_copy(gain_hbm, gain_ref, sem.at[1]),
@@ -41,7 +43,7 @@
         copy.start()
     for copy in copies:
         copy.wait()
-    tiles = features // WIDTH
+    tiles = hidden_hbm.shape[2] // WIDTH
     for i in range(0, ROWS, 4):
         part = [hidden_ref[i + k].astype(jnp.float32) for k in range(4)]
         part = jnp.concatenate(part, axis=0).astype(jnp.bfloat16)
@@ -51,35 +53,34 @@
     gain = gain_ref[...].astype(jnp.float32)
     gain = jnp.concatenate([gain, jnp.zeros((16 - tiles, WIDTH), jnp.float32)], axis=0)
     block_ref[tiles * TOKENS : tiles * TOKENS + 16, :] = gain.astype(jnp.bfloat16)
-    copies = [
-        pltpu.make_async_copy(block_ref, out_ref.at[t], sem.at[2 + t])
-        for t in range(out_ref.shape[0])
+
+
+def table_kernel(
+    key_hbm, value_hbm, len_hbm, left_hbm, row_hbm, seq_hbm,
+    turn_out, cap_out, index_out, keep_hbm, give_hbm,
+    stage_ref, index_ref, len_ref, left_ref, row_ref, seq_ref, sem,
+):
+    scalars = [
+        pltpu.make_async_copy(source, target, sem.at[9 + n])
+        for n, (source, target) in enumerate(
+            ((len_hbm, len_ref), (left_hbm, left_ref), (row_hbm, row_ref), (seq_hbm, seq_ref))
+        )
     ]
-    for copy in copies:
+    for copy in scalars:
         copy.start()
-    for copy in copies:
-        copy.wait()
-
-
-def table_kernel(
-    key_hbm, value_hbm, wq_hbm, len_ref, left_ref, row_ref, seq_ref,
-    turn_out, cap_out, index_out, keep_hbm, give_hbm, *rest,
-):
-    parts, (index_ref, sem) = rest[:-2], rest[-2:]
-    depth = parts[0].shape[0]
     me = lax.axis_index("dp")
     core = lax.rem(me, CORES)
-    copies = [
-        pltpu.make_async_copy(wq_hbm.at[n * depth : (n + 1) * depth], part, sem.at[4 + n])
-        for n, part in enumerate(parts)
-    ]
-    for n, pages in enumerate((key_hbm, value_hbm)):
-        copies.append(pltpu.make_async_copy(pages.at[:, core], keep_hbm.at[n], sem.at[2 * n]))
-        copies.append(
-            pltpu.make_async_copy(pages.at[:, 1 - core], give_hbm.at[n], sem.at[2 * n + 1])
-        )
-    for copy in copies:
+    arrivals, departures = [], []
+    for target, half in ((give_hbm, 1 - core), (keep_hbm, core)):
+        for n, pages in enumerate((key_hbm, value_hbm)):
+            place = len(arrivals)
+            staged = stage_ref.at[place]
+            arrivals.append(pltpu.make_async_copy(pages.at[:, half], staged, sem.at[place]))
+            departures.append(pltpu.make_async_copy(staged, target.at[n], sem.at[4 + place]))
+    for copy in arrivals:
         copy.start()
+    for copy in scalars:
+        copy.wait()
     row = lax.broadcasted_iota(jnp.int32, (TOKENS, WIDTH), 0)
     position = row & (STEPS - 1)
     for r in range(ROWS):
@@ -95,29 +96,33 @@
             chip, k, c = 2 * j + i // SHARED, i // SLOTS % CORES, i % SLOTS
             owner = chip * CORES + core
             holder = me if k == 0 else me + 1 - 2 * core
-            place = (holder * GROUPS + owner) * SLOTS + c
-            row = row_ref[place]
+            row = row_ref[holder, c, owner]
             length = len_ref[owner * ROWS + jnp.minimum(row, ROWS - 1)]
             cap = jnp.where(
-                lane == i, jnp.where(row < ROWS, length - seq_ref[place] * WIDTH, 0), cap
+                lane == i, jnp.where(row < ROWS, length - seq_ref[holder, c, owner] * WIDTH, 0), cap
             )
         cap_out[j : j + 1, :] = cap
+    for arrival, departure in zip(arrivals, departures):
+        arrival.wait()
+        departure.start()
     none = GROUPS * SLOTS
     for i in range(none + 1):
         index_ref[i] = none
     for chip in range(CHIPS):
         for c in range(SHARED):
             holder = chip * CORES + (core if c < SLOTS else 1 - core)
-            place = (holder * GROUPS + me) * SLOTS + c % SLOTS
-            row = row_ref[place]
+            row = row_ref[holder, c % SLOTS, me]
+            seq = seq_ref[holder, c % SLOTS, me]
             slot = chip * SHARED + c
-            index_ref[jnp.where(row < ROWS, row * SLOTS + seq_ref[place], none)] = slot
+            index_ref[jnp.where(row < ROWS, row * SLOTS + seq, none)] = slot
+            index_ref[FIRST_ROW + slot] = jnp.minimum(row, ROWS - 1)
     for r in range(ROWS):
         index_ref[FIRST_LEFT + r] = left_ref[r]
-    copies.append(pltpu.make_async_copy(index_ref, index_out, sem.at[4 + len(parts)]))
-    copies[-1].start()
-    for copy in copies:
-        copy.wait()
+    index_copy = pltpu.make_async_copy(index_ref, index_out, sem.at[8])
+    index_copy.start()
+    for departure in departures:
+        departure.wait()
+    index_copy.wait()
 
 
 def unpacked(turn):
@@ -132,13 +137,25 @@
     return scaled * cos + pltpu.roll(scaled, WIDTH // 2, 1) * sin
 
 
-def norm_kernel(x_ref, norm_ref):
-    count = x_ref.shape[0]
+def norm_kernel(*refs):
+    shards, norm_ref = refs[:-1], refs[-1]
+    count = SHARDS
     tiles = norm_ref.shape[1] // count // WIDTH
+    pieces = {0: (0,), 1: (1,), 2: (2,), 3: (3,), 4: (4, 5), 5: (6, 7), 6: (8,), 7: (9,)}
+
+    def rows(t, first, last):
+        held = pieces[t]
+        if len(held) == 1:
+            return shards[held[0]][first:last, :].astype(jnp.float32)
+        if last <= CUT:
+            return shards[held[0]][first:last, :].astype(jnp.float32)
+        if first >= CUT:
+            return shards[held[1]][first - CUT : last - CUT, :].astype(jnp.float32)
+        return jnp.concatenate([rows(t, first, CUT), rows(t, CUT, last)], axis=0)
 
     def block(n):
         t, f = n // tiles, n % tiles
-        return x_ref[t, f * TOKENS : (f + 1) * TOKENS, :].astype(jnp.float32)
+        return rows(t, f * TOKENS, (f + 1) * TOKENS)
 
     total = jnp.zeros((TOKENS, WIDTH), jnp.float32)
     for n in range(count * tiles):
@@ -147,28 +164,23 @@
     total = jnp.sum(total, axis=1, keepdims=True)
     rstd = lax.rsqrt(total * (1.0 / (count * tiles * WIDTH)) + EPSILON)
     last = tiles * TOKENS
+    me = lax.axis_index("tp")
     for n in range(count * tiles):
         t, f = n // tiles, n % tiles
-        gain = x_ref[t, last : last + 16, :].astype(jnp.float32)[f : f + 1]
-        norm_ref[:, n * WIDTH : (n + 1) * WIDTH] = (block(n) * rstd * gain).astype(jnp.bfloat16)
+        column = pl.multiple_of(((me ^ t) * tiles + f) * WIDTH, WIDTH)
+        gain = rows(t, last, last + 16)[f : f + 1]
+        norm_ref[:, pl.ds(column, WIDTH)] = (block(n) * rstd * gain).astype(jnp.bfloat16)
 
 
 def project_kernel(
-    norm_ref, qg_ref, turn_ref, row_hbm, *rest,
+    norm_ref, wq_ref, qg_ref, turn_ref, row_hbm,
+    send_ref, pack_ref, norm_hbm, row_ref, sem,
 ):
-    parts, (send_ref, pack_ref, norm_hbm, row_ref, sem) = rest[:-5], rest[-5:]
     copies = [pltpu.make_async_copy(norm_ref, norm_hbm, sem.at[1])]
     copies[0].start()
     rows_copy = pltpu.make_async_copy(row_hbm, row_ref, sem.at[0])
     rows_copy.start()
-    depth = parts[0].shape[0]
-    queries = sum(
-        jnp.dot(
-            norm_ref[:, n * depth : (n + 1) * depth], part[...],
-            preferred_element_type=jnp.float32,
-        )
-        for n, part in enumerate(parts)
-    )
+    queries = jnp.dot(norm_ref[...], wq_ref[...], preferred_element_type=jnp.float32)
     cos, sin = unpacked(turn_ref[...])
     q_gain = qg_ref[...].astype(jnp.float32)
     low = lax.broadcasted_iota(jnp.int32, (8, WIDTH), 0) < STEPS
@@ -189,8 +201,7 @@
     for chip in range(CHIPS):
         for c in range(SHARED):
             holder = chip * CORES + (core if c < SLOTS else 1 - core)
-            place = (holder * GROUPS + me) * SLOTS + c % SLOTS
-            row = jnp.minimum(row_ref[place], ROWS - 1)
+            row = jnp.minimum(row_ref[holder, c % SLOTS, me], ROWS - 1)
             send_ref[chip, c * QUERIES : (c + 1) * QUERIES, :] = pack_ref[row]
     for copy in copies:
         copy.wait()
@@ -350,8 +361,7 @@
 
 
 SPREAD_MIB = 60
-TABLE_MIB = 4
-PARTS = 4
+TABLE_MIB = 60
 NORM_MIB = 4
 NORM_COST = 20
 PROJECT_MIB = 8
@@ -391,52 +401,68 @@
 
     tiles = features // WIDTH
     rows = tiles * TOKENS + 16
-    spread = pl.pallas_call(
-        spread_kernel,
-        out_shape=pltpu.HBM((tensor, rows, WIDTH), bf16),
+    tiles = features // WIDTH
+    rows = tiles * TOKENS + 16
+    block = pl.pallas_call(
+        block_kernel,
+        out_shape=VMEM((rows, WIDTH), bf16),
         in_specs=[hbm, hbm],
-        out_specs=hbm,
-        scratch_shapes=[
-            VMEM(hidden.shape, bf16), VMEM((tiles, WIDTH), bf16), VMEM((rows, WIDTH), bf16),
-            dma((2 + tensor,)),
-        ],
+        out_specs=vmem,
+        scratch_shapes=[VMEM(hidden.shape, bf16), VMEM((tiles, WIDTH), bf16), dma((2,))],
         compiler_params=limit(SPREAD_MIB),
-        name="spread",
+        name="block",
     )(hidden, norm_gain.reshape(tiles, WIDTH))
-    gathered = lax.all_to_all(spread, "tp", split_axis=0, concat_axis=0, tiled=True)
-
-    rows_flat = page_row.reshape(-1)
-    seqs_flat = page_seq.reshape(-1)
+
+    def swapped(x, other):
+        return lax.ppermute(x, "tp", [(t, t ^ other) for t in range(SHARDS)])
+
+    def around(x):
+        left, right = swapped(x, 2), swapped(x, 6)
+        return left, swapped(left[:CUT], 6), swapped(right[CUT:], 2), right
+
+    beside = swapped(block, 1)
+    left, far_low, far_high, right = around(block)
+    left_beside, low_beside, high_beside, right_beside = around(beside)
+    gathered = (
+        block, beside, left, left_beside, far_low, far_high, low_beside, high_beside,
+        right, right_beside,
+    )
+
+    row_table = page_row.transpose(0, 2, 1)
+    seq_table = page_seq.transpose(0, 2, 1)
     page_shape = (CHIPS, CORES, SLOTS, WIDTH, WIDTH)
     moved = (2, CHIPS, SLOTS, WIDTH, WIDTH)
-    turns, caps, index, keep, give, *weights = pl.pallas_call(
+    turns, caps, index, keep, give = pl.pallas_call(
         table_kernel,
         out_shape=(
             shape((TOKENS, WIDTH), f32), shape((slots // 8, WIDTH), jnp.int32),
             VMEM((INDEX,), jnp.int32),
             pltpu.HBM(moved, bf16), pltpu.HBM(moved, bf16),
-        )
-        + (pltpu.HBM((width // PARTS, HEADS * WIDTH), bf16),) * PARTS,
-        in_specs=[hbm] * 3 + [smem] * 4,
-        out_specs=(vmem, vmem, vmem) + (hbm,) * (2 + PARTS),
-        scratch_shapes=[SMEM((INDEX,), jnp.int32), dma((5 + PARTS,))],
+        ),
+        in_specs=[hbm] * 6,
+        out_specs=(vmem,) * 3 + (hbm,) * 2,
+        scratch_shapes=[
+            VMEM((4, CHIPS, SLOTS, WIDTH, WIDTH), bf16), SMEM((INDEX,), jnp.int32),
+            SMEM(cache_len.shape, jnp.int32), SMEM(remaining.shape, jnp.int32),
+            SMEM(row_table.shape, jnp.int32), SMEM(seq_table.shape, jnp.int32), dma((13,)),
+        ],
         compiler_params=limit(TABLE_MIB),
         cost_estimate=cost(TABLE_COST),
         name="tables",
     )(
         cache_keys.reshape(page_shape), cached_value_pages.reshape(page_shape),
-        w_query, cache_len, remaining, rows_flat, seqs_flat,
+        cache_len, remaining, row_table, seq_table,
     )
     got = lax.ppermute(give, "dp", flip)
     states = pl.pallas_call(
         norm_kernel,
         out_shape=VMEM((TOKENS, width), bf16),
-        in_specs=[vmem],
+        in_specs=[vmem] * len(gathered),
         out_specs=vmem,
         compiler_params=limit(NORM_MIB),
         cost_estimate=cost(NORM_COST),
         name="normalise",
-    )(gathered)
+    )(*gathered)
     send_q, pack, normed = pl.pallas_call(
         project_kernel,
         out_shape=(
@@ -444,13 +470,13 @@
             shape((ROWS, QUERIES, WIDTH), bf16),
             pltpu.HBM((TOKENS, width), bf16),
         ),
-        in_specs=[vmem] * 3 + [hbm] + [vmem] * PARTS,
+        in_specs=[vmem] * 4 + [hbm],
         out_specs=(vmem, vmem, hbm),
-        scratch_shapes=[SMEM((rows_flat.size,), jnp.int32), dma((2,))],
+        scratch_shapes=[SMEM(row_table.shape, jnp.int32), dma((2,))],
         compiler_params=limit(PROJECT_MIB),
         cost_estimate=cost(PROJECT_COST),
         name="project",
-    )(states, query_gain[None, :], turns, rows_flat, *weights)
+    )(states, w_query, query_gain[None, :], turns, row_table)
     got_q = lax.all_to_all(
         send_q, "dp", split_axis=0, concat_axis=0, tiled=True, axis_index_groups=same_core
     )

time: 70.8 us -> 67.2 us (0.949)
  local copies, waits for them, and re-layouts: 12.2 us -> 4.19 us
  starting transfers between devices: 11 us -> 14.8 us
  waiting for transfers between devices: 11.9 us -> 13.5 us
  blocking collectives: 21.2 us -> 20.4 us
    ppermute x0 -> x9, starting transfers between devices: none -> 11.2 us  [swapped(): return lax.ppermute(x, 'tp', [(t, t ^ other) for t in range(SHARDS)])]
    unnamed x40 -> x22, local copies, waits for them, and re-layouts: 11.7 us -> 4.16 us
    all_to_all x1 -> x0, starting transfers between devices: 7.33 us -> none  [shards(): lax.all_to_all(spread, 'tp', split_axis=0, concat_axis=0, tiled=True)]
    ppermute x0 -> x9, waiting for transfers between devices: none -> 6.67 us  [swapped(): return lax.ppermute(x, 'tp', [(t, t ^ other) for t in range(SHARDS)])]
    all_to_all x1 -> x0, waiting for transfers between devices: 5.37 us -> none  [shards(): lax.all_to_all(spread, 'tp', split_axis=0, concat_axis=0, tiled=True)]
    pallas_call x1, Pallas kernels: 2.14 us -> 0.98 us  [shards(): pl.pallas_call(block_kernel, out_shape=VMEM((rows, WIDTH), bf16), in_spec...]
    all_to_all x1, blocking collectives: 21.2 us -> 20.4 us  [shards(): lax.all_to_all(send_q, 'dp', split_axis=0, concat_axis=0, tiled=True, axi...]
  transfers between devices with their start and end apart: 3 -> 11, of which waited for: 2 -> 4; matrix products, arithmetic and copies ran while one was open for 2% -> 0% of each run, Pallas kernels for 11% -> 13%
where the time goes in v5:
time: 67.2 us; the launch traced here: 66.6 us
  blocking collectives  20.4 us (30%)
  starting transfers between devices  14.8 us (22%)
  waiting for transfers between devices  13.5 us (20%)
  Pallas kernels  12.9 us (19%)
  local copies, waits for them, and re-layouts  4.19 us (6%)
  between operations  0.83 us (1%)
    all_to_all x1, blocking collectives, shards(): lax.all_to_all(send_q, 'dp', split_axis=0, concat_axis=0, tiled=True, axi...  20.4 us
    ppermute x9, starting transfers between devices, swapped(): return lax.ppermute(x, 'tp', [(t, t ^ other) for t in range(SHARDS)])  11.2 us
    all_to_all x1, waiting for transfers between devices, shards(): lax.all_to_all(send_out, 'dp', split_axis=0, concat_axis=0, tiled=True, a...  6.85 us
    ppermute x9, waiting for transfers between devices, swapped(): return lax.ppermute(x, 'tp', [(t, t ^ other) for t in range(SHARDS)])  6.67 us
    pallas_call x1, Pallas kernels, shards(): pl.pallas_call(table_kernel, out_shape=(shape((TOKENS, WIDTH), f32), shap...  5.04 us
    unnamed x22, local copies, waits for them, and re-layouts  4.16 us
    all_to_all x1, starting transfers between devices, shards(): lax.all_to_all(send_out, 'dp', split_axis=0, concat_axis=0, tiled=True, a...  3.54 us
    pallas_call x1, Pallas kernels, shards(): pl.pallas_call(page_kernel, out_shape=VMEM((CHIPS, pairs + SIDE, WIDTH),...  1.76 us
  transfers between devices with their start and end apart: 11, of which 4 were waited for; matrix products, arithmetic and copies ran while one was open for 0% of the time, Pallas kernels for 13%

profile of v5, /device:TPU:12, one launch (start us, length us, event | category | flops | bytes accessed | tf_op | source)
XLA Modules:
  0.0 66.6 jit_solution(11505147596883560613)
XLA Ops:
  0.6 1.0 %block.1.refs_0_ = bf16[656,128]{1,0:T(8,128)(2,1)S(1)} custom-call(bf16[32,4,640]{2,1,0:T(4,128)(2,1)} %hidden_hbm.1, bf16[5,128]{1,0:T(8,128)(2,1)} %bitcast.15), custom_call_target="tpu_custom_call" | custom-call | tf_op jit(solution)/shard_map/block/pallas_call | solution.py:406
  1.6 0.6 collective-permute-start
  2.2 1.6 %collective-permute-start.4 = (bf16[656,128]{1,0:T(8,128)(2,1)S(1)}, bf16[656,128]{1,0:T(8,128)(2,1)S(1)}, u32[]{:S(2)}, u32[]{:S(2)}) collective-permute-start(bf16[656,128]{1,0:T(8,128)(2,1)S(1)} %block.1.refs_0_), channel_id=1, source_target_pairs={{0,6},{1,7},{2,4},{3,5},{4,2},{5,3},{6,0},{7,1},{8,14},{9,15},{10,... | collective-permute-start | bytes 503816 | tf_op jit(solution)/shard_map/ppermute | solution.py:417
  3.8 1.9 %collective-permute-start.1 = (bf16[656,128]{1,0:T(8,128)(2,1)S(1)}, bf16[656,128]{1,0:T(8,128)(2,1)S(1)}, u32[]{:S(2)}, u32[]{:S(2)}) collective-permute-start(bf16[656,128]{1,0:T(8,128)(2,1)S(1)} %block.1.refs_0_), channel_id=1, source_target_pairs={{0,2},{1,3},{2,0},{3,1},{4,6},{5,7},{6,4},{7,5},{8,10},{9,11},{10,... | collective-permute-start | bytes 503816 | tf_op jit(solution)/shard_map/ppermute | solution.py:417
  5.7 3.6 %collective-permute-done.refs_1_ = bf16[656,128]{1,0:T(8,128)(2,1)S(1)} collective-permute-done((bf16[656,128]{1,0:T(8,128)(2,1)S(1)}, bf16[656,128]{1,0:T(8,128)(2,1)S(1)}, u32[]{:S(2)}, u32[]{:S(2)}) %collective-permute-start) | collective-permute-done | bytes 167968 | tf_op jit(solution)/shard_map/ppermute | solution.py:417
  9.2 1.6 %collective-permute-start.7 = (bf16[656,128]{1,0:T(8,128)(2,1)S(1)}, bf16[656,128]{1,0:T(8,128)(2,1)S(1)}, u32[]{:S(2)}, u32[]{:S(2)}) collective-permute-start(bf16[656,128]{1,0:T(8,128)(2,1)S(1)} %collective-permute-done.refs_1_), channel_id=1, source_target_pairs={{0,6},{1,7},{2,4},{3,5},{4,2},{5,3},{6,0},{7,1},{8,14},{9,15},{10,... | collective-permute-start | bytes 503816 | tf_op jit(solution)/shard_map/ppermute | solution.py:417
  10.8 1.9 %collective-permute-start.2 = (bf16[656,128]{1,0:T(8,128)(2,1)S(1)}, bf16[656,128]{1,0:T(8,128)(2,1)S(1)}, u32[]{:S(2)}, u32[]{:S(2)}) collective-permute-start(bf16[656,128]{1,0:T(8,128)(2,1)S(1)} %collective-permute-done.refs_1_), channel_id=1, source_target_pairs={{0,2},{1,3},{2,0},{3,1},{4,6},{5,7},{6,4},{7,5},{8,10},{9,11},{10,... | collective-permute-start | bytes 503816 | tf_op jit(solution)/shard_map/ppermute | solution.py:417
  12.7 0.0 collective-permute-done.4.refs_8_
  12.7 0.3 collective-permute-start.5
  13.0 0.0 collective-permute-done.1.refs_2_
  13.0 0.5 collective-permute-start.3
  13.5 1.8 %collective-permute-done.7.refs_9_ = bf16[656,128]{1,0:T(8,128)(2,1)S(1)} collective-permute-done((bf16[656,128]{1,0:T(8,128)(2,1)S(1)}, bf16[656,128]{1,0:T(8,128)(2,1)S(1)}, u32[]{:S(2)}, u32[]{:S(2)}) %collective-permute-start.7) | collective-permute-done | bytes 167968 | tf_op jit(solution)/shard_map/ppermute | solution.py:417
  15.3 1.1 %collective-permute-start.8 = (bf16[336,128]{1,0:T(8,128)(2,1)S(1)}, bf16[336,128]{1,0:T(8,128)(2,1)S(1)}, u32[]{:S(2)}, u32[]{:S(2)}) collective-permute-start(bf16[336,128]{1,0:T(8,128)(2,1)S(1)} %slice.19), channel_id=1, source_target_pairs={{0,2},{1,3},{2,0},{3,1},{4,6},{5,7},{6,4},{7,5},{8,10},{9,11},{10,... | collective-permute-start | bytes 258056 | tf_op jit(solution)/shard_map/ppermute | solution.py:417
  16.3 1.3 %collective-permute-done.2.refs_3_ = bf16[656,128]{1,0:T(8,128)(2,1)S(1)} collective-permute-done((bf16[656,128]{1,0:T(8,128)(2,1)S(1)}, bf16[656,128]{1,0:T(8,128)(2,1)S(1)}, u32[]{:S(2)}, u32[]{:S(2)}) %collective-permute-start.2) | collective-permute-done | bytes 167968 | tf_op jit(solution)/shard_map/ppermute | solution.py:417
  17.7 1.8 %collective-permute-start.6 = (bf16[320,128]{1,0:T(8,128)(2,1)S(1)}, bf16[320,128]{1,0:T(8,128)(2,1)S(1)}, u32[]{:S(2)}, u32[]{:S(2)}) collective-permute-start(bf16[320,128]{1,0:T(8,128)(2,1)S(1)} %slice.18), channel_id=1, source_target_pairs={{0,6},{1,7},{2,4},{3,5},{4,2},{5,3},{6,0},{7,1},{8,14},{9,15},{10,... | collective-permute-start | bytes 245768 | tf_op jit(solution)/shard_map/ppermute | solution.py:417
  19.5 5.0 %tables.1 = (f32[128,128]{1,0:T(8,128)}, s32[8,128]{1,0:T(8,128)}, s32[1024]{0:T(1024)S(1)}, bf16[2,16,2,128,128]{4,3,2,1,0:T(8,128)(2,1)}, bf16[2,16,2,128,128]{4,3,2,1,0:T(8,128)(2,1)}) custom-call(bf16[16,2,2,128,128]{4,3,2,1,0:T(8,128)(2,1)} %bitcast.16, bf16[16,2,2,128,128]{4,3,2,1,0:T(8,128)(2,1)} %bitcast.17, s32[1024]{0:T(1024)} %len_hbm.1, ...), custom_call_target="tpu_custom_call" | custom-call | flops 21474836480 | bytes 1048576 | tf_op jit(solution)/shard_map/tables/pallas_call | solution.py:435
  24.6 0.0 slice-start
  24.6 0.0 slice-start.1
  24.6 0.0 copy-start.4
  24.6 0.0 copy-start.5
  24.6 0.0 copy-start.8
  24.6 0.1 collective-permute-start.9
  24.7 0.0 collective-permute-done.3.refs_4_
  24.7 0.0 collective-permute-done.5.refs_5_
  24.8 0.0 collective-permute-done.6.refs_6_
  24.8 0.0 collective-permute-done.8.refs_7_
  24.8 0.8 %normalise.1.norm_ref = bf16[128,5120]{1,0:T(8,128)(2,1)S(1)} custom-call(bf16[656,128]{1,0:T(8,128)(2,1)S(1)} %block.1.refs_0_, bf16[656,128]{1,0:T(8,128)(2,1)S(1)} %collective-permute-done.refs_1_, bf16[656,128]{1,0:T(8,128)(2,1)S(1)} %collective-permute-done.1.refs_2_, bf16[656,128]{1,0:T(8,128)(2,1)S(1)} %collective-permute-done.2.refs_3_, ...), custom_call_target="tpu_custom_call" | custom-call | flops 21474836480 | bytes 1048576 | tf_op jit(solution)/shard_map/normalise/pallas_call | solution.py:457
  25.6 1.2 %slice-done = s8[4194304]{0:T(1024)(128)(4,1)S(1)} async-done(((s8[5242880]{0:T(1024)(128)(4,1)}), s8[4194304]{0:T(1024)(128)(4,1)S(1)}, s32[]{:S(2)}) %slice-start) | async-done | bytes 4194328
  26.8 0.3 slice-done.1
  27.1 0.0 copy-done.4
  27.1 0.0 copy-done.5
  27.1 0.0 copy-done.8
  27.1 0.0 copy-start
  27.1 0.0 copy-start.1
  27.1 1.3 %project.1 = (bf16[16,64,128]{2,1,0:T(8,128)(2,1)S(1)}, bf16[32,16,128]{2,1,0:T(8,128)(2,1)S(1)}, bf16[128,5120]{1,0:T(8,128)(2,1)}) custom-call(bf16[128,5120]{1,0:T(8,128)(2,1)S(1)} %normalise.1.norm_ref, bf16[5120,512]{1,0:T(8,128)(2,1)S(1)} %bitcast.10, bf16[1,128]{1,0:T(2,128)(2,1)S(1)} %bitcast.13, f32[128,128]{1,0:T(8,128)S(1)} %copy-done.8, ...), custom_call_target="tpu_custom_call" | custom-call | flops 10737418240 | bytes 1048576 | tf_op jit(solution)/shard_map/project/pallas_call | solution.py:466
  28.4 20.4 %all_to_all.10.q_ref = bf16[16,64,128]{2,1,0:T(8,128)(2,1)S(1)} all-to-all(bf16[16,64,128]{2,1,0:T(8,128)(2,1)S(1)} %get-tuple-element.17), channel_id=1, replica_groups={{0,16,32,48,64,80,96,112,128,144,160,176,192,208,224,240},{8,24,40,56,7..., dimensions={0} | all-to-all | bytes 524288 | tf_op jit(solution)/shard_map/all_to_all | solution.py:480
  48.7 0.0 collective-permute-done.9.got_ref
  48.7 0.0 copy-done
  48.7 0.0 copy-done.1
  48.7 0.0 copy-start.2
  48.8 0.0 copy-start.6
  48.8 1.8 %pages.1 = bf16[16,72,128]{2,1,0:T(8,128)(2,1)} custom-call(bf16[16,64,128]{2,1,0:T(8,128)(2,1)S(1)} %all_to_all.10.q_ref, bf16[2,16,2,128,128]{4,3,2,1,0:T(8,128)(2,1)S(1)} %copy-done, bf16[2,16,2,128,128]{4,3,2,1,0:T(8,128)(2,1)S(1)} %collective-permute-done.9.got_ref, s32[8,128]{1,0:T(8,128)S(1)} %copy-done.1), custom_call_target="tpu_custom_call" | custom-call | tf_op jit(solution)/shard_map/pages/pallas_call | solution.py:493
  50.5 3.5 %all-to-all-start.1 = ((bf16[16,72,128]{2,1,0:T(8,128)(2,1)}), bf16[16,72,128]{2,1,0:T(8,128)(2,1)S(1)}, u32[]{:S(2)}, u32[]{:S(2)}) async-start(bf16[16,72,128]{2,1,0:T(8,128)(2,1)} %pages.1), calls=%async_computation.1 | async-start | bytes 589824 | tf_op jit(solution)/shard_map/all_to_all | solution.py:507
  54.1 0.0 copy-done.2
  54.1 0.0 copy-done.6
  54.1 0.0 copy-start.3
  54.1 1.3 %copy-done.3 = bf16[5120,128]{1,0:T(8,128)(2,1)S(1)} copy-done((bf16[5120,128]{1,0:T(8,128)(2,1)S(1)}, bf16[5120,128]{1,0:T(8,128)(2,1)}, u32[]{:S(2)}) %copy-start.3) | copy-done | bytes 1310744
  55.4 0.0 copy-start.7
  55.4 1.3 %copy-done.7 = bf16[128,5120]{1,0:T(8,128)(2,1)S(1)} copy-done((bf16[128,5120]{1,0:T(8,128)(2,1)S(1)}, bf16[128,5120]{1,0:T(8,128)(2,1)}, u32[]{:S(2)}) %copy-start.7) | copy-done | bytes 1310744
  56.7 1.5 %fresh.1 = (bf16[128,128]{1,0:T(8,128)(2,1)}, bf16[128,128]{1,0:T(8,128)(2,1)}, f32[512,128]{1,0:T(8,128)S(1)}, f32[512,128]{1,0:T(8,128)S(1)}, f32[512,128]{1,0:T(8,128)S(1)}) custom-call(bf16[128,5120]{1,0:T(8,128)(2,1)S(1)} %copy-done.7, bf16[5120,128]{1,0:T(8,128)(2,1)S(1)} %copy-done.2, bf16[5120,128]{1,0:T(8,128)(2,1)S(1)} %copy-done.3, ...), custom_call_target="tpu_custom_call" | custom-call | flops 10737418240 | bytes 1048576 | tf_op jit(solution)/shard_map/fresh/pallas_call | solution.py:483
  58.2 6.8 %all-to-all-done.1.got_ref = bf16[16,72,128]{2,1,0:T(8,128)(2,1)S(1)} async-done(((bf16[16,72,128]{2,1,0:T(8,128)(2,1)}), bf16[16,72,128]{2,1,0:T(8,128)(2,1)S(1)}, u32[]{:S(2)}, u32[]{:S(2)}) %all-to-all-start.1) | async-done | bytes 294944 | tf_op jit(solution)/shard_map/all_to_all | solution.py:507
  65.1 1.6 %combine.1 = bf16[32,4,512]{2,1,0:T(4,128)(2,1)} custom-call(bf16[16,72,128]{2,1,0:T(8,128)(2,1)S(1)} %all-to-all-done.1.got_ref, f32[512,128]{1,0:T(8,128)S(1)} %get-tuple-element.23.max_ref, f32[512,128]{1,0:T(8,128)S(1)} %get-tuple-element.24.total_ref, f32[512,128]{1,0:T(8,128)S(1)} %get-tuple-element.25.out_ref, s32[1024]{0:T(1024)S(1)} %get-tuple-element.26.index_hbm), custom_call_target="tpu_custom_call" | custom-call | tf_op jit(solution)/shard_map/combine/pallas_call | solution.py:510
  (5 shorter events, 0.0 us)
Async XLA Ops:
  1.6 7.6 %collective-permute-start = (bf16[656,128]{1,0:T(8,128)(2,1)S(1)}, bf16[656,128]{1,0:T(8,128)(2,1)S(1)}, u32[]{:S(2)}, u32[]{:S(2)}) collective-permute-start(bf16[656,128]{1,0:T(8,128)(2,1)S(1)} %block.1.refs_0_), channel_id=1, source_target_pairs={{0,1},{1,0},{2,3},{3,2},{4,5},{5,4},{6,7},{7,6},{8,9},{9,8},{10,11... | collective-permute-start | bytes 503816 | tf_op jit(solution)/shard_map/ppermute | solution.py:417
  2.2 10.5 %collective-permute-start.4 = (bf16[656,128]{1,0:T(8,128)(2,1)S(1)}, bf16[656,128]{1,0:T(8,128)(2,1)S(1)}, u32[]{:S(2)}, u32[]{:S(2)}) collective-permute-start(bf16[656,128]{1,0:T(8,128)(2,1)S(1)} %block.1.refs_0_), channel_id=1, source_target_pairs={{0,6},{1,7},{2,4},{3,5},{4,2},{5,3},{6,0},{7,1},{8,14},{9,15},{10,... | collective-permute-start | bytes 503816 | tf_op jit(solution)/shard_map/ppermute | solution.py:417
  3.8 9.2 %collective-permute-start.1 = (bf16[656,128]{1,0:T(8,128)(2,1)S(1)}, bf16[656,128]{1,0:T(8,128)(2,1)S(1)}, u32[]{:S(2)}, u32[]{:S(2)}) collective-permute-start(bf16[656,128]{1,0:T(8,128)(2,1)S(1)} %block.1.refs_0_), channel_id=1, source_target_pairs={{0,2},{1,3},{2,0},{3,1},{4,6},{5,7},{6,4},{7,5},{8,10},{9,11},{10,... | collective-permute-start | bytes 503816 | tf_op jit(solution)/shard_map/ppermute | solution.py:417
  9.2 6.0 %collective-permute-start.7 = (bf16[656,128]{1,0:T(8,128)(2,1)S(1)}, bf16[656,128]{1,0:T(8,128)(2,1)S(1)}, u32[]{:S(2)}, u32[]{:S(2)}) collective-permute-start(bf16[656,128]{1,0:T(8,128)(2,1)S(1)} %collective-permute-done.refs_1_), channel_id=1, source_target_pairs={{0,6},{1,7},{2,4},{3,5},{4,2},{5,3},{6,0},{7,1},{8,14},{9,15},{10,... | collective-permute-start | bytes 503816 | tf_op jit(solution)/shard_map/ppermute | solution.py:417
  10.8 6.9 %collective-permute-start.2 = (bf16[656,128]{1,0:T(8,128)(2,1)S(1)}, bf16[656,128]{1,0:T(8,128)(2,1)S(1)}, u32[]{:S(2)}, u32[]{:S(2)}) collective-permute-start(bf16[656,128]{1,0:T(8,128)(2,1)S(1)} %collective-permute-done.refs_1_), channel_id=1, source_target_pairs={{0,2},{1,3},{2,0},{3,1},{4,6},{5,7},{6,4},{7,5},{8,10},{9,11},{10,... | collective-permute-start | bytes 503816 | tf_op jit(solution)/shard_map/ppermute | solution.py:417
  12.7 12.0 %collective-permute-start.5 = (bf16[336,128]{1,0:T(8,128)(2,1)S(1)}, bf16[336,128]{1,0:T(8,128)(2,1)S(1)}, u32[]{:S(2)}, u32[]{:S(2)}) collective-permute-start(bf16[336,128]{1,0:T(8,128)(2,1)S(1)} %slice.17), channel_id=1, source_target_pairs={{0,2},{1,3},{2,0},{3,1},{4,6},{5,7},{6,4},{7,5},{8,10},{9,11},{10,... | collective-permute-start | bytes 258056 | tf_op jit(solution)/shard_map/ppermute | solution.py:417
  13.0 11.8 %collective-permute-start.3 = (bf16[320,128]{1,0:T(8,128)(2,1)S(1)}, bf16[320,128]{1,0:T(8,128)(2,1)S(1)}, u32[]{:S(2)}, u32[]{:S(2)}) collective-permute-start(bf16[320,128]{1,0:T(8,128)(2,1)S(1)} %slice.16), channel_id=1, source_target_pairs={{0,6},{1,7},{2,4},{3,5},{4,2},{5,3},{6,0},{7,1},{8,14},{9,15},{10,... | collective-permute-start | bytes 245768 | tf_op jit(solution)/shard_map/ppermute | solution.py:417
  15.3 9.5 %collective-permute-start.8 = (bf16[336,128]{1,0:T(8,128)(2,1)S(1)}, bf16[336,128]{1,0:T(8,128)(2,1)S(1)}, u32[]{:S(2)}, u32[]{:S(2)}) collective-permute-start(bf16[336,128]{1,0:T(8,128)(2,1)S(1)} %slice.19), channel_id=1, source_target_pairs={{0,2},{1,3},{2,0},{3,1},{4,6},{5,7},{6,4},{7,5},{8,10},{9,11},{10,... | collective-permute-start | bytes 258056 | tf_op jit(solution)/shard_map/ppermute | solution.py:417
  17.7 7.1 %collective-permute-start.6 = (bf16[320,128]{1,0:T(8,128)(2,1)S(1)}, bf16[320,128]{1,0:T(8,128)(2,1)S(1)}, u32[]{:S(2)}, u32[]{:S(2)}) collective-permute-start(bf16[320,128]{1,0:T(8,128)(2,1)S(1)} %slice.18), channel_id=1, source_target_pairs={{0,6},{1,7},{2,4},{3,5},{4,2},{5,3},{6,0},{7,1},{8,14},{9,15},{10,... | collective-permute-start | bytes 245768 | tf_op jit(solution)/shard_map/ppermute | solution.py:417
  24.6 2.2 %slice-start = ((s8[5242880]{0:T(1024)(128)(4,1)}), s8[4194304]{0:T(1024)(128)(4,1)S(1)}, s32[]{:S(2)}) async-start(s8[5242880]{0:T(1024)(128)(4,1)} %bitcast.9), calls=%async_computation.2 | async-start | bytes 8388608
  24.6 2.5 %slice-start.1 = ((s8[5242880]{0:T(1024)(128)(4,1)}), s8[1048576]{0:T(1024)(128)(4,1)S(1)}, s32[]{:S(2)}) async-start(s8[5242880]{0:T(1024)(128)(4,1)} %bitcast.9), calls=%async_computation.3 | async-start | bytes 2097152
  24.6 2.5 %copy-start.4 = (s32[32,32,2]{1,2,0:T(2,128)S(1)}, s32[32,32,2]{1,2,0:T(2,128)}, u32[]{:S(2)}) copy-start(s32[32,32,2]{1,2,0:T(2,128)} %param.24) | copy-start | bytes 24580
  24.6 2.5 %copy-start.5 = (bf16[128]{0:T(256)(128)(2,1)S(1)}, bf16[128]{0:T(256)(128)(2,1)}, u32[]{:S(2)}) copy-start(bf16[128]{0:T(256)(128)(2,1)} %param.18) | copy-start | bytes 772
  24.6 2.5 %copy-start.8 = (f32[128,128]{1,0:T(8,128)S(1)}, f32[128,128]{1,0:T(8,128)}, u32[]{:S(2)}) copy-start(f32[128,128]{1,0:T(8,128)} %get-tuple-element.16.turn_ref) | copy-start | bytes 196612
  24.6 24.1 %collective-permute-start.9 = (bf16[2,16,2,128,128]{4,3,2,1,0:T(8,128)(2,1)}, bf16[2,16,2,128,128]{4,3,2,1,0:T(8,128)(2,1)S(1)}, u32[]{:S(2)}, u32[]{:S(2)}) collective-permute-start(bf16[2,16,2,128,128]{4,3,2,1,0:T(8,128)(2,1)} %get-tuple-element.19), channel_id=1, source_target_pairs={{0,8},{8,0},{16,24},{24,16},{32,40},{40,32},{48,56},{56,48},{64,72... | collective-permute-start | bytes 6291464 | tf_op jit(solution)/shard_map/ppermute | solution.py:456
  27.1 21.7 %copy-start = (bf16[2,16,2,128,128]{4,3,2,1,0:T(8,128)(2,1)S(1)}, bf16[2,16,2,128,128]{4,3,2,1,0:T(8,128)(2,1)}, u32[]{:S(2)}) copy-start(bf16[2,16,2,128,128]{4,3,2,1,0:T(8,128)(2,1)} %get-tuple-element.18.keep_ref) | copy-start | bytes 6291460
  27.1 21.7 %copy-start.1 = (s32[8,128]{1,0:T(8,128)S(1)}, s32[8,128]{1,0:T(8,128)}, u32[]{:S(2)}) copy-start(s32[8,128]{1,0:T(8,128)} %get-tuple-element.20.cap_ref) | copy-start | bytes 12292
  48.7 5.3 %copy-start.2 = (bf16[5120,128]{1,0:T(8,128)(2,1)S(1)}, bf16[5120,128]{1,0:T(8,128)(2,1)}, u32[]{:S(2)}) copy-start(bf16[5120,128]{1,0:T(8,128)(2,1)} %wk_ref.1) | copy-start | bytes 3932164
  48.8 5.3 %copy-start.6 = (bf16[128]{0:T(256)(128)(2,1)S(1)}, bf16[128]{0:T(256)(128)(2,1)}, u32[]{:S(2)}) copy-start(bf16[128]{0:T(256)(128)(2,1)} %param.19) | copy-start | bytes 772
  50.5 14.5 %all-to-all-start.1 = ((bf16[16,72,128]{2,1,0:T(8,128)(2,1)}), bf16[16,72,128]{2,1,0:T(8,128)(2,1)S(1)}, u32[]{:S(2)}, u32[]{:S(2)}) async-start(bf16[16,72,128]{2,1,0:T(8,128)(2,1)} %pages.1), calls=%async_computation.1 | async-start | bytes 589824 | tf_op jit(solution)/shard_map/all_to_all | solution.py:507
  54.1 1.3 %copy-start.3 = (bf16[5120,128]{1,0:T(8,128)(2,1)S(1)}, bf16[5120,128]{1,0:T(8,128)(2,1)}, u32[]{:S(2)}) copy-start(bf16[5120,128]{1,0:T(8,128)(2,1)} %wv_ref.1) | copy-start | bytes 3932164
  55.4 1.3 %copy-start.7 = (bf16[128,5120]{1,0:T(8,128)(2,1)S(1)}, bf16[128,5120]{1,0:T(8,128)(2,1)}, u32[]{:S(2)}) copy-start(bf16[128,5120]{1,0:T(8,128)(2,1)} %get-tuple-element.21.norm_ref) | copy-start | bytes 3932164

commit v6 on v5

--- a/solution.py
+++ b/solution.py
@@ -79,16 +79,24 @@
             departures.append(pltpu.make_async_copy(staged, target.at[n], sem.at[4 + place]))
     for copy in arrivals:
         copy.start()
+    for arrival, departure in zip(arrivals, departures):
+        arrival.wait()
+        departure.start()
     for copy in scalars:
         copy.wait()
-    row = lax.broadcasted_iota(jnp.int32, (TOKENS, WIDTH), 0)
-    position = row & (STEPS - 1)
-    for r in range(ROWS):
-        position = position + jnp.where(row // STEPS == r, len_ref[me * ROWS + r], 0)
-    column = lax.broadcasted_iota(jnp.int32, (TOKENS, WIDTH), 1)
-    half = (column & (WIDTH // 2 - 1)).astype(jnp.float32)
-    angle = position.astype(jnp.float32) * jnp.exp(half * (-2.0 * math.log(ROPE_BASE) / WIDTH))
-    turn_out[...] = jnp.where(column < WIDTH // 2, jnp.cos(angle), jnp.sin(angle))
+    half = TOKENS // 2
+    token = lax.broadcasted_iota(jnp.int32, (half, WIDTH), 0)
+    column = lax.broadcasted_iota(jnp.int32, (half, WIDTH), 1)
+    left = column < WIDTH // 2
+    position = token & (STEPS - 1)
+    for r in range(ROWS // 2):
+        length = jnp.where(left, len_ref[me * ROWS + r], len_ref[me * ROWS + ROWS // 2 + r])
+        position = position + jnp.where(token // STEPS == r, length, 0)
+    pair = (column & (WIDTH // 2 - 1)).astype(jnp.float32)
+    angle = position.astype(jnp.float32) * jnp.exp(pair * (-2.0 * math.log(ROPE_BASE) / WIDTH))
+    cos, sin = jnp.cos(angle), jnp.sin(angle)
+    turn_out[:half, :] = jnp.where(left, cos, pltpu.roll(sin, WIDTH // 2, 1))
+    turn_out[half:, :] = jnp.where(left, pltpu.roll(cos, WIDTH // 2, 1), sin)
     lane = lax.broadcasted_iota(jnp.int32, (1, WIDTH), 1) // QUERIES
     for j in range(GROUPS * SLOTS // 8):
         cap = jnp.zeros((1, WIDTH), jnp.int32)
@@ -102,9 +110,6 @@
                 lane == i, jnp.where(row < ROWS, length - seq_ref[holder, c, owner] * WIDTH, 0), cap
             )
         cap_out[j : j + 1, :] = cap
-    for arrival, departure in zip(arrivals, departures):
-        arrival.wait()
-        departure.start()
     none = GROUPS * SLOTS
     for i in range(none + 1):
         index_ref[i] = none

time: 67.2 us -> 66.5 us (0.990)
  Pallas kernels: 12.9 us -> 12.2 us
    pallas_call x1, Pallas kernels: 5.04 us -> 4.35 us  [shards(): pl.pallas_call(table_kernel, out_shape=(shape((TOKENS, WIDTH), f32), shap...]
  transfers between devices with their start and end apart: 11 -> 11, of which waited for: 4 -> 4; matrix products, arithmetic and copies ran while one was open for 0% -> 0% of each run, Pallas kernels for 13% -> 12%
where the time goes in v6:
time: 66.5 us; the launch traced here: 65.9 us
  blocking collectives  20.4 us (31%)
  starting transfers between devices  14.8 us (22%)
  waiting for transfers between devices  13.5 us (20%)
  Pallas kernels  12.2 us (18%)
  local copies, waits for them, and re-layouts  4.19 us (6%)
  between operations  0.83 us (1%)
    all_to_all x1, blocking collectives, shards(): lax.all_to_all(send_q, 'dp', split_axis=0, concat_axis=0, tiled=True, axi...  20.4 us
    ppermute x9, starting transfers between devices, swapped(): return lax.ppermute(x, 'tp', [(t, t ^ other) for t in range(SHARDS)])  11.2 us
    all_to_all x1, waiting for transfers between devices, shards(): lax.all_to_all(send_out, 'dp', split_axis=0, concat_axis=0, tiled=True, a...  6.85 us
    ppermute x9, waiting for transfers between devices, swapped(): return lax.ppermute(x, 'tp', [(t, t ^ other) for t in range(SHARDS)])  6.67 us
    pallas_call x1, Pallas kernels, shards(): pl.pallas_call(table_kernel, out_shape=(shape((TOKENS, WIDTH), f32), shap...  4.35 us
    unnamed x22, local copies, waits for them, and re-layouts  4.16 us
    all_to_all x1, starting transfers between devices, shards(): lax.all_to_all(send_out, 'dp', split_axis=0, concat_axis=0, tiled=True, a...  3.54 us
    pallas_call x1, Pallas kernels, shards(): pl.pallas_call(page_kernel, out_shape=VMEM((CHIPS, pairs + SIDE, WIDTH),...  1.76 us
  transfers between devices with their start and end apart: 11, of which 4 were waited for; matrix products, arithmetic and copies ran while one was open for 0% of the time, Pallas kernels for 12%

profile of v6, /device:TPU:12, one launch (start us, length us, event | category | flops | bytes accessed | tf_op | source)
XLA Modules:
  0.0 65.9 jit_solution(17431350063058844058)
XLA Ops:
  0.6 1.0 %block.1.refs_0_ = bf16[656,128]{1,0:T(8,128)(2,1)S(1)} custom-call(bf16[32,4,640]{2,1,0:T(4,128)(2,1)} %hidden_hbm.1, bf16[5,128]{1,0:T(8,128)(2,1)} %bitcast.15), custom_call_target="tpu_custom_call" | custom-call | tf_op jit(solution)/shard_map/block/pallas_call | solution.py:411
  1.6 0.6 collective-permute-start
  2.2 1.6 %collective-permute-start.4 = (bf16[656,128]{1,0:T(8,128)(2,1)S(1)}, bf16[656,128]{1,0:T(8,128)(2,1)S(1)}, u32[]{:S(2)}, u32[]{:S(2)}) collective-permute-start(bf16[656,128]{1,0:T(8,128)(2,1)S(1)} %block.1.refs_0_), channel_id=1, source_target_pairs={{0,6},{1,7},{2,4},{3,5},{4,2},{5,3},{6,0},{7,1},{8,14},{9,15},{10,... | collective-permute-start | bytes 503816 | tf_op jit(solution)/shard_map/ppermute | solution.py:422
  3.8 1.9 %collective-permute-start.1 = (bf16[656,128]{1,0:T(8,128)(2,1)S(1)}, bf16[656,128]{1,0:T(8,128)(2,1)S(1)}, u32[]{:S(2)}, u32[]{:S(2)}) collective-permute-start(bf16[656,128]{1,0:T(8,128)(2,1)S(1)} %block.1.refs_0_), channel_id=1, source_target_pairs={{0,2},{1,3},{2,0},{3,1},{4,6},{5,7},{6,4},{7,5},{8,10},{9,11},{10,... | collective-permute-start | bytes 503816 | tf_op jit(solution)/shard_map/ppermute | solution.py:422
  5.7 3.6 %collective-permute-done.refs_1_ = bf16[656,128]{1,0:T(8,128)(2,1)S(1)} collective-permute-done((bf16[656,128]{1,0:T(8,128)(2,1)S(1)}, bf16[656,128]{1,0:T(8,128)(2,1)S(1)}, u32[]{:S(2)}, u32[]{:S(2)}) %collective-permute-start) | collective-permute-done | bytes 167968 | tf_op jit(solution)/shard_map/ppermute | solution.py:422
  9.2 1.6 %collective-permute-start.7 = (bf16[656,128]{1,0:T(8,128)(2,1)S(1)}, bf16[656,128]{1,0:T(8,128)(2,1)S(1)}, u32[]{:S(2)}, u32[]{:S(2)}) collective-permute-start(bf16[656,128]{1,0:T(8,128)(2,1)S(1)} %collective-permute-done.refs_1_), channel_id=1, source_target_pairs={{0,6},{1,7},{2,4},{3,5},{4,2},{5,3},{6,0},{7,1},{8,14},{9,15},{10,... | collective-permute-start | bytes 503816 | tf_op jit(solution)/shard_map/ppermute | solution.py:422
  10.8 1.9 %collective-permute-start.2 = (bf16[656,128]{1,0:T(8,128)(2,1)S(1)}, bf16[656,128]{1,0:T(8,128)(2,1)S(1)}, u32[]{:S(2)}, u32[]{:S(2)}) collective-permute-start(bf16[656,128]{1,0:T(8,128)(2,1)S(1)} %collective-permute-done.refs_1_), channel_id=1, source_target_pairs={{0,2},{1,3},{2,0},{3,1},{4,6},{5,7},{6,4},{7,5},{8,10},{9,11},{10,... | collective-permute-start | bytes 503816 | tf_op jit(solution)/shard_map/ppermute | solution.py:422
  12.7 0.0 collective-permute-done.4.refs_8_
  12.7 0.3 collective-permute-start.5
  13.0 0.0 collective-permute-done.1.refs_2_
  13.0 0.5 collective-permute-start.3
  13.5 1.8 %collective-permute-done.7.refs_9_ = bf16[656,128]{1,0:T(8,128)(2,1)S(1)} collective-permute-done((bf16[656,128]{1,0:T(8,128)(2,1)S(1)}, bf16[656,128]{1,0:T(8,128)(2,1)S(1)}, u32[]{:S(2)}, u32[]{:S(2)}) %collective-permute-start.7) | collective-permute-done | bytes 167968 | tf_op jit(solution)/shard_map/ppermute | solution.py:422
  15.3 1.1 %collective-permute-start.8 = (bf16[336,128]{1,0:T(8,128)(2,1)S(1)}, bf16[336,128]{1,0:T(8,128)(2,1)S(1)}, u32[]{:S(2)}, u32[]{:S(2)}) collective-permute-start(bf16[336,128]{1,0:T(8,128)(2,1)S(1)} %slice.19), channel_id=1, source_target_pairs={{0,2},{1,3},{2,0},{3,1},{4,6},{5,7},{6,4},{7,5},{8,10},{9,11},{10,... | collective-permute-start | bytes 258056 | tf_op jit(solution)/shard_map/ppermute | solution.py:422
  16.3 1.3 %collective-permute-done.2.refs_3_ = bf16[656,128]{1,0:T(8,128)(2,1)S(1)} collective-permute-done((bf16[656,128]{1,0:T(8,128)(2,1)S(1)}, bf16[656,128]{1,0:T(8,128)(2,1)S(1)}, u32[]{:S(2)}, u32[]{:S(2)}) %collective-permute-start.2) | collective-permute-done | bytes 167968 | tf_op jit(solution)/shard_map/ppermute | solution.py:422
  17.7 1.8 %collective-permute-start.6 = (bf16[320,128]{1,0:T(8,128)(2,1)S(1)}, bf16[320,128]{1,0:T(8,128)(2,1)S(1)}, u32[]{:S(2)}, u32[]{:S(2)}) collective-permute-start(bf16[320,128]{1,0:T(8,128)(2,1)S(1)} %slice.18), channel_id=1, source_target_pairs={{0,6},{1,7},{2,4},{3,5},{4,2},{5,3},{6,0},{7,1},{8,14},{9,15},{10,... | collective-permute-start | bytes 245768 | tf_op jit(solution)/shard_map/ppermute | solution.py:422
  19.5 4.3 %tables.1 = (f32[128,128]{1,0:T(8,128)}, s32[8,128]{1,0:T(8,128)}, s32[1024]{0:T(1024)S(1)}, bf16[2,16,2,128,128]{4,3,2,1,0:T(8,128)(2,1)}, bf16[2,16,2,128,128]{4,3,2,1,0:T(8,128)(2,1)}) custom-call(bf16[16,2,2,128,128]{4,3,2,1,0:T(8,128)(2,1)} %bitcast.16, bf16[16,2,2,128,128]{4,3,2,1,0:T(8,128)(2,1)} %bitcast.17, s32[1024]{0:T(1024)} %len_hbm.1, ...), custom_call_target="tpu_custom_call" | custom-call | flops 21474836480 | bytes 1048576 | tf_op jit(solution)/shard_map/tables/pallas_call | solution.py:440
  23.9 0.0 slice-start
  23.9 0.0 slice-start.1
  23.9 0.0 copy-start.4
  23.9 0.0 copy-start.5
  23.9 0.0 copy-start.8
  23.9 0.1 collective-permute-start.9
  24.0 0.0 collective-permute-done.3.refs_4_
  24.1 0.0 collective-permute-done.5.refs_5_
  24.1 0.0 collective-permute-done.6.refs_6_
  24.1 0.0 collective-permute-done.8.refs_7_
  24.1 0.8 %normalise.1.norm_ref = bf16[128,5120]{1,0:T(8,128)(2,1)S(1)} custom-call(bf16[656,128]{1,0:T(8,128)(2,1)S(1)} %block.1.refs_0_, bf16[656,128]{1,0:T(8,128)(2,1)S(1)} %collective-permute-done.refs_1_, bf16[656,128]{1,0:T(8,128)(2,1)S(1)} %collective-permute-done.1.refs_2_, bf16[656,128]{1,0:T(8,128)(2,1)S(1)} %collective-permute-done.2.refs_3_, ...), custom_call_target="tpu_custom_call" | custom-call | flops 21474836480 | bytes 1048576 | tf_op jit(solution)/shard_map/normalise/pallas_call | solution.py:462
  24.9 1.2 %slice-done = s8[4194304]{0:T(1024)(128)(4,1)S(1)} async-done(((s8[5242880]{0:T(1024)(128)(4,1)}), s8[4194304]{0:T(1024)(128)(4,1)S(1)}, s32[]{:S(2)}) %slice-start) | async-done | bytes 4194328
  26.1 0.3 slice-done.1
  26.4 0.0 copy-done.4
  26.4 0.0 copy-done.5
  26.4 0.0 copy-done.8
  26.4 0.0 copy-start
  26.4 0.0 copy-start.1
  26.4 1.3 %project.1 = (bf16[16,64,128]{2,1,0:T(8,128)(2,1)S(1)}, bf16[32,16,128]{2,1,0:T(8,128)(2,1)S(1)}, bf16[128,5120]{1,0:T(8,128)(2,1)}) custom-call(bf16[128,5120]{1,0:T(8,128)(2,1)S(1)} %normalise.1.norm_ref, bf16[5120,512]{1,0:T(8,128)(2,1)S(1)} %bitcast.10, bf16[1,128]{1,0:T(2,128)(2,1)S(1)} %bitcast.13, f32[128,128]{1,0:T(8,128)S(1)} %copy-done.8, ...), custom_call_target="tpu_custom_call" | custom-call | flops 10737418240 | bytes 1048576 | tf_op jit(solution)/shard_map/project/pallas_call | solution.py:471
  27.7 20.4 %all_to_all.10.q_ref = bf16[16,64,128]{2,1,0:T(8,128)(2,1)S(1)} all-to-all(bf16[16,64,128]{2,1,0:T(8,128)(2,1)S(1)} %get-tuple-element.17), channel_id=1, replica_groups={{0,16,32,48,64,80,96,112,128,144,160,176,192,208,224,240},{8,24,40,56,7..., dimensions={0} | all-to-all | bytes 524288 | tf_op jit(solution)/shard_map/all_to_all | solution.py:485
  48.0 0.0 collective-permute-done.9.got_ref
  48.0 0.0 copy-done
  48.0 0.0 copy-done.1
  48.1 0.0 copy-start.2
  48.1 0.0 copy-start.6
  48.1 1.8 %pages.1 = bf16[16,72,128]{2,1,0:T(8,128)(2,1)} custom-call(bf16[16,64,128]{2,1,0:T(8,128)(2,1)S(1)} %all_to_all.10.q_ref, bf16[2,16,2,128,128]{4,3,2,1,0:T(8,128)(2,1)S(1)} %copy-done, bf16[2,16,2,128,128]{4,3,2,1,0:T(8,128)(2,1)S(1)} %collective-permute-done.9.got_ref, s32[8,128]{1,0:T(8,128)S(1)} %copy-done.1), custom_call_target="tpu_custom_call" | custom-call | tf_op jit(solution)/shard_map/pages/pallas_call | solution.py:498
  49.8 3.5 %all-to-all-start.1 = ((bf16[16,72,128]{2,1,0:T(8,128)(2,1)}), bf16[16,72,128]{2,1,0:T(8,128)(2,1)S(1)}, u32[]{:S(2)}, u32[]{:S(2)}) async-start(bf16[16,72,128]{2,1,0:T(8,128)(2,1)} %pages.1), calls=%async_computation.1 | async-start | bytes 589824 | tf_op jit(solution)/shard_map/all_to_all | solution.py:512
  53.4 0.0 copy-done.2
  53.4 0.0 copy-done.6
  53.4 0.0 copy-start.3
  53.4 1.3 %copy-done.3 = bf16[5120,128]{1,0:T(8,128)(2,1)S(1)} copy-done((bf16[5120,128]{1,0:T(8,128)(2,1)S(1)}, bf16[5120,128]{1,0:T(8,128)(2,1)}, u32[]{:S(2)}) %copy-start.3) | copy-done | bytes 1310744
  54.7 0.0 copy-start.7
  54.7 1.3 %copy-done.7 = bf16[128,5120]{1,0:T(8,128)(2,1)S(1)} copy-done((bf16[128,5120]{1,0:T(8,128)(2,1)S(1)}, bf16[128,5120]{1,0:T(8,128)(2,1)}, u32[]{:S(2)}) %copy-start.7) | copy-done | bytes 1310744
  56.0 1.5 %fresh.1 = (bf16[128,128]{1,0:T(8,128)(2,1)}, bf16[128,128]{1,0:T(8,128)(2,1)}, f32[512,128]{1,0:T(8,128)S(1)}, f32[512,128]{1,0:T(8,128)S(1)}, f32[512,128]{1,0:T(8,128)S(1)}) custom-call(bf16[128,5120]{1,0:T(8,128)(2,1)S(1)} %copy-done.7, bf16[5120,128]{1,0:T(8,128)(2,1)S(1)} %copy-done.2, bf16[5120,128]{1,0:T(8,128)(2,1)S(1)} %copy-done.3, ...), custom_call_target="tpu_custom_call" | custom-call | flops 10737418240 | bytes 1048576 | tf_op jit(solution)/shard_map/fresh/pallas_call | solution.py:488
  57.5 6.8 %all-to-all-done.1.got_ref = bf16[16,72,128]{2,1,0:T(8,128)(2,1)S(1)} async-done(((bf16[16,72,128]{2,1,0:T(8,128)(2,1)}), bf16[16,72,128]{2,1,0:T(8,128)(2,1)S(1)}, u32[]{:S(2)}, u32[]{:S(2)}) %all-to-all-start.1) | async-done | bytes 294944 | tf_op jit(solution)/shard_map/all_to_all | solution.py:512
  64.4 1.6 %combine.1 = bf16[32,4,512]{2,1,0:T(4,128)(2,1)} custom-call(bf16[16,72,128]{2,1,0:T(8,128)(2,1)S(1)} %all-to-all-done.1.got_ref, f32[512,128]{1,0:T(8,128)S(1)} %get-tuple-element.23.max_ref, f32[512,128]{1,0:T(8,128)S(1)} %get-tuple-element.24.total_ref, f32[512,128]{1,0:T(8,128)S(1)} %get-tuple-element.25.out_ref, s32[1024]{0:T(1024)S(1)} %get-tuple-element.26.index_hbm), custom_call_target="tpu_custom_call" | custom-call | tf_op jit(solution)/shard_map/combine/pallas_call | solution.py:515
  (5 shorter events, 0.0 us)
Async XLA Ops:
  1.6 7.6 %collective-permute-start = (bf16[656,128]{1,0:T(8,128)(2,1)S(1)}, bf16[656,128]{1,0:T(8,128)(2,1)S(1)}, u32[]{:S(2)}, u32[]{:S(2)}) collective-permute-start(bf16[656,128]{1,0:T(8,128)(2,1)S(1)} %block.1.refs_0_), channel_id=1, source_target_pairs={{0,1},{1,0},{2,3},{3,2},{4,5},{5,4},{6,7},{7,6},{8,9},{9,8},{10,11... | collective-permute-start | bytes 503816 | tf_op jit(solution)/shard_map/ppermute | solution.py:422
  2.2 10.5 %collective-permute-start.4 = (bf16[656,128]{1,0:T(8,128)(2,1)S(1)}, bf16[656,128]{1,0:T(8,128)(2,1)S(1)}, u32[]{:S(2)}, u32[]{:S(2)}) collective-permute-start(bf16[656,128]{1,0:T(8,128)(2,1)S(1)} %block.1.refs_0_), channel_id=1, source_target_pairs={{0,6},{1,7},{2,4},{3,5},{4,2},{5,3},{6,0},{7,1},{8,14},{9,15},{10,... | collective-permute-start | bytes 503816 | tf_op jit(solution)/shard_map/ppermute | solution.py:422
  3.8 9.2 %collective-permute-start.1 = (bf16[656,128]{1,0:T(8,128)(2,1)S(1)}, bf16[656,128]{1,0:T(8,128)(2,1)S(1)}, u32[]{:S(2)}, u32[]{:S(2)}) collective-permute-start(bf16[656,128]{1,0:T(8,128)(2,1)S(1)} %block.1.refs_0_), channel_id=1, source_target_pairs={{0,2},{1,3},{2,0},{3,1},{4,6},{5,7},{6,4},{7,5},{8,10},{9,11},{10,... | collective-permute-start | bytes 503816 | tf_op jit(solution)/shard_map/ppermute | solution.py:422
  9.2 6.0 %collective-permute-start.7 = (bf16[656,128]{1,0:T(8,128)(2,1)S(1)}, bf16[656,128]{1,0:T(8,128)(2,1)S(1)}, u32[]{:S(2)}, u32[]{:S(2)}) collective-permute-start(bf16[656,128]{1,0:T(8,128)(2,1)S(1)} %collective-permute-done.refs_1_), channel_id=1, source_target_pairs={{0,6},{1,7},{2,4},{3,5},{4,2},{5,3},{6,0},{7,1},{8,14},{9,15},{10,... | collective-permute-start | bytes 503816 | tf_op jit(solution)/shard_map/ppermute | solution.py:422
  10.8 6.9 %collective-permute-start.2 = (bf16[656,128]{1,0:T(8,128)(2,1)S(1)}, bf16[656,128]{1,0:T(8,128)(2,1)S(1)}, u32[]{:S(2)}, u32[]{:S(2)}) collective-permute-start(bf16[656,128]{1,0:T(8,128)(2,1)S(1)} %collective-permute-done.refs_1_), channel_id=1, source_target_pairs={{0,2},{1,3},{2,0},{3,1},{4,6},{5,7},{6,4},{7,5},{8,10},{9,11},{10,... | collective-permute-start | bytes 503816 | tf_op jit(solution)/shard_map/ppermute | solution.py:422
  12.7 11.3 %collective-permute-start.5 = (bf16[336,128]{1,0:T(8,128)(2,1)S(1)}, bf16[336,128]{1,0:T(8,128)(2,1)S(1)}, u32[]{:S(2)}, u32[]{:S(2)}) collective-permute-start(bf16[336,128]{1,0:T(8,128)(2,1)S(1)} %slice.17), channel_id=1, source_target_pairs={{0,2},{1,3},{2,0},{3,1},{4,6},{5,7},{6,4},{7,5},{8,10},{9,11},{10,... | collective-permute-start | bytes 258056 | tf_op jit(solution)/shard_map/ppermute | solution.py:422
  13.0 11.1 %collective-permute-start.3 = (bf16[320,128]{1,0:T(8,128)(2,1)S(1)}, bf16[320,128]{1,0:T(8,128)(2,1)S(1)}, u32[]{:S(2)}, u32[]{:S(2)}) collective-permute-start(bf16[320,128]{1,0:T(8,128)(2,1)S(1)} %slice.16), channel_id=1, source_target_pairs={{0,6},{1,7},{2,4},{3,5},{4,2},{5,3},{6,0},{7,1},{8,14},{9,15},{10,... | collective-permute-start | bytes 245768 | tf_op jit(solution)/shard_map/ppermute | solution.py:422
  15.3 8.8 %collective-permute-start.8 = (bf16[336,128]{1,0:T(8,128)(2,1)S(1)}, bf16[336,128]{1,0:T(8,128)(2,1)S(1)}, u32[]{:S(2)}, u32[]{:S(2)}) collective-permute-start(bf16[336,128]{1,0:T(8,128)(2,1)S(1)} %slice.19), channel_id=1, source_target_pairs={{0,2},{1,3},{2,0},{3,1},{4,6},{5,7},{6,4},{7,5},{8,10},{9,11},{10,... | collective-permute-start | bytes 258056 | tf_op jit(solution)/shard_map/ppermute | solution.py:422
  17.7 6.4 %collective-permute-start.6 = (bf16[320,128]{1,0:T(8,128)(2,1)S(1)}, bf16[320,128]{1,0:T(8,128)(2,1)S(1)}, u32[]{:S(2)}, u32[]{:S(2)}) collective-permute-start(bf16[320,128]{1,0:T(8,128)(2,1)S(1)} %slice.18), channel_id=1, source_target_pairs={{0,6},{1,7},{2,4},{3,5},{4,2},{5,3},{6,0},{7,1},{8,14},{9,15},{10,... | collective-permute-start | bytes 245768 | tf_op jit(solution)/shard_map/ppermute | solution.py:422
  23.9 2.2 %slice-start = ((s8[5242880]{0:T(1024)(128)(4,1)}), s8[4194304]{0:T(1024)(128)(4,1)S(1)}, s32[]{:S(2)}) async-start(s8[5242880]{0:T(1024)(128)(4,1)} %bitcast.9), calls=%async_computation.2 | async-start | bytes 8388608
  23.9 2.5 %slice-start.1 = ((s8[5242880]{0:T(1024)(128)(4,1)}), s8[1048576]{0:T(1024)(128)(4,1)S(1)}, s32[]{:S(2)}) async-start(s8[5242880]{0:T(1024)(128)(4,1)} %bitcast.9), calls=%async_computation.3 | async-start | bytes 2097152
  23.9 2.5 %copy-start.4 = (s32[32,32,2]{1,2,0:T(2,128)S(1)}, s32[32,32,2]{1,2,0:T(2,128)}, u32[]{:S(2)}) copy-start(s32[32,32,2]{1,2,0:T(2,128)} %param.24) | copy-start | bytes 24580
  23.9 2.5 %copy-start.5 = (bf16[128]{0:T(256)(128)(2,1)S(1)}, bf16[128]{0:T(256)(128)(2,1)}, u32[]{:S(2)}) copy-start(bf16[128]{0:T(256)(128)(2,1)} %param.18) | copy-start | bytes 772
  23.9 2.5 %copy-start.8 = (f32[128,128]{1,0:T(8,128)S(1)}, f32[128,128]{1,0:T(8,128)}, u32[]{:S(2)}) copy-start(f32[128,128]{1,0:T(8,128)} %get-tuple-element.16.turn_ref) | copy-start | bytes 196612
  23.9 24.1 %collective-permute-start.9 = (bf16[2,16,2,128,128]{4,3,2,1,0:T(8,128)(2,1)}, bf16[2,16,2,128,128]{4,3,2,1,0:T(8,128)(2,1)S(1)}, u32[]{:S(2)}, u32[]{:S(2)}) collective-permute-start(bf16[2,16,2,128,128]{4,3,2,1,0:T(8,128)(2,1)} %get-tuple-element.19), channel_id=1, source_target_pairs={{0,8},{8,0},{16,24},{24,16},{32,40},{40,32},{48,56},{56,48},{64,72... | collective-permute-start | bytes 6291464 | tf_op jit(solution)/shard_map/ppermute | solution.py:461
  26.4 21.7 %copy-start = (bf16[2,16,2,128,128]{4,3,2,1,0:T(8,128)(2,1)S(1)}, bf16[2,16,2,128,128]{4,3,2,1,0:T(8,128)(2,1)}, u32[]{:S(2)}) copy-start(bf16[2,16,2,128,128]{4,3,2,1,0:T(8,128)(2,1)} %get-tuple-element.18.keep_ref) | copy-start | bytes 6291460
  26.4 21.7 %copy-start.1 = (s32[8,128]{1,0:T(8,128)S(1)}, s32[8,128]{1,0:T(8,128)}, u32[]{:S(2)}) copy-start(s32[8,128]{1,0:T(8,128)} %get-tuple-element.20.cap_ref) | copy-start | bytes 12292
  48.1 5.3 %copy-start.2 = (bf16[5120,128]{1,0:T(8,128)(2,1)S(1)}, bf16[5120,128]{1,0:T(8,128)(2,1)}, u32[]{:S(2)}) copy-start(bf16[5120,128]{1,0:T(8,128)(2,1)} %wk_ref.1) | copy-start | bytes 3932164
  48.1 5.3 %copy-start.6 = (bf16[128]{0:T(256)(128)(2,1)S(1)}, bf16[128]{0:T(256)(128)(2,1)}, u32[]{:S(2)}) copy-start(bf16[128]{0:T(256)(128)(2,1)} %param.19) | copy-start | bytes 772
  49.8 14.5 %all-to-all-start.1 = ((bf16[16,72,128]{2,1,0:T(8,128)(2,1)}), bf16[16,72,128]{2,1,0:T(8,128)(2,1)S(1)}, u32[]{:S(2)}, u32[]{:S(2)}) async-start(bf16[16,72,128]{2,1,0:T(8,128)(2,1)} %pages.1), calls=%async_computation.1 | async-start | bytes 589824 | tf_op jit(solution)/shard_map/all_to_all | solution.py:512
  53.4 1.3 %copy-start.3 = (bf16[5120,128]{1,0:T(8,128)(2,1)S(1)}, bf16[5120,128]{1,0:T(8,128)(2,1)}, u32[]{:S(2)}) copy-start(bf16[5120,128]{1,0:T(8,128)(2,1)} %wv_ref.1) | copy-start | bytes 3932164
  54.7 1.3 %copy-start.7 = (bf16[128,5120]{1,0:T(8,128)(2,1)S(1)}, bf16[128,5120]{1,0:T(8,128)(2,1)}, u32[]{:S(2)}) copy-start(bf16[128,5120]{1,0:T(8,128)(2,1)} %get-tuple-element.21.norm_ref) | copy-start | bytes 3932164
